TPU v7x, 32 devices: a whole 2x2x4 slice. The times are simulated.
32 devices in a mesh: row: 4 (over y, x), col: 8 (over z, core).
Axes of the slice: x: 2, y: 2, z: 4, core: 2. Of those that a mesh axis runs over, the one named last changes fastest.
Arguments:
- iterate: bfloat16 [4096, 6144], P(('row', 'col')), may hold values from -0.25 to 0.25
Outputs:
- update: bfloat16 [4096, 6144], P('row', 'col')
All inputs are finite; a program needn't handle non-finite values.
Results may differ from a plain program's by a relative error of at most 0.0084.
Values may be sent and summed in bfloat16 or wider, within the bound.
No kernel may reach another device: no remote copies, remote signals or barrier semaphores. Data moves between devices by JAX's collectives and lax.ppermute only.
A program may use at most 64 MiB of HBM per device.

v0:
```python
import math

import jax
import jax.numpy as jnp
from jax import lax
from jax.sharding import PartitionSpec as P

M = 4096
D = 6144


linear_weight = 3.4445
cubic_weight = -4.775
quintic_weight = 2.0315
output_gain = 0.2


def gather_rows(block_rows):
    return lax.all_gather(block_rows, "row", axis=0, tiled=True)


def strided_order(panel_rows, row_devices, col_devices):
    total_rows, column_count = panel_rows.shape
    per_device = total_rows // (row_devices * col_devices)
    grouped = panel_rows.reshape(row_devices, col_devices, per_device, column_count)
    return jnp.transpose(grouped, (1, 0, 2, 3)).reshape(total_rows, column_count)


def row_product(left_rows, right_rows):
    return lax.dot_general(
        left_rows, right_rows, (((1,), (1,)), ((), ())), preferred_element_type=jnp.float32
    )


def shards(iterate):
    scaled_tile = lax.all_to_all(iterate, "col", split_axis=1, concat_axis=0, tiled=True)
    row_devices = lax.axis_size("row")
    col_devices = lax.axis_size("col")
    strided_rows = gather_rows(iterate)
    panel_rows = lax.all_gather(scaled_tile, "col", axis=1, tiled=True)
    gram_tile = row_product(panel_rows, strided_rows).astype(jnp.bfloat16)
    gram_wide = lax.all_gather(gram_tile, "col", axis=1, tiled=True)
    scaled_columns = strided_order(gather_rows(scaled_tile), row_devices, col_devices)
    image_tile = jnp.dot(gram_wide, scaled_columns, preferred_element_type=jnp.float32).astype(
        jnp.bfloat16
    )
    image_columns = strided_order(gather_rows(image_tile), row_devices, col_devices)
    second_term = jnp.dot(gram_wide, image_columns, preferred_element_type=jnp.float32)
    combined = (
        linear_weight * scaled_tile.astype(jnp.float32)
        + cubic_weight * image_tile.astype(jnp.float32)
        + quintic_weight * second_term
    )
    update_tile = (output_gain * math.sqrt(max(M, D)) * combined).astype(jnp.bfloat16)
    return update_tile


def solution(mesh):
    return jax.shard_map(
        shards,
        mesh=mesh,
        in_specs=(P(("row", "col"), None),),
        out_specs=P("row", "col"),
        check_vma=False,
    )
```

profile of v0, /device:TPU:0, one launch (start us, length us, event | category | flops | bytes accessed | tf_op | source)
XLA Modules:
  0.0 455.6 jit_solution(4881474069112988442)
XLA Ops:
  6.5 0.0 all-gather.8.cloned.1.call-start
  6.5 0.7 all-gather.8.cloned.1.call-update
  7.3 0.0 all-gather.6.cloned.1.call-start
  7.3 1.5 copy.8
  8.8 44.1 %all_to_all.19 = bf16[128,8,768]{2,0,1:T(8,128)(2,1)} all-to-all(bf16[128,8,768]{2,0,1:T(8,128)(2,1)S(1)} %bitcast.29), channel_id=1, replica_groups=mesh['row'=4,'col'=8] {'col'}, dimensions={1} | all-to-all | bytes 3145728 | tf_op jit(solution)/shard_map/all_to_all | solution.py:36
  52.9 0.0 all-gather.6.cloned.1.call-update
  52.9 0.0 all-gather.12.cloned.1.call-start
  53.0 0.7 all-gather.12.cloned.1.call-update
  53.6 0.0 all-gather.10.cloned.1.call-start
  53.7 28.4 %all-gather.8.cloned.1.call-done = bf16[512,6144]{1,0:T(8,128)(2,1)} async-done(((bf16[128,6144]{1,0:T(8,128)(2,1)}), bf16[512,6144]{1,0:T(8,128)(2,1)}) %all-gather.8.cloned.1.call-update) | async-done | bytes 6291472 | tf_op jit(solution)/shard_map/all_gather | solution.py:19
  82.1 118.4 %all-gather.6.cloned.1.call-done = bf16[1024,6144]{1,0:T(8,128)(2,1)} async-done(((bf16[1024,768]{1,0:T(8,128)(2,1)}), bf16[1024,6144]{1,0:T(8,128)(2,1)}) %all-gather.6.cloned.1.call-update) | async-done | bytes 12582928 | tf_op jit(solution)/shard_map/all_gather | solution.py:40
  200.5 12.3 %convolution_convert_fusion.1 = bf16[1024,512]{1,0:T(8,128)(2,1)} fusion(bf16[1024,6144]{1,0:T(8,128)(2,1)} %all-gather.6.cloned.1.call-done, bf16[512,6144]{1,0:T(8,128)(2,1)} %all-gather.8.cloned.1.call-done), kind=kOutput, calls=%fused_computation.3 | convolution fusion | flops 6442975232 | bytes 19922944 | tf_op jit(solution)/shard_map/dot_general | solution.py:30
  212.8 0.0 all-gather.10.cloned.1.call-update
  212.8 0.0 all-gather.14.cloned.1.call-start
  212.8 57.9 %all-gather.12.cloned.1.call-done = bf16[4096,768]{1,0:T(8,128)(2,1)} async-done(((bf16[1024,768]{1,0:T(8,128)(2,1)}), bf16[4096,768]{1,0:T(8,128)(2,1)}) %all-gather.12.cloned.1.call-update) | async-done | bytes 6291472 | tf_op jit(solution)/shard_map/all_gather | solution.py:19
  270.7 6.0 %copy.4 = bf16[4,8,128,768]{3,2,0,1:T(8,128)(2,1)} copy(bf16[4,8,128,768]{3,2,1,0:T(8,128)(2,1)} %bitcast.24) | data formatting | bytes 12582912 | tf_op jit(solution)/shard_map/reshape | solution.py:25
  276.7 77.5 %all-gather.10.cloned.1.call-done = bf16[1024,4096]{1,0:T(8,128)(2,1)} async-done(((bf16[1024,512]{1,0:T(8,128)(2,1)}), bf16[1024,4096]{1,0:T(8,128)(2,1)}) %all-gather.10.cloned.1.call-update) | async-done | bytes 8388624 | tf_op jit(solution)/shard_map/all_gather | solution.py:42
  354.2 11.8 %convolution_convert_fusion = bf16[1024,768]{1,0:T(8,128)(2,1)} fusion(bf16[1024,4096]{1,0:T(8,128)(2,1)} %all-gather.10.cloned.1.call-done, bf16[4096,768]{1,0:T(8,128)(2,1)} %bitcast.26), kind=kOutput, calls=%fused_computation.1 | convolution fusion | flops 6443237376 | bytes 16252928 | tf_op jit(solution)/shard_map/dot_general | solution.py:44
  366.0 0.0 all-gather.14.cloned.1.call-update
  366.0 68.8 %all-gather.14.cloned.1.call-done = bf16[4096,768]{1,0:T(8,128)(2,1)} async-done(((bf16[1024,768]{1,0:T(8,128)(2,1)}), bf16[4096,768]{1,0:T(8,128)(2,1)}) %all-gather.14.cloned.1.call-update) | async-done | bytes 6291472 | tf_op jit(solution)/shard_map/all_gather | solution.py:19
  434.9 3.3 copy.5
  438.2 0.3 copy-done.1
  438.6 2.5 copy-done.2
  441.0 8.1 %multiply_convert_fusion = bf16[1024,768]{1,0:T(8,128)(2,1)} fusion(bf16[1024,768]{1,0:T(8,128)(2,1)S(1)} %copy-done.1, bf16[1024,768]{1,0:T(8,128)(2,1)S(1)} %bitcast.23, bf16[1024,4096]{1,0:T(8,128)(2,1)S(1)} %copy-done.2, bf16[4096,768]{1,0:T(8,128)(2,1)S(1)} %bitcast.27), kind=kOutput, calls=%fused_computation | convolution fusion | flops 6449528832 | bytes 19398656 | tf_op jit(solution)/shard_map/dot_general | solution.py:48
  (4 shorter events, 0.0 us)
Async XLA Ops:
  6.5 75.6 %all-gather.8.cloned.1.call-start = ((), (), s32[]{:S(2)}) async-start(), calls=%async_computation.2 | async-start | bytes 7864320 | tf_op jit(solution)/shard_map/all_gather | solution.py:19
  7.3 193.2 %all-gather.6.cloned.1.call-start = ((), (), s32[]{:S(2)}) async-start(), calls=%async_computation.1 | async-start | bytes 14155776 | tf_op jit(solution)/shard_map/all_gather | solution.py:40
  52.9 217.8 %all-gather.12.cloned.1.call-start = ((), (), s32[]{:S(2)}) async-start(), calls=%async_computation.4 | async-start | bytes 7864320 | tf_op jit(solution)/shard_map/all_gather | solution.py:19
  53.6 300.6 %all-gather.10.cloned.1.call-start = ((), (), s32[]{:S(2)}) async-start(), calls=%async_computation.3 | async-start | bytes 9437184 | tf_op jit(solution)/shard_map/all_gather | solution.py:42
  212.8 222.1 %all-gather.14.cloned.1.call-start = ((), (), s32[]{:S(2)}) async-start(), calls=%async_computation.5 | async-start | bytes 7864320 | tf_op jit(solution)/shard_map/all_gather | solution.py:19
  434.9 3.4 copy-start
  434.9 3.7 copy-start.1
  434.9 6.2 %copy-start.2 = (bf16[1024,4096]{1,0:T(8,128)(2,1)S(1)}, bf16[1024,4096]{1,0:T(8,128)(2,1)}, u32[]{:S(2)}) copy-start(bf16[1024,4096]{1,0:T(8,128)(2,1)} %all-gather.10.cloned.1.call-done) | copy-start | bytes 25165828
Sparse Core Ops, SparseCore 0:
  9.2 72.8 all-gather.7
  83.7 116.7 all-gather.5
  202.3 68.3 all-gather.11
  272.2 82.0 all-gather.9
  366.2 68.6 all-gather.13
where the time goes:
time: 456 us
  waiting for transfers between devices  352 us (77%)
  blocking collectives  44.1 us (10%)
  matrix products  32.1 us (7%)
  local copies, waits for them, and re-layouts  13.7 us (3%)
  between operations  13.2 us (3%)
    all_gather x3, waiting for transfers between devices, gather_rows(): return lax.all_gather(block_rows, 'row', axis=0, tiled=True)  155 us
    all_gather x1, waiting for transfers between devices, shards(): panel_rows = lax.all_gather(scaled_tile, 'col', axis=1, tiled=True)  118 us
    all_gather x1, waiting for transfers between devices, shards(): gram_wide = lax.all_gather(gram_tile, 'col', axis=1, tiled=True)  77.5 us
    all_to_all x1, blocking collectives, shards(): lax.all_to_all(iterate, 'col', split_axis=1, concat_axis=0, tiled=True)  44.1 us
    dot_general x1, matrix products, row_product(): lax.dot_general(left_rows, right_rows, (((1,), (1,)), ((), ())), preferre...  12.3 us
    dot_general x1, matrix products, shards(): jnp.dot(gram_wide, scaled_columns, preferred_element_type=jnp.float32)  11.8 us
    reshape x2, local copies, waits for them, and re-layouts, strided_order(): panel_rows.reshape(row_devices, col_devices, per_device, column_count)  9.39 us
  transfers between devices with their start and end apart: 5, of which 5 were waited for; matrix products, arithmetic and copies ran while one was open for 4% of the time, Pallas kernels for 0%

commit v1 on v0

--- a/solution.py
+++ b/solution.py
@@ -1,13 +1,12 @@
+import functools
 import math
 
 import jax
 import jax.numpy as jnp
 from jax import lax
+from jax.experimental import pallas as pl
+from jax.experimental.pallas import tpu as pltpu
 from jax.sharding import PartitionSpec as P
-
-M = 4096
-D = 6144
-
 
 linear_weight = 3.4445
 cubic_weight = -4.775
@@ -32,7 +31,16 @@
     )
 
 
-def shards(iterate):
+def combine(scaled_tile, image_tile, second_term, gain):
+    combined = (
+        linear_weight * scaled_tile.astype(jnp.float32)
+        + cubic_weight * image_tile.astype(jnp.float32)
+        + quintic_weight * second_term
+    )
+    return (gain * combined).astype(jnp.bfloat16)
+
+
+def gathered_plan(iterate, gain):
     scaled_tile = lax.all_to_all(iterate, "col", split_axis=1, concat_axis=0, tiled=True)
     row_devices = lax.axis_size("row")
     col_devices = lax.axis_size("col")
@@ -46,20 +54,442 @@
     )
     image_columns = strided_order(gather_rows(image_tile), row_devices, col_devices)
     second_term = jnp.dot(gram_wide, image_columns, preferred_element_type=jnp.float32)
-    combined = (
-        linear_weight * scaled_tile.astype(jnp.float32)
-        + cubic_weight * image_tile.astype(jnp.float32)
-        + quintic_weight * second_term
-    )
-    update_tile = (output_gain * math.sqrt(max(M, D)) * combined).astype(jnp.bfloat16)
-    return update_tile
+    return combine(scaled_tile, image_tile, second_term, gain)
+
+
+def call(
+    kernel, out_shape, operands, flops, scratch=(), space=pltpu.VMEM, out_space=pltpu.VMEM
+):
+    specs = [pl.BlockSpec(memory_space=pltpu.SMEM)]
+    specs += [pl.BlockSpec(memory_space=space)] * (len(operands) - 1)
+    moved = sum(math.prod(v.shape) * v.dtype.itemsize for v in operands)
+    return pl.pallas_call(
+        kernel,
+        in_specs=specs,
+        out_specs=pl.BlockSpec(memory_space=out_space),
+        out_shape=out_shape,
+        scratch_shapes=list(scratch),
+        compiler_params=pltpu.CompilerParams(vmem_limit_bytes=48 * 1024 * 1024),
+        cost_estimate=pl.CostEstimate(flops=flops, bytes_accessed=moved, transcendentals=0),
+    )(*operands)
+
+
+def matmul(left, right):
+    return jnp.dot(left, right, preferred_element_type=jnp.float32)
+
+
+def taken_core(meta_ref, e, distance):
+    return meta_ref[3] ^ (e >> 1) if distance == 2 else meta_ref[2] ^ (e & 1)
+
+
+def level_of(meta_ref, slot, line):
+    return lax.rem(meta_ref[0] + slot, line)
+
+
+def place_pieces(held_ref, refs, levels):
+    half = refs[3].shape[0]
+    for i, level in enumerate(levels):
+        for e in range(3):
+            held_ref[e, level] = refs[5 * i + e][...]
+        held_ref[3, level, :half] = refs[5 * i + 3][...]
+        held_ref[3, level, half:] = refs[5 * i + 4][...]
+
+
+def own_blocks_kernel(line, meta_ref, *refs):
+    out_ref, mine_ref, pair_ref = refs[-3:]
+    count, depth = mine_ref.shape[1:]
+    size = line * count
+    for i in range(line):
+        level = level_of(meta_ref, i, line)
+        mine_ref[level] = refs[i][...]
+        pair_ref[level] = refs[line + i][...]
+
+    def step(i, carry):
+        left = mine_ref[pl.ds(2 * i, 2)].reshape(2 * count, depth)
+        for index, right_ref in enumerate((mine_ref, pair_ref)):
+            product = row_product(left, right_ref[...].reshape(size, depth))
+            out_ref[pl.ds(2 * i, 2), :, index * size:(index + 1) * size] = product.astype(
+                out_ref.dtype
+            ).reshape(2, count, size)
+        return carry
+
+    lax.fori_loop(0, line // 2, step, 0)
+
+
+def cross_blocks_kernel(line, distances, meta_ref, *refs):
+    out_ref, mine_ref, right_ref = refs[-3:]
+    count, depth = mine_ref.shape[1:]
+    size = line * count
+    half = count // 2
+    levels = [level_of(meta_ref, i, line) for i in range(line)]
+    own = refs[:line]
+    pieces = 2 if distances == (3,) else 1
+    step_refs = 2 * pieces * len(distances)
+    for i in range(line):
+        mine_ref[levels[i]] = own[i][...]
+    for index, d in enumerate(distances):
+        for core in range(2):
+
+            @pl.when(taken_core(meta_ref, 0, d) == core)
+            def _():
+                for i in range(line):
+                    first = line + step_refs * i + 2 * pieces * index + pieces * core
+                    if pieces == 1:
+                        right_ref[levels[i]] = refs[first][...]
+                    else:
+                        right_ref[levels[i], :half] = refs[first][...]
+                        right_ref[levels[i], half:] = refs[first + 1][...]
+
+        def step(i, carry):
+            left = mine_ref[pl.ds(2 * i, 2)].reshape(2 * count, depth)
+            product = row_product(left, right_ref[...].reshape(size, depth))
+            out_ref[pl.ds(2 * i, 2), :, index * size:(index + 1) * size] = product.astype(
+                out_ref.dtype
+            ).reshape(2, count, size)
+            return carry
+
+        lax.fori_loop(0, line // 2, step, 0)
+
+
+def columns_kernel(line, slab, meta_ref, *refs):
+    out_ref, held_ref = refs[-2:]
+    count = held_ref.shape[2]
+    levels = [level_of(meta_ref, i, line) for i in range(line)]
+    columns = pl.ds(pl.multiple_of(meta_ref[1] * slab, slab), slab)
+    for i in range(line):
+        for k in range(2):
+            group = refs[10 * i + 5 * k:10 * i + 5 * k + 5]
+            for e in range(3):
+                held_ref[2 * e + k, levels[i]] = group[e][:, columns]
+            held_ref[6 + k, levels[i], :count // 2] = group[3][:, columns]
+            held_ref[6 + k, levels[i], count // 2:] = group[4][:, columns]
+
+    def step(i, carry):
+        group, level = i // line, lax.rem(i, line)
+        out_ref[group // 2, lax.rem(group, 2), level] = held_ref[group, level].T
+        return carry
+
+    lax.fori_loop(0, 8 * line, step, 0)
+
+
+def met_places(meta_ref, e, k):
+    return [(e, k), (e, 1 - k)] + [(e ^ d, k ^ taken_core(meta_ref, e, d)) for d in (1, 2, 3)]
+
+
+def side_by_side(turned_ref, places):
+    line = turned_ref.shape[2]
+    return jnp.concatenate(
+        [turned_ref[a, b, level] for a, b in places for level in range(line)], axis=1
+    )
+
+
+def start_all(copies):
+    for copy in copies:
+        copy.start()
+    return copies
+
+
+def wait_all(copies):
+    for copy in copies:
+        copy.wait()
+
+
+def shard_copies(refs, held_ref, sems):
+    half = held_ref.shape[3] // 2
+    copies = []
+    for i in range(held_ref.shape[2]):
+        for k in range(2):
+            group = refs[10 * i + 5 * k:10 * i + 5 * k + 5]
+            targets = [held_ref.at[e, k, i] for e in range(3)]
+            targets += [held_ref.at[3, k, i, :half], held_ref.at[3, k, i, half:]]
+            for source, target in zip(group, targets):
+                copies.append(pltpu.make_async_copy(source, target, sems.at[len(copies)]))
+    return copies
+
+
+def image_parts(meta_ref, xt_ref, held_ref, levels, e, k):
+    line, width, count = xt_ref.shape[2:]
+    size = line * count
+    slots = len(levels)
+    left, right = [], []
+    for d in (1, 2, 3):
+        a = e ^ d
+        b = k ^ taken_core(meta_ref, a, d)
+        for n in range(slots):
+            left.append(xt_ref[a, b, levels[n]])
+            right.append(held_ref[a, b, n, :, (1 + d) * size:(2 + d) * size])
+    back = matmul(jnp.concatenate(left, axis=1), jnp.concatenate(right))
+    forth = row_product(
+        side_by_side(xt_ref, met_places(meta_ref, e, k)),
+        held_ref[e, k].reshape(slots * count, 5 * size),
+    )
+    return back, forth
+
+
+def early_kernel(slots, meta_ref, xt_hbm, *refs):
+    acc_hbm, xt_ref, held_ref, acc_ref, sems, out_sems = refs[-6:]
+    line, width, count = xt_ref.shape[2:]
+    levels = [level_of(meta_ref, i, line) for i in range(slots)]
+    copies = shard_copies(refs, held_ref, sems)
+    copies.append(pltpu.make_async_copy(xt_hbm, xt_ref, sems.at[len(copies)]))
+    wait_all(start_all(copies))
+
+    def out_copy(i):
+        return pltpu.make_async_copy(
+            acc_ref.at[i // 2, lax.rem(i, 2)], acc_hbm.at[i // 2, lax.rem(i, 2)], out_sems.at[i]
+        )
+
+    def step(i, carry):
+        e, k = i // 2, lax.rem(i, 2)
+        back, forth = image_parts(meta_ref, xt_ref, held_ref, levels, e, k)
+        for level in range(line):
+            acc_ref[e, k, level] = back[:, level * count:(level + 1) * count]
+        for n in range(slots):
+            acc_ref[e, k, levels[n]] += forth[:, n * count:(n + 1) * count]
+        out_copy(i).start()
+        return carry
+
+    lax.fori_loop(0, 8, step, 0)
+    for i in range(8):
+        out_copy(i).wait()
+
+
+def last_kernel(gain, slots, meta_ref, xt_hbm, acc_hbm, *refs):
+    out_ref, xt_ref, held_ref, acc_ref, image_ref, own_ref, cross_ref, back_ref = refs[-11:-3]
+    sems, acc_sems, later_sems = refs[-3:]
+    line, width, count = xt_ref.shape[2:]
+    size = line * count
+    half = count // 2
+    slot_levels = [level_of(meta_ref, i, line) for i in range(line)]
+    levels = slot_levels[line - slots:]
+    copies = shard_copies(refs[10 * (line - slots):10 * line], held_ref, sems)
+    copies.append(pltpu.make_async_copy(xt_hbm, xt_ref, sems.at[len(copies)]))
+    start_all(copies)
+
+    def acc_copy(i):
+        held = lax.rem(i, 2)
+        return pltpu.make_async_copy(
+            acc_hbm.at[i // 2, held], acc_ref.at[held], acc_sems.at[held]
+        )
+
+    for i in range(2):
+        acc_copy(i).start()
+    later = []
+    for i in range(line):
+        for k in range(2):
+            group = refs[10 * i + 5 * k:10 * i + 5 * k + 5]
+            parts = [(group[0], own_ref.at[k, i])]
+            for d in (1, 2):
+                columns = pl.ds((1 + d) * size, size)
+                parts.append((group[d].at[:, columns], cross_ref.at[d - 1, k, i]))
+            columns = pl.ds(4 * size, size)
+            parts.append((group[3].at[:, columns], cross_ref.at[2, k, i, :half]))
+            parts.append((group[4].at[:, columns], cross_ref.at[2, k, i, half:]))
+            for source, target in parts:
+                later.append(pltpu.make_async_copy(source, target, later_sems.at[len(later)]))
+    start_all(later)
+    wait_all(copies)
+
+    def step(i, carry):
+        e, k = i // 2, lax.rem(i, 2)
+        back, forth = image_parts(meta_ref, xt_ref, held_ref, levels, e, k)
+        acc_copy(i).wait()
+        for n in range(slots):
+            acc_ref[k, levels[n]] += forth[:, n * count:(n + 1) * count]
+        for level in range(line):
+            total = acc_ref[k, level] + back[:, level * count:(level + 1) * count]
+            image_ref[e, k, level] = total.astype(jnp.bfloat16)
+
+        @pl.when(i < 6)
+        def _():
+            acc_copy(i + 2).start()
+
+        return carry
+
+    lax.fori_loop(0, 8, step, 0)
+    wait_all(later)
+
+    def finish(k, carry):
+        places = [(d, k ^ taken_core(meta_ref, d, d)) for d in (1, 2, 3)]
+        blocks = [cross_ref[d - 1, b].reshape(size, size) for d, b in places]
+        rows = [image_ref[d, b, level] for d, b in places for level in slot_levels]
+        back = matmul(jnp.concatenate(rows, axis=1), jnp.concatenate(blocks))
+        for level in range(line):
+            back_ref[level] = back[:, level * count:(level + 1) * count]
+        forth = row_product(
+            side_by_side(image_ref, met_places(meta_ref, 0, k)),
+            own_ref[k].reshape(size, 5 * size),
+        )
+        core = meta_ref[1] ^ k
+        for i, level in enumerate(slot_levels):
+            second = forth[:, i * count:(i + 1) * count] + back_ref[level]
+            turned = combine(xt_ref[0, k, level], image_ref[0, k, level], second, gain)
+            out_ref[level, core] = turned.T
+        return carry
+
+    lax.fori_loop(0, 2, finish, 0)
+
+
+def after(values, *others):
+    return lax.optimization_barrier((values,) + others)[0]
+
+
+def neighbour_plan(iterate, gain):
+    line = lax.axis_size("col") // 2
+    count, width = iterate.shape
+    slab = width // (2 * line)
+    size = line * count
+    row_devices = lax.axis_size("row")
+    place, row = lax.axis_index("col"), lax.axis_index("row")
+    level, core = place // 2, place % 2
+    meta = jnp.stack([level, core, row & 1, row >> 1]).astype(jnp.int32)
+
+    def along(values, hop):
+        pairs = [(2 * a + k, 2 * ((a - hop) % line) + k) for a in range(line) for k in range(2)]
+        return lax.ppermute(values, "col", pairs)
+
+    def swap(values):
+        pairs = [(2 * a + k, 2 * a + 1 - k) for a in range(line) for k in range(2)]
+        return lax.ppermute(values, "col", pairs)
+
+    def across(values, bit):
+        return lax.ppermute(values, "row", [(i, i ^ bit) for i in range(row_devices)])
+
+    pieces, last = [None] * line, None
+    for hop in sorted(range(line), key=lambda h: min(h, line - h)):
+        start = ((level - hop) % line) * (2 * slab)
+        piece = lax.dynamic_slice(iterate, (0, start), (count, 2 * slab))
+        if hop:
+            piece = after(piece, last) if 1 < hop < line - 1 else piece
+            piece = along(piece, hop)
+            last = piece if last is None else last
+        pieces[hop] = piece
+    flops = 4 * size * size * slab
+    held = [pltpu.VMEM((line, count, 2 * slab), jnp.bfloat16)] * 2
+
+    def summed(partial, *others):
+        chunks = [
+            along(lax.dynamic_index_in_dim(partial, (level - hop) % line, 0, False), hop)
+            for hop in range(1, line)
+        ]
+        if others:
+            chunks[0] = after(chunks[0], *others)
+        total = lax.dynamic_index_in_dim(partial, level, 0, False).astype(jnp.float32)
+        for chunk in chunks:
+            total += chunk.astype(jnp.float32)
+        return total.astype(jnp.bfloat16)
+
+    own_swapped = [swap(piece) for piece in pieces]
+    own_blocks = call(
+        functools.partial(own_blocks_kernel, line),
+        jax.ShapeDtypeStruct((line, count, 2 * size), jnp.bfloat16),
+        [meta] + pieces + own_swapped,
+        2 * flops,
+        scratch=held,
+    )
+    own_shard = summed(own_blocks)
+
+    half = count // 2
+    x_slots = []
+    for index, piece in enumerate(pieces):
+        one, two = across(piece, 1), across(piece, 2)
+        x_slots.append([piece, one, two, None, None, own_swapped[index], swap(one), swap(two)])
+    side_blocks = call(
+        functools.partial(cross_blocks_kernel, line, (1, 2)),
+        jax.ShapeDtypeStruct((line, count, 2 * size), jnp.bfloat16),
+        [meta] + pieces + [v for slot in x_slots for v in (slot[1], slot[6], slot[2], slot[7])],
+        2 * flops,
+        scratch=held,
+    )
+    for index, slot in enumerate(x_slots):
+        one, two = slot[1], slot[2]
+        if 1 < index < line - 1:
+            one, two = after(one, own_blocks), after(two, own_blocks)
+        slot[3], slot[4] = across(one[:half], 2), across(two[half:], 1)
+        slot += [swap(slot[3]), swap(slot[4])]
+    corner_blocks = call(
+        functools.partial(cross_blocks_kernel, line, (3,)),
+        jax.ShapeDtypeStruct((line, count, size), jnp.bfloat16),
+        [meta] + pieces + [v for slot in x_slots for v in (slot[3], slot[4], slot[8], slot[9])],
+        flops,
+        scratch=held,
+    )
+    side_shard = summed(side_blocks)
+    xt = call(
+        functools.partial(columns_kernel, line, slab),
+        jax.ShapeDtypeStruct((4, 2, line, slab, count), jnp.bfloat16),
+        [meta] + [v for slot in x_slots for v in slot],
+        size * slab * 512,
+        scratch=[pltpu.VMEM((8, line, count, slab), jnp.bfloat16)],
+    )
+    corner_shard = summed(corner_blocks, xt)
+    shard = jnp.concatenate([own_shard, side_shard, corner_shard], axis=1)
+
+    cut = line // 2
+    shards = [shard]
+    for hop in range(1, line):
+        shards.append(along(shards[-1], 1))
+    slots, acc = [], None
+    for first in range(0, line, cut):
+        group = []
+        for shard in shards[first:first + cut]:
+            group.append((shard, across(shard, 1), across(shard, 2)))
+        for shard, one, two in group:
+            if acc is not None:
+                one, two = after(one, acc), after(two, acc)
+            blocks = [shard, one, two, across(one[:half], 2), across(two[half:], 1)]
+            slots.append(blocks + [swap(block) for block in blocks])
+        if acc is not None:
+            break
+        acc = call(
+            functools.partial(early_kernel, cut),
+            jax.ShapeDtypeStruct(xt.shape, jnp.float32),
+            [meta, xt] + [v for slot in slots for v in slot],
+            128 * cut * count * size * slab,
+            scratch=[
+                pltpu.VMEM(xt.shape, jnp.bfloat16),
+                pltpu.VMEM((4, 2, cut, count, 5 * size), jnp.bfloat16),
+                pltpu.VMEM(xt.shape, jnp.float32),
+                pltpu.SemaphoreType.DMA((10 * cut + 1,)),
+                pltpu.SemaphoreType.DMA((8,)),
+            ],
+            space=pl.ANY,
+            out_space=pl.ANY,
+        )
+    update = call(
+        functools.partial(last_kernel, gain, line - cut),
+        jax.ShapeDtypeStruct((line, 2, count, slab), jnp.bfloat16),
+        [meta, xt, acc] + [v for slot in slots for v in slot],
+        (128 * (line - cut) * count + 32 * size) * size * slab,
+        scratch=[
+            pltpu.VMEM(xt.shape, jnp.bfloat16),
+            pltpu.VMEM((4, 2, line - cut, count, 5 * size), jnp.bfloat16),
+            pltpu.VMEM((2, line, slab, count), jnp.float32),
+            pltpu.VMEM(xt.shape, jnp.bfloat16),
+            pltpu.VMEM((2, line, count, 5 * size), jnp.bfloat16),
+            pltpu.VMEM((3, 2, line, count, size), jnp.bfloat16),
+            pltpu.VMEM((line, slab, count), jnp.float32),
+            pltpu.SemaphoreType.DMA((10 * (line - cut) + 1,)),
+            pltpu.SemaphoreType.DMA((2,)),
+            pltpu.SemaphoreType.DMA((10 * line,)),
+        ],
+        space=pl.ANY,
+    )
+    return update.reshape(2 * size, slab)
 
 
 def solution(mesh):
-    return jax.shard_map(
-        shards,
-        mesh=mesh,
-        in_specs=(P(("row", "col"), None),),
-        out_specs=P("row", "col"),
-        check_vma=False,
-    )
+    square_of_lines = mesh.shape["row"] == 4 and mesh.shape["col"] in (4, 6, 8)
+
+    def program(iterate):
+        gain = output_gain * math.sqrt(max(iterate.shape))
+        plan = neighbour_plan if square_of_lines else gathered_plan
+        return jax.shard_map(
+            lambda block: plan(block, gain),
+            mesh=mesh,
+            in_specs=(P(("row", "col"), None),),
+            out_specs=P("row", "col"),
+            check_vma=False,
+        )(iterate)
+
+    return program

time: 456 us -> 303 us (0.66)
  waiting for transfers between devices: 352 us -> 117 us
  starting transfers between devices: 0.16 us -> 80.2 us
  Pallas kernels: 0 us -> 76.4 us
  blocking collectives: 44.1 us -> 0 us
  matrix products: 32.1 us -> 0 us
  between operations: 13.2 us -> 0.91 us
  local copies, waits for them, and re-layouts: 13.7 us -> 25.5 us
    all_gather x5 -> x0, waiting for transfers between devices: 351 us -> none  [the longest x3 155 us: gather_rows(): return lax.all_gather(block_rows, 'row', axis=0, tiled=True)]
    ppermute x0 -> x87, waiting for transfers between devices: none -> 117 us  [the longest x32 60 us: across(): lax.ppermute(values, 'row', [(i, i ^ bit) for i in range(row_devices)])]
    ppermute x0 -> x87, starting transfers between devices: none -> 80.2 us  [the longest x15 39.9 us: along(): return lax.ppermute(values, 'col', pairs)]
    pallas_call x0 -> x6, Pallas kernels: none -> 76.4 us  [call(): pl.pallas_call(kernel, in_specs=specs, out_specs=pl.BlockSpec(memory_spac...]
    all_to_all x1 -> x0, blocking collectives: 44.1 us -> none  [shards(): lax.all_to_all(iterate, 'col', split_axis=1, concat_axis=0, tiled=True)]
    dot_general x3 -> x0, matrix products: 32.1 us -> none  [the longest x1 12.3 us: row_product(): lax.dot_general(left_rows, right_rows, (((1,), (1,)), ((), ())), preferre...]
    unnamed x6 -> x140, local copies, waits for them, and re-layouts: 2.8 us -> 18.4 us
    reshape x2 -> x0, local copies, waits for them, and re-layouts: 9.39 us -> none  [strided_order(): panel_rows.reshape(row_devices, col_devices, per_device, column_count)]
  transfers between devices with their start and end apart: 5 -> 87, of which waited for: 5 -> 26; matrix products, arithmetic and copies ran while one was open for 4% -> 2% of each run, Pallas kernels for 0% -> 14%
where the time goes in v1:
time: 303 us; the launch traced here: 302 us
  waiting for transfers between devices  117 us (39%)
  starting transfers between devices  80.2 us (26%)
  Pallas kernels  76.4 us (25%)
  local copies, waits for them, and re-layouts  25.5 us (8%)
    pallas_call x6, Pallas kernels, call(): pl.pallas_call(kernel, in_specs=specs, out_specs=pl.BlockSpec(memory_spac...  76.4 us
    ppermute x32, waiting for transfers between devices, across(): lax.ppermute(values, 'row', [(i, i ^ bit) for i in range(row_devices)])  60 us
    ppermute x15, waiting for transfers between devices, along(): return lax.ppermute(values, 'col', pairs)  53.3 us
    ppermute x15, starting transfers between devices, along(): return lax.ppermute(values, 'col', pairs)  39.9 us
    ppermute x32, starting transfers between devices, across(): lax.ppermute(values, 'row', [(i, i ^ bit) for i in range(row_devices)])  34.6 us
    unnamed x140, local copies, waits for them, and re-layouts  18.4 us
  transfers between devices with their start and end apart: 87, of which 26 were waited for; matrix products, arithmetic and copies ran while one was open for 2% of the time, Pallas kernels for 14%

profile of v1, /device:TPU:0, one launch (start us, length us, event | category | flops | bytes accessed | tf_op | source)
XLA Modules:
  0.0 302.4 jit_solution(10840275398992668638)
XLA Ops:
  9.8 6.7 %collective-permute-done.22.refs_3_.refs_30_ = bf16[128,1536]{1,0:T(8,128)(2,1)S(1)} collective-permute-done((bf16[128,1536]{1,0:T(8,128)(2,1)S(1)}, bf16[128,1536]{1,0:T(8,128)(2,1)S(1)}, u32[]{:S(2)}, u32[]{:S(2)}) %collective-permute-start.22) | collective-permute-done | bytes 393248 | tf_op jit(solution)/shard_map/ppermute | solution.py:349
  20.5 3.6 %collective-permute-done.9.refs_1_.refs_10_ = bf16[128,1536]{1,0:T(8,128)(2,1)S(1)} collective-permute-done((bf16[128,1536]{1,0:T(8,128)(2,1)S(1)}, bf16[128,1536]{1,0:T(8,128)(2,1)S(1)}, u32[]{:S(2)}, u32[]{:S(2)}) %collective-permute-start.9) | collective-permute-done | bytes 393248 | tf_op jit(solution)/shard_map/ppermute | solution.py:349
  26.4 4.8 %collective-permute-done.3.refs_4_.refs_5_ = bf16[64,1536]{1,0:T(8,128)(2,1)S(1)} collective-permute-done((bf16[64,1536]{1,0:T(8,128)(2,1)S(1)}, bf16[64,1536]{1,0:T(8,128)(2,1)S(1)}, u32[]{:S(2)}, u32[]{:S(2)}) %collective-permute-start.3) | collective-permute-done | bytes 196640 | tf_op jit(solution)/shard_map/ppermute | solution.py:356
  31.2 5.0 %collective-permute-start.19 = (bf16[128,1536]{1,0:T(8,128)(2,1)S(1)}, bf16[128,1536]{1,0:T(8,128)(2,1)S(1)}, u32[]{:S(2)}, u32[]{:S(2)}) collective-permute-start(bf16[128,1536]{1,0:T(8,128)(2,1)S(1)} %get-tuple-element.13), channel_id=1, source_target_pairs={{0,4},{1,5},{2,6},{3,7},{4,0},{5,1},{6,2},{7,3},{8,12},{9,13},{10,... | collective-permute-start | bytes 1179656 | tf_op jit(solution)/shard_map/ppermute | solution.py:349
  39.1 9.3 %collective-permute-done.19.refs_2_.refs_20_ = bf16[128,1536]{1,0:T(8,128)(2,1)S(1)} collective-permute-done((bf16[128,1536]{1,0:T(8,128)(2,1)S(1)}, bf16[128,1536]{1,0:T(8,128)(2,1)S(1)}, u32[]{:S(2)}, u32[]{:S(2)}) %collective-permute-start.19) | collective-permute-done | bytes 393248 | tf_op jit(solution)/shard_map/ppermute | solution.py:349
  95.0 3.5 %collective-permute-start.39 = (bf16[128,1024]{1,0:T(8,128)(2,1)S(1)}, bf16[128,1024]{1,0:T(8,128)(2,1)S(1)}, u32[]{:S(2)}, u32[]{:S(2)}) collective-permute-start(bf16[128,1024]{1,0:T(8,128)(2,1)S(1)} %get-tuple-element.25), channel_id=1, source_target_pairs={{0,6},{1,7},{2,0},{3,1},{4,2},{5,3},{6,4},{7,5},{8,14},{9,15},{10,... | collective-permute-start | bytes 786440 | tf_op jit(solution)/shard_map/ppermute | solution.py:349
  103.0 5.8 %shard_map.19 = bf16[4,128,1024]{2,1,0:T(8,128)(2,1)} custom-call(s32[4]{0:T(128)S(1)} %pad_add_fusion.meta_ref, bf16[128,1536]{1,0:T(8,128)(2,1)S(1)} %get-tuple-element.23.refs_0_, bf16[128,1536]{1,0:T(8,128)(2,1)S(1)} %collective-permute-done.9.refs_1_.refs_10_, bf16[128,1536]{1,0:T(8,128)(2,1)S(1)} %collective-permute-done.19.refs_2_.refs_20_, ...), custom_call_target="tpu_custom_call" | custom-call | flops 1610612736 | bytes 7864336 | tf_op jit(solution)/shard_map/pallas_call | solution.py:66
  111.6 4.4 %collective-permute-start.42 = (bf16[128,1024]{1,0:T(8,128)(2,1)S(1)}, bf16[128,1024]{1,0:T(8,128)(2,1)S(1)}, u32[]{:S(2)}, u32[]{:S(2)}) collective-permute-start(bf16[128,1024]{1,0:T(8,128)(2,1)S(1)} %get-tuple-element.28), channel_id=1, source_target_pairs={{0,6},{1,7},{2,0},{3,1},{4,2},{5,3},{6,4},{7,5},{8,14},{9,15},{10,... | collective-permute-start | bytes 786440 | tf_op jit(solution)/shard_map/ppermute | solution.py:349
  116.0 10.8 %collective-permute-done.40 = bf16[128,1024]{1,0:T(8,128)(2,1)S(1)} collective-permute-done((bf16[128,1024]{1,0:T(8,128)(2,1)S(1)}, bf16[128,1024]{1,0:T(8,128)(2,1)S(1)}, u32[]{:S(2)}, u32[]{:S(2)}) %collective-permute-start.40) | collective-permute-done | bytes 262176 | tf_op jit(solution)/shard_map/ppermute | solution.py:349
  126.8 5.6 %collective-permute-start.44 = (bf16[128,1024]{1,0:T(8,128)(2,1)S(1)}, bf16[128,1024]{1,0:T(8,128)(2,1)S(1)}, u32[]{:S(2)}, u32[]{:S(2)}) collective-permute-start(bf16[128,1024]{1,0:T(8,128)(2,1)S(1)} %get-tuple-element.29), channel_id=1, source_target_pairs={{0,2},{1,3},{2,4},{3,5},{4,6},{5,7},{6,0},{7,1},{8,10},{9,11},{10,... | collective-permute-start | bytes 786440 | tf_op jit(solution)/shard_map/ppermute | solution.py:349
  132.4 3.5 %collective-permute-start.43 = (bf16[128,1024]{1,0:T(8,128)(2,1)S(1)}, bf16[128,1024]{1,0:T(8,128)(2,1)S(1)}, u32[]{:S(2)}, u32[]{:S(2)}) collective-permute-start(bf16[128,1024]{1,0:T(8,128)(2,1)S(1)} %get-tuple-element.30), channel_id=1, source_target_pairs={{0,4},{1,5},{2,6},{3,7},{4,0},{5,1},{6,2},{7,3},{8,12},{9,13},{10,... | collective-permute-start | bytes 786440 | tf_op jit(solution)/shard_map/ppermute | solution.py:349
  137.1 9.7 %shard_map.18.xt_hbm = bf16[4,2,4,768,128]{4,3,2,1,0:T(8,128)(2,1)} custom-call(s32[4]{0:T(128)S(1)} %pad_add_fusion.meta_ref, bf16[128,1536]{1,0:T(8,128)(2,1)S(1)} %get-tuple-element.23.refs_0_, bf16[128,1536]{1,0:T(8,128)(2,1)S(1)} %collective-permute-done.refs_1_.refs_4_, bf16[128,1536]{1,0:T(8,128)(2,1)S(1)} %collective-permute-done.1.refs_2_.refs_6_, ...), custom_call_target="tpu_custom_call" | custom-call | flops 201326592 | bytes 12582928 | tf_op jit(solution)/shard_map/pallas_call | solution.py:66
  146.9 7.1 %collective-permute-done.43 = bf16[128,1024]{1,0:T(8,128)(2,1)S(1)} collective-permute-done((bf16[128,1024]{1,0:T(8,128)(2,1)S(1)}, bf16[128,1024]{1,0:T(8,128)(2,1)S(1)}, u32[]{:S(2)}, u32[]{:S(2)}) %collective-permute-start.43) | collective-permute-done | bytes 262176 | tf_op jit(solution)/shard_map/ppermute | solution.py:349
  159.8 11.2 %collective-permute-done.57.refs_10_ = bf16[128,2560]{1,0:T(8,128)(2,1)S(1)} collective-permute-done((bf16[128,2560]{1,0:T(8,128)(2,1)S(1)}, bf16[128,2560]{1,0:T(8,128)(2,1)S(1)}, u32[]{:S(2)}, u32[]{:S(2)}) %collective-permute-start.57) | collective-permute-done | bytes 655392 | tf_op jit(solution)/shard_map/ppermute | solution.py:349
  171.0 4.1 %collective-permute-start.67 = (bf16[128,2560]{1,0:T(8,128)(2,1)S(1)}, bf16[128,2560]{1,0:T(8,128)(2,1)S(1)}, u32[]{:S(2)}, u32[]{:S(2)}) collective-permute-start(bf16[128,2560]{1,0:T(8,128)(2,1)S(1)} %collective-permute-done.57.refs_10_), channel_id=1, source_target_pairs={{0,6},{1,7},{2,0},{3,1},{4,2},{5,3},{6,4},{7,5},{8,14},{9,15},{10,... | collective-permute-start | bytes 1966088 | tf_op jit(solution)/shard_map/ppermute | solution.py:349
  179.3 6.5 %collective-permute-done.51.refs_4_ = bf16[64,2560]{1,0:T(8,128)(2,1)S(1)} collective-permute-done((bf16[64,2560]{1,0:T(8,128)(2,1)S(1)}, bf16[64,2560]{1,0:T(8,128)(2,1)S(1)}, u32[]{:S(2)}, u32[]{:S(2)}) %collective-permute-start.51) | collective-permute-done | bytes 327712 | tf_op jit(solution)/shard_map/ppermute | solution.py:356
  185.8 11.9 %collective-permute-done.50.refs_3_ = bf16[64,2560]{1,0:T(8,128)(2,1)S(1)} collective-permute-done((bf16[64,2560]{1,0:T(8,128)(2,1)S(1)}, bf16[64,2560]{1,0:T(8,128)(2,1)S(1)}, u32[]{:S(2)}, u32[]{:S(2)}) %collective-permute-start.50) | collective-permute-done | bytes 327712 | tf_op jit(solution)/shard_map/ppermute | solution.py:356
  202.8 8.7 %collective-permute-done.61.refs_14_ = bf16[64,2560]{1,0:T(8,128)(2,1)S(1)} collective-permute-done((bf16[64,2560]{1,0:T(8,128)(2,1)S(1)}, bf16[64,2560]{1,0:T(8,128)(2,1)S(1)}, u32[]{:S(2)}, u32[]{:S(2)}) %collective-permute-start.61) | collective-permute-done | bytes 327712 | tf_op jit(solution)/shard_map/ppermute | solution.py:356
  212.0 3.8 %collective-permute-done.77.refs_30_ = bf16[128,2560]{1,0:T(8,128)(2,1)S(1)} collective-permute-done((bf16[128,2560]{1,0:T(8,128)(2,1)S(1)}, bf16[128,2560]{1,0:T(8,128)(2,1)S(1)}, u32[]{:S(2)}, u32[]{:S(2)}) %collective-permute-start.77) | collective-permute-done | bytes 655392 | tf_op jit(solution)/shard_map/ppermute | solution.py:349
  220.0 22.5 %shard_map.21.acc_hbm = f32[4,2,4,768,128]{4,3,2,1,0:T(8,128)} custom-call(s32[4]{0:T(128)S(1)} %pad_add_fusion.meta_ref, bf16[4,2,4,768,128]{4,3,2,1,0:T(8,128)(2,1)} %shard_map.18.xt_hbm, bf16[128,2560]{1,0:T(8,128)(2,1)S(1)} %pad_maximum_fusion.refs_0_, bf16[128,2560]{1,0:T(8,128)(2,1)S(1)} %collective-permute-done.48.refs_1_, ...), custom_call_target="tpu_custom_call" | custom-call | flops 12884901888 | bytes 16777232 | tf_op jit(solution)/shard_map/pallas_call | solution.py:66
  243.3 3.7 %collective-permute-done.79.refs_32_ = bf16[128,2560]{1,0:T(8,128)(2,1)S(1)} collective-permute-done((bf16[128,2560]{1,0:T(8,128)(2,1)S(1)}, bf16[128,2560]{1,0:T(8,128)(2,1)S(1)}, u32[]{:S(2)}, u32[]{:S(2)}) %collective-permute-start.79) | collective-permute-done | bytes 655392 | tf_op jit(solution)/shard_map/ppermute | solution.py:356
  248.8 7.5 %collective-permute-done.71.refs_24_ = bf16[64,2560]{1,0:T(8,128)(2,1)S(1)} collective-permute-done((bf16[64,2560]{1,0:T(8,128)(2,1)S(1)}, bf16[64,2560]{1,0:T(8,128)(2,1)S(1)}, u32[]{:S(2)}, u32[]{:S(2)}) %collective-permute-start.71) | collective-permute-done | bytes 327712 | tf_op jit(solution)/shard_map/ppermute | solution.py:356
  259.1 7.9 %collective-permute-done.81.refs_34_ = bf16[64,2560]{1,0:T(8,128)(2,1)S(1)} collective-permute-done((bf16[64,2560]{1,0:T(8,128)(2,1)S(1)}, bf16[64,2560]{1,0:T(8,128)(2,1)S(1)}, u32[]{:S(2)}, u32[]{:S(2)}) %collective-permute-start.81) | collective-permute-done | bytes 327712 | tf_op jit(solution)/shard_map/ppermute | solution.py:356
  269.7 32.6 %shard_map.22 = bf16[4,2,128,768]{3,2,1,0:T(8,128)(2,1)} custom-call(s32[4]{0:T(128)S(1)} %pad_add_fusion.meta_ref, bf16[4,2,4,768,128]{4,3,2,1,0:T(8,128)(2,1)} %shard_map.18.xt_hbm, f32[4,2,4,768,128]{4,3,2,1,0:T(8,128)} %shard_map.21.acc_hbm, bf16[128,2560]{1,0:T(8,128)(2,1)S(1)} %pad_maximum_fusion.refs_0_, bf16[128,2560]{1,0:T(8,128)(2,1)} %copy-done.46, ...), custom_call_target="tpu_custom_call" | custom-call | flops 19327352832 | bytes 39845904 | tf_op jit(solution)/shard_map/pallas_call | solution.py:66
  (321 shorter events, 101.3 us)
Async XLA Ops:
  16.6 19.7 %collective-permute-start.32 = (bf16[128,1536]{1,0:T(8,128)(2,1)S(1)}, bf16[128,1536]{1,0:T(8,128)(2,1)S(1)}, u32[]{:S(2)}, u32[]{:S(2)}) collective-permute-start(bf16[128,1536]{1,0:T(8,128)(2,1)S(1)} %collective-permute-done.22.refs_3_.refs_30_), channel_id=1, source_target_pairs={{0,16},{8,24},{16,0},{24,8},{1,17},{9,25},{17,1},{25,9},{2,18},{10... | collective-permute-start | bytes 1179656 | tf_op jit(solution)/shard_map/ppermute | solution.py:356
  18.3 18.5 %collective-permute-start.31 = (bf16[128,1536]{1,0:T(8,128)(2,1)S(1)}, bf16[128,1536]{1,0:T(8,128)(2,1)}, u32[]{:S(2)}, u32[]{:S(2)}) collective-permute-start(bf16[128,1536]{1,0:T(8,128)(2,1)S(1)} %collective-permute-done.22.refs_3_.refs_30_), channel_id=1, source_target_pairs={{0,8},{8,0},{16,24},{24,16},{1,9},{9,1},{17,25},{25,17},{2,10},{10... | collective-permute-start | bytes 1179656 | tf_op jit(solution)/shard_map/ppermute | solution.py:356
  31.2 17.2 %collective-permute-start.19 = (bf16[128,1536]{1,0:T(8,128)(2,1)S(1)}, bf16[128,1536]{1,0:T(8,128)(2,1)S(1)}, u32[]{:S(2)}, u32[]{:S(2)}) collective-permute-start(bf16[128,1536]{1,0:T(8,128)(2,1)S(1)} %get-tuple-element.13), channel_id=1, source_target_pairs={{0,4},{1,5},{2,6},{3,7},{4,0},{5,1},{6,2},{7,3},{8,12},{9,13},{10,... | collective-permute-start | bytes 1179656 | tf_op jit(solution)/shard_map/ppermute | solution.py:349
  84.6 17.7 %collective-permute-start.27 = (bf16[128,1536]{1,0:T(8,128)(2,1)}, bf16[128,1536]{1,0:T(8,128)(2,1)}, u32[]{:S(2)}, u32[]{:S(2)}) collective-permute-start(bf16[128,1536]{1,0:T(8,128)(2,1)} %collective-permute-done.20.refs_21_.refs_12_), channel_id=1, source_target_pairs={{0,1},{1,0},{2,3},{3,2},{4,5},{5,4},{6,7},{7,6},{8,9},{9,8},{10,11... | collective-permute-start | bytes 1179656 | tf_op jit(solution)/shard_map/ppermute | solution.py:353
  98.5 28.3 %collective-permute-start.40 = (bf16[128,1024]{1,0:T(8,128)(2,1)S(1)}, bf16[128,1024]{1,0:T(8,128)(2,1)S(1)}, u32[]{:S(2)}, u32[]{:S(2)}) collective-permute-start(bf16[128,1024]{1,0:T(8,128)(2,1)S(1)} %get-tuple-element.27), channel_id=1, source_target_pairs={{0,4},{1,5},{2,6},{3,7},{4,0},{5,1},{6,2},{7,3},{8,12},{9,13},{10,... | collective-permute-start | bytes 786440 | tf_op jit(solution)/shard_map/ppermute | solution.py:349
  99.1 33.3 %collective-permute-start.45 = (bf16[128,512]{1,0:T(8,128)(2,1)S(1)}, bf16[128,512]{1,0:T(8,128)(2,1)S(1)}, u32[]{:S(2)}, u32[]{:S(2)}) collective-permute-start(bf16[128,512]{1,0:T(8,128)(2,1)S(1)} %get-tuple-element.31), channel_id=1, source_target_pairs={{0,6},{1,7},{2,0},{3,1},{4,2},{5,3},{6,4},{7,5},{8,14},{9,15},{10,... | collective-permute-start | bytes 393224 | tf_op jit(solution)/shard_map/ppermute | solution.py:349
  102.4 44.4 %collective-permute-start.47 = (bf16[128,512]{1,0:T(8,128)(2,1)S(1)}, bf16[128,512]{1,0:T(8,128)(2,1)S(1)}, u32[]{:S(2)}, u32[]{:S(2)}) collective-permute-start(bf16[128,512]{1,0:T(8,128)(2,1)S(1)} %get-tuple-element.32), channel_id=1, source_target_pairs={{0,2},{1,3},{2,4},{3,5},{4,6},{5,7},{6,0},{7,1},{8,10},{9,11},{10,... | collective-permute-start | bytes 393224 | tf_op jit(solution)/shard_map/ppermute | solution.py:349
  110.8 36.0 %collective-permute-start.46 = (bf16[128,512]{1,0:T(8,128)(2,1)S(1)}, bf16[128,512]{1,0:T(8,128)(2,1)S(1)}, u32[]{:S(2)}, u32[]{:S(2)}) collective-permute-start(bf16[128,512]{1,0:T(8,128)(2,1)S(1)} %get-tuple-element.33), channel_id=1, source_target_pairs={{0,4},{1,5},{2,6},{3,7},{4,0},{5,1},{6,2},{7,3},{8,12},{9,13},{10,... | collective-permute-start | bytes 393224 | tf_op jit(solution)/shard_map/ppermute | solution.py:349
  111.6 35.3 %collective-permute-start.42 = (bf16[128,1024]{1,0:T(8,128)(2,1)S(1)}, bf16[128,1024]{1,0:T(8,128)(2,1)S(1)}, u32[]{:S(2)}, u32[]{:S(2)}) collective-permute-start(bf16[128,1024]{1,0:T(8,128)(2,1)S(1)} %get-tuple-element.28), channel_id=1, source_target_pairs={{0,6},{1,7},{2,0},{3,1},{4,2},{5,3},{6,4},{7,5},{8,14},{9,15},{10,... | collective-permute-start | bytes 786440 | tf_op jit(solution)/shard_map/ppermute | solution.py:349
  126.8 20.1 %collective-permute-start.44 = (bf16[128,1024]{1,0:T(8,128)(2,1)S(1)}, bf16[128,1024]{1,0:T(8,128)(2,1)S(1)}, u32[]{:S(2)}, u32[]{:S(2)}) collective-permute-start(bf16[128,1024]{1,0:T(8,128)(2,1)S(1)} %get-tuple-element.29), channel_id=1, source_target_pairs={{0,2},{1,3},{2,4},{3,5},{4,6},{5,7},{6,0},{7,1},{8,10},{9,11},{10,... | collective-permute-start | bytes 786440 | tf_op jit(solution)/shard_map/ppermute | solution.py:349
  132.4 21.6 %collective-permute-start.43 = (bf16[128,1024]{1,0:T(8,128)(2,1)S(1)}, bf16[128,1024]{1,0:T(8,128)(2,1)S(1)}, u32[]{:S(2)}, u32[]{:S(2)}) collective-permute-start(bf16[128,1024]{1,0:T(8,128)(2,1)S(1)} %get-tuple-element.30), channel_id=1, source_target_pairs={{0,4},{1,5},{2,6},{3,7},{4,0},{5,1},{6,2},{7,3},{8,12},{9,13},{10,... | collective-permute-start | bytes 786440 | tf_op jit(solution)/shard_map/ppermute | solution.py:349
  157.8 17.3 %collective-permute-start.49 = (bf16[128,2560]{1,0:T(8,128)(2,1)S(1)}, bf16[128,2560]{1,0:T(8,128)(2,1)S(1)}, u32[]{:S(2)}, u32[]{:S(2)}) collective-permute-start(bf16[128,2560]{1,0:T(8,128)(2,1)S(1)} %pad_maximum_fusion.refs_0_), channel_id=1, source_target_pairs={{0,16},{8,24},{16,0},{24,8},{1,17},{9,25},{17,1},{25,9},{2,18},{10... | collective-permute-start | bytes 1966088 | tf_op jit(solution)/shard_map/ppermute | solution.py:356
  158.3 18.9 %collective-permute-start.48 = (bf16[128,2560]{1,0:T(8,128)(2,1)S(1)}, bf16[128,2560]{1,0:T(8,128)(2,1)S(1)}, u32[]{:S(2)}, u32[]{:S(2)}) collective-permute-start(bf16[128,2560]{1,0:T(8,128)(2,1)S(1)} %pad_maximum_fusion.refs_0_), channel_id=1, source_target_pairs={{0,8},{8,0},{16,24},{24,16},{1,9},{9,1},{17,25},{25,17},{2,10},{10... | collective-permute-start | bytes 1966088 | tf_op jit(solution)/shard_map/ppermute | solution.py:356
  159.8 19.0 %collective-permute-start.52 = (bf16[128,2560]{1,0:T(8,128)(2,1)S(1)}, bf16[128,2560]{1,0:T(8,128)(2,1)S(1)}, u32[]{:S(2)}, u32[]{:S(2)}) collective-permute-start(bf16[128,2560]{1,0:T(8,128)(2,1)S(1)} %pad_maximum_fusion.refs_0_), channel_id=1, source_target_pairs={{0,1},{1,0},{2,3},{3,2},{4,5},{5,4},{6,7},{7,6},{8,9},{9,8},{10,11... | collective-permute-start | bytes 1966088 | tf_op jit(solution)/shard_map/ppermute | solution.py:353
  171.0 26.7 %collective-permute-start.67 = (bf16[128,2560]{1,0:T(8,128)(2,1)S(1)}, bf16[128,2560]{1,0:T(8,128)(2,1)S(1)}, u32[]{:S(2)}, u32[]{:S(2)}) collective-permute-start(bf16[128,2560]{1,0:T(8,128)(2,1)S(1)} %collective-permute-done.57.refs_10_), channel_id=1, source_target_pairs={{0,6},{1,7},{2,0},{3,1},{4,2},{5,3},{6,4},{7,5},{8,14},{9,15},{10,... | collective-permute-start | bytes 1966088 | tf_op jit(solution)/shard_map/ppermute | solution.py:349
  176.7 21.5 %collective-permute-start.59 = (bf16[128,2560]{1,0:T(8,128)(2,1)S(1)}, bf16[128,2560]{1,0:T(8,128)(2,1)S(1)}, u32[]{:S(2)}, u32[]{:S(2)}) collective-permute-start(bf16[128,2560]{1,0:T(8,128)(2,1)S(1)} %collective-permute-done.57.refs_10_), channel_id=1, source_target_pairs={{0,16},{8,24},{16,0},{24,8},{1,17},{9,25},{17,1},{25,9},{2,18},{10... | collective-permute-start | bytes 1966088 | tf_op jit(solution)/shard_map/ppermute | solution.py:356
  177.2 20.5 %collective-permute-start.50 = (bf16[64,2560]{1,0:T(8,128)(2,1)S(1)}, bf16[64,2560]{1,0:T(8,128)(2,1)S(1)}, u32[]{:S(2)}, u32[]{:S(2)}) collective-permute-start(bf16[64,2560]{1,0:T(8,128)(2,1)S(1)} %slice.70), channel_id=1, source_target_pairs={{0,16},{8,24},{16,0},{24,8},{1,17},{9,25},{17,1},{25,9},{2,18},{10... | collective-permute-start | bytes 983048 | tf_op jit(solution)/shard_map/ppermute | solution.py:356
  178.8 19.5 %collective-permute-start.58 = (bf16[128,2560]{1,0:T(8,128)(2,1)S(1)}, bf16[128,2560]{1,0:T(8,128)(2,1)S(1)}, u32[]{:S(2)}, u32[]{:S(2)}) collective-permute-start(bf16[128,2560]{1,0:T(8,128)(2,1)S(1)} %collective-permute-done.57.refs_10_), channel_id=1, source_target_pairs={{0,8},{8,0},{16,24},{24,16},{1,9},{9,1},{17,25},{25,17},{2,10},{10... | collective-permute-start | bytes 1966088 | tf_op jit(solution)/shard_map/ppermute | solution.py:356
  198.8 17.0 %collective-permute-start.77 = (bf16[128,2560]{1,0:T(8,128)(2,1)S(1)}, bf16[128,2560]{1,0:T(8,128)(2,1)S(1)}, u32[]{:S(2)}, u32[]{:S(2)}) collective-permute-start(bf16[128,2560]{1,0:T(8,128)(2,1)S(1)} %collective-permute-done.67.refs_20_), channel_id=1, source_target_pairs={{0,6},{1,7},{2,0},{3,1},{4,2},{5,3},{6,4},{7,5},{8,14},{9,15},{10,... | collective-permute-start | bytes 1966088 | tf_op jit(solution)/shard_map/ppermute | solution.py:349
  215.8 27.4 %collective-permute-start.72 = (bf16[128,2560]{1,0:T(8,128)(2,1)S(1)}, bf16[128,2560]{1,0:T(8,128)(2,1)S(1)}, u32[]{:S(2)}, u32[]{:S(2)}) collective-permute-start(bf16[128,2560]{1,0:T(8,128)(2,1)S(1)} %collective-permute-done.67.refs_20_), channel_id=1, source_target_pairs={{0,1},{1,0},{2,3},{3,2},{4,5},{5,4},{6,7},{7,6},{8,9},{9,8},{10,11... | collective-permute-start | bytes 1966088 | tf_op jit(solution)/shard_map/ppermute | solution.py:353
  215.8 26.8 %collective-permute-start.69 = (bf16[128,2560]{1,0:T(8,128)(2,1)S(1)}, bf16[128,2560]{1,0:T(8,128)(2,1)S(1)}, u32[]{:S(2)}, u32[]{:S(2)}) collective-permute-start(bf16[128,2560]{1,0:T(8,128)(2,1)S(1)} %collective-permute-done.67.refs_20_), channel_id=1, source_target_pairs={{0,16},{8,24},{16,0},{24,8},{1,17},{9,25},{17,1},{25,9},{2,18},{10... | collective-permute-start | bytes 1966088 | tf_op jit(solution)/shard_map/ppermute | solution.py:356
  216.4 26.3 %collective-permute-start.68 = (bf16[128,2560]{1,0:T(8,128)(2,1)S(1)}, bf16[128,2560]{1,0:T(8,128)(2,1)S(1)}, u32[]{:S(2)}, u32[]{:S(2)}) collective-permute-start(bf16[128,2560]{1,0:T(8,128)(2,1)S(1)} %collective-permute-done.67.refs_20_), channel_id=1, source_target_pairs={{0,8},{8,0},{16,24},{24,16},{1,9},{9,1},{17,25},{25,17},{2,10},{10... | collective-permute-start | bytes 1966088 | tf_op jit(solution)/shard_map/ppermute | solution.py:356
  216.9 30.1 %collective-permute-start.79 = (bf16[128,2560]{1,0:T(8,128)(2,1)S(1)}, bf16[128,2560]{1,0:T(8,128)(2,1)S(1)}, u32[]{:S(2)}, u32[]{:S(2)}) collective-permute-start(bf16[128,2560]{1,0:T(8,128)(2,1)S(1)} %collective-permute-done.77.refs_30_), channel_id=1, source_target_pairs={{0,16},{8,24},{16,0},{24,8},{1,17},{9,25},{17,1},{25,9},{2,18},{10... | collective-permute-start | bytes 1966088 | tf_op jit(solution)/shard_map/ppermute | solution.py:356
  218.4 29.1 %collective-permute-start.78 = (bf16[128,2560]{1,0:T(8,128)(2,1)S(1)}, bf16[128,2560]{1,0:T(8,128)(2,1)S(1)}, u32[]{:S(2)}, u32[]{:S(2)}) collective-permute-start(bf16[128,2560]{1,0:T(8,128)(2,1)S(1)} %collective-permute-done.77.refs_30_), channel_id=1, source_target_pairs={{0,8},{8,0},{16,24},{24,16},{1,9},{9,1},{17,25},{25,17},{2,10},{10... | collective-permute-start | bytes 1966088 | tf_op jit(solution)/shard_map/ppermute | solution.py:356
  (133 other events, 1745.7 us)

commit v2 on v1

v2 whole, which is shorter than its diff:
```python
import functools
import math

import jax
import jax.numpy as jnp
from jax import lax
from jax.experimental import pallas as pl
from jax.experimental.pallas import tpu as pltpu
from jax.sharding import PartitionSpec as P

linear_weight = 3.4445
cubic_weight = -4.775
quintic_weight = 2.0315
output_gain = 0.2


def gather_rows(block_rows):
    return lax.all_gather(block_rows, "row", axis=0, tiled=True)


def strided_order(panel_rows, row_devices, col_devices):
    total_rows, column_count = panel_rows.shape
    per_device = total_rows // (row_devices * col_devices)
    grouped = panel_rows.reshape(row_devices, col_devices, per_device, column_count)
    return jnp.transpose(grouped, (1, 0, 2, 3)).reshape(total_rows, column_count)


def row_product(left_rows, right_rows):
    return lax.dot_general(
        left_rows, right_rows, (((1,), (1,)), ((), ())), preferred_element_type=jnp.float32
    )


def combine(scaled_tile, image_tile, second_term, gain):
    combined = (
        linear_weight * scaled_tile.astype(jnp.float32)
        + cubic_weight * image_tile.astype(jnp.float32)
        + quintic_weight * second_term
    )
    return (gain * combined).astype(jnp.bfloat16)


def gathered_plan(iterate, gain):
    scaled_tile = lax.all_to_all(iterate, "col", split_axis=1, concat_axis=0, tiled=True)
    row_devices = lax.axis_size("row")
    col_devices = lax.axis_size("col")
    strided_rows = gather_rows(iterate)
    panel_rows = lax.all_gather(scaled_tile, "col", axis=1, tiled=True)
    gram_tile = row_product(panel_rows, strided_rows).astype(jnp.bfloat16)
    gram_wide = lax.all_gather(gram_tile, "col", axis=1, tiled=True)
    scaled_columns = strided_order(gather_rows(scaled_tile), row_devices, col_devices)
    image_tile = jnp.dot(gram_wide, scaled_columns, preferred_element_type=jnp.float32).astype(
        jnp.bfloat16
    )
    image_columns = strided_order(gather_rows(image_tile), row_devices, col_devices)
    second_term = jnp.dot(gram_wide, image_columns, preferred_element_type=jnp.float32)
    return combine(scaled_tile, image_tile, second_term, gain)


def call(
    kernel, out_shape, operands, flops, scratch=(), space=pltpu.VMEM, out_space=pltpu.VMEM
):
    specs = [pl.BlockSpec(memory_space=pltpu.SMEM)]
    specs += [pl.BlockSpec(memory_space=space)] * (len(operands) - 1)
    moved = sum(math.prod(v.shape) * v.dtype.itemsize for v in operands)
    return pl.pallas_call(
        kernel,
        in_specs=specs,
        out_specs=pl.BlockSpec(memory_space=out_space),
        out_shape=out_shape,
        scratch_shapes=list(scratch),
        compiler_params=pltpu.CompilerParams(vmem_limit_bytes=48 * 1024 * 1024),
        cost_estimate=pl.CostEstimate(flops=flops, bytes_accessed=moved, transcendentals=0),
    )(*operands)


def matmul(left, right):
    return jnp.dot(left, right, preferred_element_type=jnp.float32)


def taken_core(meta_ref, e, distance):
    return meta_ref[3] ^ (e >> 1) if distance == 2 else meta_ref[2] ^ (e & 1)


def level_of(meta_ref, slot, line):
    return lax.rem(meta_ref[0] + slot, line)


def place_rows(held_ref, lead, parts, levels, columns=slice(None)):
    half = held_ref.shape[-2] // 2
    done = 0
    for part in parts:
        for start in range(0, part.shape[0], half):
            slot, place = divmod(done + start, 2 * half)
            to = lead + (levels[slot], slice(place, place + half))
            held_ref[to] = part[start:start + half, columns]
        done += part.shape[0]


def left_products(mine_ref, right, out_ref, index):
    line, count, depth = mine_ref.shape
    size = line * count

    def step(i, carry):
        left = mine_ref[pl.ds(2 * i, 2)].reshape(2 * count, depth)
        product = row_product(left, right[...].reshape(size, depth))
        out_ref[pl.ds(2 * i, 2), :, index * size:(index + 1) * size] = product.astype(
            out_ref.dtype
        ).reshape(2, count, size)
        return carry

    lax.fori_loop(0, line // 2, step, 0)


def own_blocks_kernel(meta_ref, *refs):
    out_ref, mine_ref, pair_ref = refs[-3:]
    line = mine_ref.shape[0]
    levels = [level_of(meta_ref, i, line) for i in range(line)]
    place_rows(mine_ref, (), refs[:1], levels)
    place_rows(pair_ref, (), refs[1:2], levels)
    left_products(mine_ref, mine_ref, out_ref, 0)
    left_products(mine_ref, pair_ref, out_ref, 1)


def group_of(meta_ref, k, order):
    core = meta_ref[1] ^ k
    return (0, 1 + core, 2 - core, 3)[order]


def side_blocks_kernel(meta_ref, *refs):
    out_ref, mine_ref, right_ref = refs[-3:]
    line = mine_ref.shape[0]
    levels = [level_of(meta_ref, i, line) for i in range(line)]
    place_rows(mine_ref, (), refs[:1], levels)
    for d in (1, 2):
        for k in range(2):
            for order in (1, 2):
                is_core = taken_core(meta_ref, 0, d) == k

                @pl.when(jnp.logical_and(is_core, group_of(meta_ref, k, order) == d))
                def _():
                    place_rows(right_ref, (), [refs[2 * k + order]], levels)

        left_products(mine_ref, right_ref, out_ref, d - 1)


def corner_blocks_kernel(meta_ref, *refs):
    out_ref, mine_ref, right_ref = refs[-3:]
    line = mine_ref.shape[0]
    levels = [level_of(meta_ref, i, line) for i in range(line)]
    place_rows(mine_ref, (), refs[:1], levels)
    for k in range(2):

        @pl.when(taken_core(meta_ref, 0, 3) == k)
        def _():
            place_rows(right_ref, (), [refs[1 + k]], levels)

    left_products(mine_ref, right_ref, out_ref, 0)


def columns_kernel(slab, orders, meta_ref, *refs):
    out_ref, held_ref = refs[-2:]
    groups, _, line = held_ref.shape[:3]
    levels = [level_of(meta_ref, i, line) for i in range(line)]
    columns = pl.ds(pl.multiple_of(meta_ref[1] * slab, slab), slab)
    for k in range(2):
        for index, order in enumerate(orders):
            e = group_of(meta_ref, k, order) - orders[0]
            place_rows(held_ref, (e, k), [refs[len(orders) * k + index]], levels, columns)

    def step(i, carry):
        group, level = i // line, lax.rem(i, line)
        e, k = group // 2, lax.rem(group, 2)
        out_ref[e, k, level] = held_ref[e, k, level].T
        return carry

    lax.fori_loop(0, 2 * groups * line, step, 0)


def met_places(meta_ref, e, k):
    return [(e, k), (e, 1 - k)] + [(e ^ d, k ^ taken_core(meta_ref, e, d)) for d in (1, 2, 3)]


def side_by_side(turned_ref, places):
    line = turned_ref.shape[2]
    return jnp.concatenate(
        [turned_ref[a, b, level] for a, b in places for level in range(line)], axis=1
    )


def start_all(copies):
    for copy in copies:
        copy.start()
    return copies


def wait_all(copies):
    for copy in copies:
        copy.wait()


def shard_copies(meta_ref, refs, slots, held_ref, sems):
    copies = []
    for i, slot in enumerate(slots):
        for k in range(2):
            for order in range(4):
                source = refs[8 * slot + 4 * k + order]
                target = held_ref.at[group_of(meta_ref, k, order), k, i]
                copies.append(pltpu.make_async_copy(source, target, sems.at[len(copies)]))
    return copies


def column_copies(near_hbm, far_hbm, xt_ref, sems, used):
    parts = ((near_hbm, xt_ref.at[:3]), (far_hbm, xt_ref.at[3:]))
    return [
        pltpu.make_async_copy(source, target, sems.at[used + i])
        for i, (source, target) in enumerate(parts)
    ]


def image_parts(meta_ref, xt_ref, held_ref, levels, e, k):
    line, width, count = xt_ref.shape[2:]
    size = line * count
    slots = len(levels)
    left, right = [], []
    for d in (1, 2, 3):
        a = e ^ d
        b = k ^ taken_core(meta_ref, a, d)
        for n in range(slots):
            left.append(xt_ref[a, b, levels[n]])
            right.append(held_ref[a, b, n, :, (1 + d) * size:(2 + d) * size])
    back = matmul(jnp.concatenate(left, axis=1), jnp.concatenate(right))
    forth = row_product(
        side_by_side(xt_ref, met_places(meta_ref, e, k)),
        held_ref[e, k].reshape(slots * count, 5 * size),
    )
    return back, forth


def early_kernel(slots, meta_ref, near_hbm, far_hbm, *refs):
    acc_hbm, xt_ref, held_ref, acc_ref, sems, out_sems = refs[-6:]
    line, width, count = xt_ref.shape[2:]
    levels = [level_of(meta_ref, i, line) for i in range(slots)]
    copies = shard_copies(meta_ref, refs, range(slots), held_ref, sems)
    copies += column_copies(near_hbm, far_hbm, xt_ref, sems, len(copies))
    wait_all(start_all(copies))

    def out_copy(i):
        return pltpu.make_async_copy(
            acc_ref.at[i // 2, lax.rem(i, 2)], acc_hbm.at[i // 2, lax.rem(i, 2)], out_sems.at[i]
        )

    def step(i, carry):
        e, k = i // 2, lax.rem(i, 2)
        back, forth = image_parts(meta_ref, xt_ref, held_ref, levels, e, k)
        for level in range(line):
            acc_ref[e, k, level] = back[:, level * count:(level + 1) * count]
        for n in range(slots):
            acc_ref[e, k, levels[n]] += forth[:, n * count:(n + 1) * count]
        out_copy(i).start()
        return carry

    lax.fori_loop(0, 8, step, 0)
    for i in range(8):
        out_copy(i).wait()


def last_kernel(gain, slots, meta_ref, near_hbm, far_hbm, acc_hbm, *refs):
    out_ref, xt_ref, held_ref, acc_ref, image_ref, own_ref, cross_ref, back_ref = refs[-11:-3]
    sems, acc_sems, later_sems = refs[-3:]
    line, width, count = xt_ref.shape[2:]
    size = line * count
    slot_levels = [level_of(meta_ref, i, line) for i in range(line)]
    levels = slot_levels[line - slots:]
    copies = shard_copies(meta_ref, refs, range(line - slots, line), held_ref, sems)
    copies += column_copies(near_hbm, far_hbm, xt_ref, sems, len(copies))
    start_all(copies)

    def acc_copy(i):
        held = lax.rem(i, 2)
        return pltpu.make_async_copy(
            acc_hbm.at[i // 2, held], acc_ref.at[held], acc_sems.at[held]
        )

    for i in range(2):
        acc_copy(i).start()
    later = []
    for i in range(line):
        for k in range(2):
            for order in range(4):
                source, target = refs[8 * i + 4 * k + order], own_ref.at[k, i]
                if order:
                    e = group_of(meta_ref, k, order)
                    first = (1 + e) * size
                    first = pl.multiple_of(first, size) if order < 3 else first
                    source, target = source.at[:, pl.ds(first, size)], cross_ref.at[e - 1, k, i]
                later.append(pltpu.make_async_copy(source, target, later_sems.at[len(later)]))
    start_all(later)
    wait_all(copies)

    def step(i, carry):
        e, k = i // 2, lax.rem(i, 2)
        back, forth = image_parts(meta_ref, xt_ref, held_ref, levels, e, k)
        acc_copy(i).wait()
        for n in range(slots):
            acc_ref[k, levels[n]] += forth[:, n * count:(n + 1) * count]
        for level in range(line):
            total = acc_ref[k, level] + back[:, level * count:(level + 1) * count]
            image_ref[e, k, level] = total.astype(jnp.bfloat16)

        @pl.when(i < 6)
        def _():
            acc_copy(i + 2).start()

        return carry

    lax.fori_loop(0, 8, step, 0)
    wait_all(later)

    def finish(k, carry):
        places = [(d, k ^ taken_core(meta_ref, d, d)) for d in (1, 2, 3)]
        blocks = [cross_ref[d - 1, b].reshape(size, size) for d, b in places]
        rows = [image_ref[d, b, level] for d, b in places for level in slot_levels]
        back = matmul(jnp.concatenate(rows, axis=1), jnp.concatenate(blocks))
        for level in range(line):
            back_ref[level] = back[:, level * count:(level + 1) * count]
        forth = row_product(
            side_by_side(image_ref, met_places(meta_ref, 0, k)),
            own_ref[k].reshape(size, 5 * size),
        )
        core = meta_ref[1] ^ k
        for i, level in enumerate(slot_levels):
            second = forth[:, i * count:(i + 1) * count] + back_ref[level]
            turned = combine(xt_ref[0, k, level], image_ref[0, k, level], second, gain)
            out_ref[level, core] = turned.T
        return carry

    lax.fori_loop(0, 2, finish, 0)


def after(values, *others):
    return lax.optimization_barrier((values,) + others)[0]


def neighbour_plan(iterate, gain):
    line = lax.axis_size("col") // 2
    count, width = iterate.shape
    slab = width // (2 * line)
    size = line * count
    row_devices = lax.axis_size("row")
    place, row = lax.axis_index("col"), lax.axis_index("row")
    level, core = place // 2, place % 2
    meta = jnp.stack([level, core, row & 1, row >> 1]).astype(jnp.int32)

    def along(values, hop):
        pairs = [(2 * a + k, 2 * ((a - hop) % line) + k) for a in range(line) for k in range(2)]
        return lax.ppermute(values, "col", pairs)

    def swap(values):
        pairs = [(2 * a + k, 2 * a + 1 - k) for a in range(line) for k in range(2)]
        return lax.ppermute(values, "col", pairs)

    def across(values, turn):
        pairs = [
            (r * 2 * line + c, (r ^ (1 + (c + turn) % 2)) * 2 * line + c)
            for r in range(row_devices)
            for c in range(2 * line)
        ]
        return lax.ppermute(values, ("row", "col"), pairs)

    def sent(partial):
        return [
            along(lax.dynamic_index_in_dim(partial, (level - hop) % line, 0, False), hop)
            for hop in range(1, line)
        ]

    def summed(partial, chunks):
        total = lax.dynamic_index_in_dim(partial, level, 0, False).astype(jnp.float32)
        for chunk in chunks:
            total += chunk.astype(jnp.float32)
        return total.astype(jnp.bfloat16)

    def piece(hop):
        start = ((level - hop) % line) * (2 * slab)
        return lax.dynamic_slice(iterate, (0, start), (count, 2 * slab))

    tower = jnp.concatenate(
        [along(piece(hop), hop) if hop else piece(0) for hop in range(line)]
    )
    pair_tower = swap(tower)
    flops = 4 * size * size * slab
    held = [pltpu.VMEM((line, count, 2 * slab), jnp.bfloat16)] * 2
    own_blocks = call(
        own_blocks_kernel,
        jax.ShapeDtypeStruct((line, count, 2 * size), jnp.bfloat16),
        [meta, tower, pair_tower],
        2 * flops,
        scratch=held,
    )
    own_shard = summed(own_blocks, sent(own_blocks))
    one, two = after(across(tower, 0), own_shard), after(across(tower, 1), own_shard)
    pair_one, pair_two = swap(one), swap(two)
    side_blocks = call(
        side_blocks_kernel,
        jax.ShapeDtypeStruct((line, count, 2 * size), jnp.bfloat16),
        [meta, tower, one, two, pair_one, pair_two],
        2 * flops,
        scratch=held,
    )
    def columns(orders, *blocks):
        return call(
            functools.partial(columns_kernel, slab, orders),
            jax.ShapeDtypeStruct((len(orders), 2, line, slab, count), jnp.bfloat16),
            [meta] + list(blocks),
            size * slab * 128 * len(orders),
            scratch=[pltpu.VMEM((len(orders), 2, line, count, slab), jnp.bfloat16)],
        )

    side_sent = sent(side_blocks)
    near_columns = columns((0, 1, 2), tower, one, two, pair_tower, pair_one, pair_two)
    three = after(across(one, 1), side_sent[0], side_sent[-1], near_columns)
    pair_three = swap(three)
    corner_blocks = call(
        corner_blocks_kernel,
        jax.ShapeDtypeStruct((line, count, size), jnp.bfloat16),
        [meta, tower, three, pair_three],
        flops,
        scratch=held,
    )
    far_columns = columns((3,), three, pair_three)
    side_shard = summed(side_blocks, side_sent)
    corner_shard = summed(corner_blocks, sent(corner_blocks))
    shard = jnp.concatenate([own_shard, side_shard, corner_shard], axis=1)

    cut = line // 2
    turned = (4, 2, line, slab, count)
    near, ring, one, two, three = [shard], [], [], [], []

    def pieces(slots):
        own = [[near[i], one[i], two[i], three[i]] for i in slots]
        return [v for blocks in own for v in blocks + [swap(block) for block in blocks]]

    def early():
        return call(
            functools.partial(early_kernel, cut),
            jax.ShapeDtypeStruct(turned, jnp.float32),
            [meta, near_columns, far_columns] + pieces(range(cut)),
            128 * cut * count * size * slab,
            scratch=[
                pltpu.VMEM(turned, jnp.bfloat16),
                pltpu.VMEM((4, 2, cut, count, 5 * size), jnp.bfloat16),
                pltpu.VMEM(turned, jnp.float32),
                pltpu.SemaphoreType.DMA((8 * cut + 2,)),
                pltpu.SemaphoreType.DMA((8,)),
            ],
            space=pl.ANY,
            out_space=pl.ANY,
        )

    for step in range(line + 1):
        done = [blocks[-1] for blocks in (ring, one, two, three) if blocks]
        if step == line:
            acc = early()
            done.append(acc)
        if step:
            three.append(across(after(one[-1], *done), 1))
        if step < line:
            here = after(near[step], *done) if step else near[0]
            one.append(across(here, 0))
            two.append(across(here, 1))
        if step < line - 1:
            ring.append(along(here, 1))
            near.append(ring[-1])
    update = call(
        functools.partial(last_kernel, gain, line - cut),
        jax.ShapeDtypeStruct((line, 2, count, slab), jnp.bfloat16),
        [meta, near_columns, far_columns, acc] + pieces(range(line)),
        (128 * (line - cut) * count + 32 * size) * size * slab,
        scratch=[
            pltpu.VMEM(turned, jnp.bfloat16),
            pltpu.VMEM((4, 2, line - cut, count, 5 * size), jnp.bfloat16),
            pltpu.VMEM((2, line, slab, count), jnp.float32),
            pltpu.VMEM(turned, jnp.bfloat16),
            pltpu.VMEM((2, line, count, 5 * size), jnp.bfloat16),
            pltpu.VMEM((3, 2, line, count, size), jnp.bfloat16),
            pltpu.VMEM((line, slab, count), jnp.float32),
            pltpu.SemaphoreType.DMA((8 * (line - cut) + 2,)),
            pltpu.SemaphoreType.DMA((2,)),
            pltpu.SemaphoreType.DMA((8 * line,)),
        ],
        space=pl.ANY,
    )
    return update.reshape(2 * size, slab)


def solution(mesh):
    square_of_lines = mesh.shape["row"] == 4 and mesh.shape["col"] in (4, 6, 8)

    def program(iterate):
        gain = output_gain * math.sqrt(max(iterate.shape))
        plan = neighbour_plan if square_of_lines else gathered_plan
        return jax.shard_map(
            lambda block: plan(block, gain),
            mesh=mesh,
            in_specs=(P(("row", "col"), None),),
            out_specs=P("row", "col"),
            check_vma=False,
        )(iterate)

    return program
```

time: 303 us -> 276 us (0.911)
  starting transfers between devices: 80.2 us -> 51 us
  waiting for transfers between devices: 117 us -> 140 us
  local copies, waits for them, and re-layouts: 25.5 us -> 6.66 us
    ppermute x15, waiting for transfers between devices: 53.3 us -> 83 us  [along(): return lax.ppermute(values, 'col', pairs)]
    ppermute x15, starting transfers between devices: 39.9 us -> 24.8 us  [along(): return lax.ppermute(values, 'col', pairs)]
    unnamed x140 -> x50, local copies, waits for them, and re-layouts: 18.4 us -> 4.18 us
    ppermute x32 -> x15, starting transfers between devices: 34.6 us -> 23.1 us  [across(): return lax.ppermute(values, ('row', 'col'), pairs)]
    ppermute x32 -> x15, waiting for transfers between devices: 60 us -> 49.6 us  [across(): return lax.ppermute(values, ('row', 'col'), pairs)]
    ppermute x40 -> x20, waiting for transfers between devices: 3.54 us -> 7.29 us  [swap(): return lax.ppermute(values, 'col', pairs)]
    slice x16 -> x0, local copies, waits for them, and re-layouts: 3.17 us -> none  [the longest x8 2.99 us: neighbour_plan(): slot[3], slot[4] = (across(one[:half], 2), across(two[half:], 1))]
    pallas_call x6 -> x7, Pallas kernels: 76.4 us -> 76 us  [call(): pl.pallas_call(kernel, in_specs=specs, out_specs=pl.BlockSpec(memory_spac...]
  transfers between devices with their start and end apart: 87 -> 50, of which waited for: 26 -> 24; matrix products, arithmetic and copies ran while one was open for 2% -> 1% of each run, Pallas kernels for 14% -> 16%
where the time goes in v2:
time: 276 us
  waiting for transfers between devices  140 us (51%)
  Pallas kernels  76 us (28%)
  starting transfers between devices  51 us (18%)
  local copies, waits for them, and re-layouts  6.66 us (2%)
    ppermute x15, waiting for transfers between devices, along(): return lax.ppermute(values, 'col', pairs)  83 us
    pallas_call x7, Pallas kernels, call(): pl.pallas_call(kernel, in_specs=specs, out_specs=pl.BlockSpec(memory_spac...  76 us
    ppermute x15, waiting for transfers between devices, across(): return lax.ppermute(values, ('row', 'col'), pairs)  49.6 us
    ppermute x15, starting transfers between devices, along(): return lax.ppermute(values, 'col', pairs)  24.8 us
    ppermute x15, starting transfers between devices, across(): return lax.ppermute(values, ('row', 'col'), pairs)  23.1 us
    ppermute x20, waiting for transfers between devices, swap(): return lax.ppermute(values, 'col', pairs)  7.29 us
  transfers between devices with their start and end apart: 50, of which 24 were waited for; matrix products, arithmetic and copies ran while one was open for 1% of the time, Pallas kernels for 16%

profile of v2, /device:TPU:0, one launch (start us, length us, event | category | flops | bytes accessed | tf_op | source)
XLA Modules:
  0.0 276.0 jit_solution(5124126958744925372)
XLA Ops:
  1.5 5.1 %collective-permute-start = (bf16[128,1536]{1,0:T(8,128)(2,1)S(1)}, bf16[128,1536]{1,0:T(8,128)(2,1)S(1)}, u32[]{:S(2)}, u32[]{:S(2)}) collective-permute-start(bf16[128,1536]{1,0:T(8,128)(2,1)S(1)} %get-tuple-element.26), channel_id=1, source_target_pairs={{0,6},{1,7},{2,0},{3,1},{4,2},{5,3},{6,4},{7,5},{8,14},{9,15},{10,... | collective-permute-start | bytes 1179656 | tf_op jit(solution)/shard_map/ppermute | solution.py:357
  7.6 8.5 %collective-permute-done = bf16[128,1536]{1,0:T(8,128)(2,1)S(1)} collective-permute-done((bf16[128,1536]{1,0:T(8,128)(2,1)S(1)}, bf16[128,1536]{1,0:T(8,128)(2,1)S(1)}, u32[]{:S(2)}, u32[]{:S(2)}) %collective-permute-start) | collective-permute-done | bytes 393248 | tf_op jit(solution)/shard_map/ppermute | solution.py:357
  16.1 9.4 %collective-permute-done.2 = bf16[128,1536]{1,0:T(8,128)(2,1)S(1)} collective-permute-done((bf16[128,1536]{1,0:T(8,128)(2,1)S(1)}, bf16[128,1536]{1,0:T(8,128)(2,1)S(1)}, u32[]{:S(2)}, u32[]{:S(2)}) %collective-permute-start.2) | collective-permute-done | bytes 393248 | tf_op jit(solution)/shard_map/ppermute | solution.py:357
  25.5 14.6 %collective-permute-done.1 = bf16[128,1536]{1,0:T(8,128)(2,1)S(1)} collective-permute-done((bf16[128,1536]{1,0:T(8,128)(2,1)S(1)}, bf16[128,1536]{1,0:T(8,128)(2,1)S(1)}, u32[]{:S(2)}, u32[]{:S(2)}) %collective-permute-start.1) | collective-permute-done | bytes 393248 | tf_op jit(solution)/shard_map/ppermute | solution.py:357
  43.8 4.0 %shard_map.17 = bf16[4,128,1024]{2,1,0:T(8,128)(2,1)S(1)} custom-call(s32[4]{0:T(128)S(1)} %pad_add_fusion.meta_ref, bf16[512,1536]{1,0:T(8,128)(2,1)S(1)} %pad_maximum_fusion.refs_0_, bf16[512,1536]{1,0:T(8,128)(2,1)} %collective-permute-done.4.refs_1_.refs_3_), custom_call_target="tpu_custom_call" | custom-call | flops 1610612736 | bytes 3145744 | tf_op jit(solution)/shard_map/pallas_call | solution.py:66
  49.8 2.6 collective-permute-start.5
  53.0 12.6 %collective-permute-done.5 = bf16[128,1024]{1,0:T(8,128)(2,1)S(1)} collective-permute-done((bf16[128,1024]{1,0:T(8,128)(2,1)}, bf16[128,1024]{1,0:T(8,128)(2,1)S(1)}, u32[]{:S(2)}, u32[]{:S(2)}) %collective-permute-start.5) | collective-permute-done | bytes 262176 | tf_op jit(solution)/shard_map/ppermute | solution.py:357
  65.5 9.0 %collective-permute-done.6 = bf16[128,1024]{1,0:T(8,128)(2,1)} collective-permute-done((bf16[128,1024]{1,0:T(8,128)(2,1)}, bf16[128,1024]{1,0:T(8,128)(2,1)}, u32[]{:S(2)}, u32[]{:S(2)}) %collective-permute-start.6) | collective-permute-done | bytes 262176 | tf_op jit(solution)/shard_map/ppermute | solution.py:357
  84.0 5.1 %shard_map.19 = bf16[4,128,1024]{2,1,0:T(8,128)(2,1)S(1)} custom-call(s32[4]{0:T(128)S(1)} %pad_add_fusion.meta_ref, bf16[512,1536]{1,0:T(8,128)(2,1)S(1)} %pad_maximum_fusion.refs_0_, bf16[512,1536]{1,0:T(8,128)(2,1)} %collective-permute-done.3.refs_1_, bf16[512,1536]{1,0:T(8,128)(2,1)S(1)} %collective-permute-done.8.refs_2_, bf16[512,1536]{1,0:T(8,128)(2,1)} %copy-done.3, ...), custom_call_target="tpu_custom_call" | custom-call | flops 1610612736 | bytes 7864336 | tf_op jit(solution)/shard_map/pallas_call | solution.py:66
  89.3 3.8 %collective-permute-start.12 = (bf16[128,1024]{1,0:T(8,128)(2,1)S(1)}, bf16[128,1024]{1,0:T(8,128)(2,1)S(1)}, u32[]{:S(2)}, u32[]{:S(2)}) collective-permute-start(bf16[128,1024]{1,0:T(8,128)(2,1)S(1)} %get-tuple-element.31), channel_id=1, source_target_pairs={{0,6},{1,7},{2,0},{3,1},{4,2},{5,3},{6,4},{7,5},{8,14},{9,15},{10,... | collective-permute-start | bytes 786440 | tf_op jit(solution)/shard_map/ppermute | solution.py:357
  93.1 8.0 %shard_map.18.near_hbm = bf16[3,2,4,768,128]{4,3,2,1,0:T(8,128)(2,1)} custom-call(s32[4]{0:T(128)S(1)} %pad_add_fusion.meta_ref, bf16[512,1536]{1,0:T(8,128)(2,1)S(1)} %pad_maximum_fusion.refs_0_, bf16[512,1536]{1,0:T(8,128)(2,1)} %collective-permute-done.3.refs_1_, bf16[512,1536]{1,0:T(8,128)(2,1)S(1)} %collective-permute-done.8.refs_2_, ...), custom_call_target="tpu_custom_call" | custom-call | flops 150994944 | bytes 9437200 | tf_op jit(solution)/shard_map/pallas_call | solution.py:66
  113.2 11.4 %collective-permute-done.15 = bf16[128,1024]{1,0:T(8,128)(2,1)S(1)} collective-permute-done((bf16[128,1024]{1,0:T(8,128)(2,1)S(1)}, bf16[128,1024]{1,0:T(8,128)(2,1)S(1)}, u32[]{:S(2)}, u32[]{:S(2)}) %collective-permute-start.15) | collective-permute-done | bytes 262176 | tf_op jit(solution)/shard_map/ppermute | solution.py:357
  124.8 5.0 %collective-permute-done.17 = bf16[128,512]{1,0:T(8,128)(2,1)S(1)} collective-permute-done((bf16[128,512]{1,0:T(8,128)(2,1)S(1)}, bf16[128,512]{1,0:T(8,128)(2,1)S(1)}, u32[]{:S(2)}, u32[]{:S(2)}) %collective-permute-start.17) | collective-permute-done | bytes 131104 | tf_op jit(solution)/shard_map/ppermute | solution.py:357
  134.1 2.7 collective-permute-start.19
  136.9 9.6 %collective-permute-done.21.refs_8_ = bf16[128,2560]{1,0:T(8,128)(2,1)S(1)} collective-permute-done((bf16[128,2560]{1,0:T(8,128)(2,1)S(1)}, bf16[128,2560]{1,0:T(8,128)(2,1)S(1)}, u32[]{:S(2)}, u32[]{:S(2)}) %collective-permute-start.21) | collective-permute-done | bytes 655392 | tf_op jit(solution)/shard_map/ppermute | solution.py:357
  146.5 2.8 %collective-permute-done.20.refs_2_ = bf16[128,2560]{1,0:T(8,128)(2,1)S(1)} collective-permute-done((bf16[128,2560]{1,0:T(8,128)(2,1)S(1)}, bf16[128,2560]{1,0:T(8,128)(2,1)S(1)}, u32[]{:S(2)}, u32[]{:S(2)}) %collective-permute-start.20) | collective-permute-done | bytes 655392 | tf_op jit(solution)/shard_map/ppermute | solution.py:369
  152.8 2.7 collective-permute-start.27
  155.6 10.5 %collective-permute-done.22.refs_3_ = bf16[128,2560]{1,0:T(8,128)(2,1)S(1)} collective-permute-done((bf16[128,2560]{1,0:T(8,128)(2,1)S(1)}, bf16[128,2560]{1,0:T(8,128)(2,1)S(1)}, u32[]{:S(2)}, u32[]{:S(2)}) %collective-permute-start.22) | collective-permute-done | bytes 655392 | tf_op jit(solution)/shard_map/ppermute | solution.py:369
  166.7 7.6 %collective-permute-done.28.refs_10_ = bf16[128,2560]{1,0:T(8,128)(2,1)S(1)} collective-permute-done((bf16[128,2560]{1,0:T(8,128)(2,1)S(1)}, bf16[128,2560]{1,0:T(8,128)(2,1)S(1)}, u32[]{:S(2)}, u32[]{:S(2)}) %collective-permute-start.28) | collective-permute-done | bytes 655392 | tf_op jit(solution)/shard_map/ppermute | solution.py:369
  179.6 11.9 %collective-permute-done.30.refs_11_ = bf16[128,2560]{1,0:T(8,128)(2,1)S(1)} collective-permute-done((bf16[128,2560]{1,0:T(8,128)(2,1)S(1)}, bf16[128,2560]{1,0:T(8,128)(2,1)S(1)}, u32[]{:S(2)}, u32[]{:S(2)}) %collective-permute-start.30) | collective-permute-done | bytes 655392 | tf_op jit(solution)/shard_map/ppermute | solution.py:369
  192.0 7.0 %collective-permute-done.36.refs_18_ = bf16[128,2560]{1,0:T(8,128)(2,1)S(1)} collective-permute-done((bf16[128,2560]{1,0:T(8,128)(2,1)S(1)}, bf16[128,2560]{1,0:T(8,128)(2,1)S(1)}, u32[]{:S(2)}, u32[]{:S(2)}) %collective-permute-start.36) | collective-permute-done | bytes 655392 | tf_op jit(solution)/shard_map/ppermute | solution.py:369
  206.2 22.8 %shard_map.22.acc_hbm = f32[4,2,4,768,128]{4,3,2,1,0:T(8,128)} custom-call(s32[4]{0:T(128)S(1)} %pad_add_fusion.meta_ref, bf16[3,2,4,768,128]{4,3,2,1,0:T(8,128)(2,1)} %shard_map.18.near_hbm, bf16[1,2,4,768,128]{4,3,2,1,0:T(8,128)(2,1)} %copy-done, bf16[128,2560]{1,0:T(8,128)(2,1)S(1)} %pad_maximum_fusion.1.refs_0_, ...), custom_call_target="tpu_custom_call" | custom-call | flops 12884901888 | bytes 16777232 | tf_op jit(solution)/shard_map/pallas_call | solution.py:66
  232.2 8.0 %collective-permute-done.45.refs_27_ = bf16[128,2560]{1,0:T(8,128)(2,1)S(1)} collective-permute-done((bf16[128,2560]{1,0:T(8,128)(2,1)S(1)}, bf16[128,2560]{1,0:T(8,128)(2,1)S(1)}, u32[]{:S(2)}, u32[]{:S(2)}) %collective-permute-start.45) | collective-permute-done | bytes 655392 | tf_op jit(solution)/shard_map/ppermute | solution.py:369
  243.3 32.5 %shard_map.23 = bf16[4,2,128,768]{3,2,1,0:T(8,128)(2,1)} custom-call(s32[4]{0:T(128)S(1)} %pad_add_fusion.meta_ref, bf16[3,2,4,768,128]{4,3,2,1,0:T(8,128)(2,1)} %shard_map.18.near_hbm, bf16[1,2,4,768,128]{4,3,2,1,0:T(8,128)(2,1)} %copy-done, f32[4,2,4,768,128]{4,3,2,1,0:T(8,128)} %shard_map.22.acc_hbm, bf16[128,2560]{1,0:T(8,128)(2,1)S(1)} %pad_maximum_fusion.1.refs_0_, ...), custom_call_target="tpu_custom_call" | custom-call | flops 19327352832 | bytes 39845904 | tf_op jit(solution)/shard_map/pallas_call | solution.py:66
  (143 shorter events, 57.7 us)
Async XLA Ops:
  6.6 19.0 %collective-permute-start.2 = (bf16[128,1536]{1,0:T(8,128)(2,1)S(1)}, bf16[128,1536]{1,0:T(8,128)(2,1)S(1)}, u32[]{:S(2)}, u32[]{:S(2)}) collective-permute-start(bf16[128,1536]{1,0:T(8,128)(2,1)S(1)} %get-tuple-element.27), channel_id=1, source_target_pairs={{0,2},{1,3},{2,4},{3,5},{4,6},{5,7},{6,0},{7,1},{8,10},{9,11},{10,... | collective-permute-start | bytes 1179656 | tf_op jit(solution)/shard_map/ppermute | solution.py:357
  6.6 33.5 %collective-permute-start.1 = (bf16[128,1536]{1,0:T(8,128)(2,1)S(1)}, bf16[128,1536]{1,0:T(8,128)(2,1)S(1)}, u32[]{:S(2)}, u32[]{:S(2)}) collective-permute-start(bf16[128,1536]{1,0:T(8,128)(2,1)S(1)} %get-tuple-element.28), channel_id=1, source_target_pairs={{0,4},{1,5},{2,6},{3,7},{4,0},{5,1},{6,2},{7,3},{8,12},{9,13},{10,... | collective-permute-start | bytes 1179656 | tf_op jit(solution)/shard_map/ppermute | solution.py:357
  40.3 36.7 %collective-permute-start.8 = (bf16[512,1536]{1,0:T(8,128)(2,1)S(1)}, bf16[512,1536]{1,0:T(8,128)(2,1)S(1)}, u32[]{:S(2)}, u32[]{:S(2)}) collective-permute-start(bf16[512,1536]{1,0:T(8,128)(2,1)S(1)} %pad_maximum_fusion.refs_0_), channel_id=1, source_target_pairs={{0,16},{1,9},{2,18},{3,11},{4,20},{5,13},{6,22},{7,15},{8,24},{9,1... | collective-permute-start | bytes 4718600 | tf_op jit(solution)/shard_map/ppermute | solution.py:369
  41.9 35.3 %collective-permute-start.3 = (bf16[512,1536]{1,0:T(8,128)(2,1)S(1)}, bf16[512,1536]{1,0:T(8,128)(2,1)}, u32[]{:S(2)}, u32[]{:S(2)}) collective-permute-start(bf16[512,1536]{1,0:T(8,128)(2,1)S(1)} %pad_maximum_fusion.refs_0_), channel_id=1, source_target_pairs={{0,8},{1,17},{2,10},{3,19},{4,12},{5,21},{6,14},{7,23},{8,0},{9,25... | collective-permute-start | bytes 4718600 | tf_op jit(solution)/shard_map/ppermute | solution.py:369
  52.4 22.2 %collective-permute-start.6 = (bf16[128,1024]{1,0:T(8,128)(2,1)}, bf16[128,1024]{1,0:T(8,128)(2,1)}, u32[]{:S(2)}, u32[]{:S(2)}) collective-permute-start(bf16[128,1024]{1,0:T(8,128)(2,1)} %get-tuple-element.34), channel_id=1, source_target_pairs={{0,4},{1,5},{2,6},{3,7},{4,0},{5,1},{6,2},{7,3},{8,12},{9,13},{10,... | collective-permute-start | bytes 786440 | tf_op jit(solution)/shard_map/ppermute | solution.py:357
  77.6 23.6 %collective-permute-start.11 = (bf16[512,1536]{1,0:T(8,128)(2,1)}, bf16[512,1536]{1,0:T(8,128)(2,1)S(1)}, u32[]{:S(2)}, u32[]{:S(2)}) collective-permute-start(bf16[512,1536]{1,0:T(8,128)(2,1)} %collective-permute-done.3.refs_1_), channel_id=1, source_target_pairs={{0,16},{1,9},{2,18},{3,11},{4,20},{5,13},{6,22},{7,15},{8,24},{9,1... | collective-permute-start | bytes 4718600 | tf_op jit(solution)/shard_map/ppermute | solution.py:369
  103.3 21.3 %collective-permute-start.15 = (bf16[128,1024]{1,0:T(8,128)(2,1)S(1)}, bf16[128,1024]{1,0:T(8,128)(2,1)S(1)}, u32[]{:S(2)}, u32[]{:S(2)}) collective-permute-start(bf16[128,1024]{1,0:T(8,128)(2,1)S(1)} %get-tuple-element.29), channel_id=1, source_target_pairs={{0,4},{1,5},{2,6},{3,7},{4,0},{5,1},{6,2},{7,3},{8,12},{9,13},{10,... | collective-permute-start | bytes 786440 | tf_op jit(solution)/shard_map/ppermute | solution.py:357
  108.8 16.0 %collective-permute-start.16 = (bf16[128,512]{1,0:T(8,128)(2,1)S(1)}, bf16[128,512]{1,0:T(8,128)(2,1)S(1)}, u32[]{:S(2)}, u32[]{:S(2)}) collective-permute-start(bf16[128,512]{1,0:T(8,128)(2,1)S(1)} %get-tuple-element.35), channel_id=1, source_target_pairs={{0,6},{1,7},{2,0},{3,1},{4,2},{5,3},{6,4},{7,5},{8,14},{9,15},{10,... | collective-permute-start | bytes 393224 | tf_op jit(solution)/shard_map/ppermute | solution.py:357
  111.4 18.4 %collective-permute-start.17 = (bf16[128,512]{1,0:T(8,128)(2,1)S(1)}, bf16[128,512]{1,0:T(8,128)(2,1)S(1)}, u32[]{:S(2)}, u32[]{:S(2)}) collective-permute-start(bf16[128,512]{1,0:T(8,128)(2,1)S(1)} %get-tuple-element.37), channel_id=1, source_target_pairs={{0,4},{1,5},{2,6},{3,7},{4,0},{5,1},{6,2},{7,3},{8,12},{9,13},{10,... | collective-permute-start | bytes 393224 | tf_op jit(solution)/shard_map/ppermute | solution.py:357
  130.0 16.5 %collective-permute-start.21 = (bf16[128,2560]{1,0:T(8,128)(2,1)S(1)}, bf16[128,2560]{1,0:T(8,128)(2,1)S(1)}, u32[]{:S(2)}, u32[]{:S(2)}) collective-permute-start(bf16[128,2560]{1,0:T(8,128)(2,1)S(1)} %pad_maximum_fusion.1.refs_0_), channel_id=1, source_target_pairs={{0,6},{1,7},{2,0},{3,1},{4,2},{5,3},{6,4},{7,5},{8,14},{9,15},{10,... | collective-permute-start | bytes 1966088 | tf_op jit(solution)/shard_map/ppermute | solution.py:357
  132.6 16.7 %collective-permute-start.20 = (bf16[128,2560]{1,0:T(8,128)(2,1)S(1)}, bf16[128,2560]{1,0:T(8,128)(2,1)S(1)}, u32[]{:S(2)}, u32[]{:S(2)}) collective-permute-start(bf16[128,2560]{1,0:T(8,128)(2,1)S(1)} %pad_maximum_fusion.1.refs_0_), channel_id=1, source_target_pairs={{0,16},{1,9},{2,18},{3,11},{4,20},{5,13},{6,22},{7,15},{8,24},{9,1... | collective-permute-start | bytes 1966088 | tf_op jit(solution)/shard_map/ppermute | solution.py:369
  149.7 16.4 %collective-permute-start.22 = (bf16[128,2560]{1,0:T(8,128)(2,1)S(1)}, bf16[128,2560]{1,0:T(8,128)(2,1)S(1)}, u32[]{:S(2)}, u32[]{:S(2)}) collective-permute-start(bf16[128,2560]{1,0:T(8,128)(2,1)S(1)} %collective-permute-done.19.refs_1_), channel_id=1, source_target_pairs={{0,16},{1,9},{2,18},{3,11},{4,20},{5,13},{6,22},{7,15},{8,24},{9,1... | collective-permute-start | bytes 1966088 | tf_op jit(solution)/shard_map/ppermute | solution.py:369
  152.3 22.0 %collective-permute-start.28 = (bf16[128,2560]{1,0:T(8,128)(2,1)S(1)}, bf16[128,2560]{1,0:T(8,128)(2,1)S(1)}, u32[]{:S(2)}, u32[]{:S(2)}) collective-permute-start(bf16[128,2560]{1,0:T(8,128)(2,1)S(1)} %collective-permute-done.21.refs_8_), channel_id=1, source_target_pairs={{0,16},{1,9},{2,18},{3,11},{4,20},{5,13},{6,22},{7,15},{8,24},{9,1... | collective-permute-start | bytes 1966088 | tf_op jit(solution)/shard_map/ppermute | solution.py:369
  152.8 21.5 %collective-permute-start.27 = (bf16[128,2560]{1,0:T(8,128)(2,1)S(1)}, bf16[128,2560]{1,0:T(8,128)(2,1)S(1)}, u32[]{:S(2)}, u32[]{:S(2)}) collective-permute-start(bf16[128,2560]{1,0:T(8,128)(2,1)S(1)} %collective-permute-done.21.refs_8_), channel_id=1, source_target_pairs={{0,8},{1,17},{2,10},{3,19},{4,12},{5,21},{6,14},{7,23},{8,0},{9,25... | collective-permute-start | bytes 1966088 | tf_op jit(solution)/shard_map/ppermute | solution.py:369
  155.6 21.5 %collective-permute-start.23 = (bf16[128,2560]{1,0:T(8,128)(2,1)S(1)}, bf16[128,2560]{1,0:T(8,128)(2,1)S(1)}, u32[]{:S(2)}, u32[]{:S(2)}) collective-permute-start(bf16[128,2560]{1,0:T(8,128)(2,1)S(1)} %pad_maximum_fusion.1.refs_0_), channel_id=1, source_target_pairs={{0,1},{1,0},{2,3},{3,2},{4,5},{5,4},{6,7},{7,6},{8,9},{9,8},{10,11... | collective-permute-start | bytes 1966088 | tf_op jit(solution)/shard_map/ppermute | solution.py:361
  174.3 17.2 %collective-permute-start.30 = (bf16[128,2560]{1,0:T(8,128)(2,1)S(1)}, bf16[128,2560]{1,0:T(8,128)(2,1)S(1)}, u32[]{:S(2)}, u32[]{:S(2)}) collective-permute-start(bf16[128,2560]{1,0:T(8,128)(2,1)S(1)} %collective-permute-done.27.refs_9_), channel_id=1, source_target_pairs={{0,16},{1,9},{2,18},{3,11},{4,20},{5,13},{6,22},{7,15},{8,24},{9,1... | collective-permute-start | bytes 1966088 | tf_op jit(solution)/shard_map/ppermute | solution.py:369
  177.0 22.0 %collective-permute-start.36 = (bf16[128,2560]{1,0:T(8,128)(2,1)S(1)}, bf16[128,2560]{1,0:T(8,128)(2,1)S(1)}, u32[]{:S(2)}, u32[]{:S(2)}) collective-permute-start(bf16[128,2560]{1,0:T(8,128)(2,1)S(1)} %collective-permute-done.29.refs_16_), channel_id=1, source_target_pairs={{0,16},{1,9},{2,18},{3,11},{4,20},{5,13},{6,22},{7,15},{8,24},{9,1... | collective-permute-start | bytes 1966088 | tf_op jit(solution)/shard_map/ppermute | solution.py:369
  177.5 21.5 %collective-permute-start.35 = (bf16[128,2560]{1,0:T(8,128)(2,1)S(1)}, bf16[128,2560]{1,0:T(8,128)(2,1)S(1)}, u32[]{:S(2)}, u32[]{:S(2)}) collective-permute-start(bf16[128,2560]{1,0:T(8,128)(2,1)S(1)} %collective-permute-done.29.refs_16_), channel_id=1, source_target_pairs={{0,8},{1,17},{2,10},{3,19},{4,12},{5,21},{6,14},{7,23},{8,0},{9,25... | collective-permute-start | bytes 1966088 | tf_op jit(solution)/shard_map/ppermute | solution.py:369
  179.6 22.7 %collective-permute-start.24 = (bf16[128,2560]{1,0:T(8,128)(2,1)S(1)}, bf16[128,2560]{1,0:T(8,128)(2,1)S(1)}, u32[]{:S(2)}, u32[]{:S(2)}) collective-permute-start(bf16[128,2560]{1,0:T(8,128)(2,1)S(1)} %collective-permute-done.19.refs_1_), channel_id=1, source_target_pairs={{0,1},{1,0},{2,3},{3,2},{4,5},{5,4},{6,7},{7,6},{8,9},{9,8},{10,11... | collective-permute-start | bytes 1966088 | tf_op jit(solution)/shard_map/ppermute | solution.py:361
  202.3 28.9 %collective-permute-start.39 = (bf16[128,2560]{1,0:T(8,128)(2,1)S(1)}, bf16[128,2560]{1,0:T(8,128)(2,1)S(1)}, u32[]{:S(2)}, u32[]{:S(2)}) collective-permute-start(bf16[128,2560]{1,0:T(8,128)(2,1)S(1)} %collective-permute-done.29.refs_16_), channel_id=1, source_target_pairs={{0,1},{1,0},{2,3},{3,2},{4,5},{5,4},{6,7},{7,6},{8,9},{9,8},{10,11... | collective-permute-start | bytes 1966088 | tf_op jit(solution)/shard_map/ppermute | solution.py:361
  202.4 27.2 %collective-permute-start.44 = (bf16[128,2560]{1,0:T(8,128)(2,1)S(1)}, bf16[128,2560]{1,0:T(8,128)(2,1)S(1)}, u32[]{:S(2)}, u32[]{:S(2)}) collective-permute-start(bf16[128,2560]{1,0:T(8,128)(2,1)S(1)} %collective-permute-done.37.refs_24_), channel_id=1, source_target_pairs={{0,16},{1,9},{2,18},{3,11},{4,20},{5,13},{6,22},{7,15},{8,24},{9,1... | collective-permute-start | bytes 1966088 | tf_op jit(solution)/shard_map/ppermute | solution.py:369
  203.9 25.7 %collective-permute-start.43 = (bf16[128,2560]{1,0:T(8,128)(2,1)S(1)}, bf16[128,2560]{1,0:T(8,128)(2,1)S(1)}, u32[]{:S(2)}, u32[]{:S(2)}) collective-permute-start(bf16[128,2560]{1,0:T(8,128)(2,1)S(1)} %collective-permute-done.37.refs_24_), channel_id=1, source_target_pairs={{0,8},{1,17},{2,10},{3,19},{4,12},{5,21},{6,14},{7,23},{8,0},{9,25... | collective-permute-start | bytes 1966088 | tf_op jit(solution)/shard_map/ppermute | solution.py:369
  205.7 23.4 %collective-permute-start.38 = (bf16[128,2560]{1,0:T(8,128)(2,1)S(1)}, bf16[128,2560]{1,0:T(8,128)(2,1)S(1)}, u32[]{:S(2)}, u32[]{:S(2)}) collective-permute-start(bf16[128,2560]{1,0:T(8,128)(2,1)S(1)} %collective-permute-done.35.refs_17_), channel_id=1, source_target_pairs={{0,16},{1,9},{2,18},{3,11},{4,20},{5,13},{6,22},{7,15},{8,24},{9,1... | collective-permute-start | bytes 1966088 | tf_op jit(solution)/shard_map/ppermute | solution.py:369
  206.2 25.6 %collective-permute-start.46 = (bf16[128,2560]{1,0:T(8,128)(2,1)S(1)}, bf16[128,2560]{1,0:T(8,128)(2,1)S(1)}, u32[]{:S(2)}, u32[]{:S(2)}) collective-permute-start(bf16[128,2560]{1,0:T(8,128)(2,1)S(1)} %collective-permute-done.37.refs_24_), channel_id=1, source_target_pairs={{0,1},{1,0},{2,3},{3,2},{4,5},{5,4},{6,7},{7,6},{8,9},{9,8},{10,11... | collective-permute-start | bytes 1966088 | tf_op jit(solution)/shard_map/ppermute | solution.py:361
  (51 other events, 547.7 us)

commit v3 on v2

--- a/solution.py
+++ b/solution.py
@@ -399,6 +399,8 @@
     )
     own_shard = summed(own_blocks, sent(own_blocks))
     one, two = after(across(tower, 0), own_shard), after(across(tower, 1), own_shard)
+    own_ring = along(own_shard, 1)
+    own_one, own_two = across(own_shard, 0), across(own_shard, 1)
     pair_one, pair_two = swap(one), swap(two)
     side_blocks = call(
         side_blocks_kernel,
@@ -411,7 +413,7 @@
         return call(
             functools.partial(columns_kernel, slab, orders),
             jax.ShapeDtypeStruct((len(orders), 2, line, slab, count), jnp.bfloat16),
-            [meta] + list(blocks),
+            [after(meta, own_ring)] + list(blocks),
             size * slab * 128 * len(orders),
             scratch=[pltpu.VMEM((len(orders), 2, line, count, slab), jnp.bfloat16)],
         )
@@ -429,12 +431,23 @@
     )
     far_columns = columns((3,), three, pair_three)
     side_shard = summed(side_blocks, side_sent)
-    corner_shard = summed(corner_blocks, sent(corner_blocks))
-    shard = jnp.concatenate([own_shard, side_shard, corner_shard], axis=1)
+    own_three = across(own_one, 1)
+    corner_sent = [after(chunk, own_two, own_three) for chunk in sent(corner_blocks)]
+    corner_shard = summed(corner_blocks, corner_sent)
+    cross_shard = jnp.concatenate([side_shard, corner_shard], axis=1)
 
     cut = line // 2
     turned = (4, 2, line, slab, count)
-    near, ring, one, two, three = [shard], [], [], [], []
+
+    def wide(own, cross):
+        return jnp.concatenate([own, cross], axis=1)
+
+    cross_ring = along(cross_shard, 1)
+    cross_one, cross_two = across(cross_shard, 0), across(cross_shard, 1)
+    held_back = [cross_ring, cross_one, cross_two, far_columns]
+    near = [wide(own_shard, cross_shard), wide(own_ring, after(cross_ring, *held_back))]
+    one, two = [wide(own_one, cross_one)], [wide(own_two, cross_two)]
+    three, ring = [], [near[1]]
 
     def pieces(slots):
         own = [[near[i], one[i], two[i], three[i]] for i in slots]
@@ -457,15 +470,18 @@
             out_space=pl.ANY,
         )
 
-    for step in range(line + 1):
-        done = [blocks[-1] for blocks in (ring, one, two, three) if blocks]
+    for step in range(1, line + 1):
+        done = held_back if step == 1 else [b[-1] for b in (ring, one, two, three)]
         if step == line:
             acc = early()
-            done.append(acc)
-        if step:
+            done = done + [acc]
+        if step == 1:
+            cross_three = across(after(cross_one, *done), 1)
+            three.append(wide(own_three, cross_three))
+        else:
             three.append(across(after(one[-1], *done), 1))
         if step < line:
-            here = after(near[step], *done) if step else near[0]
+            here = after(near[step], *done)
             one.append(across(here, 0))
             two.append(across(here, 1))
         if step < line - 1:

time: 276 us -> 266 us (0.964)
  waiting for transfers between devices: 140 us -> 125 us
  starting transfers between devices: 51 us -> 56.3 us
    ppermute x15 -> x18, waiting for transfers between devices: 49.6 us -> 39.9 us  [across(): return lax.ppermute(values, ('row', 'col'), pairs)]
    ppermute x20, waiting for transfers between devices: 7.29 us -> 3.72 us  [swap(): return lax.ppermute(values, 'col', pairs)]
    ppermute x15 -> x16, starting transfers between devices: 24.8 us -> 27.6 us  [along(): return lax.ppermute(values, 'col', pairs)]
    ppermute x15 -> x18, starting transfers between devices: 23.1 us -> 26 us  [across(): return lax.ppermute(values, ('row', 'col'), pairs)]
    ppermute x15 -> x16, waiting for transfers between devices: 83 us -> 81.1 us  [along(): return lax.ppermute(values, 'col', pairs)]
  transfers between devices with their start and end apart: 50 -> 54, of which waited for: 24 -> 25; matrix products, arithmetic and copies ran while one was open for 1% -> 1% of each run, Pallas kernels for 16% -> 16%
where the time goes in v3:
time: 266 us
  waiting for transfers between devices  125 us (47%)
  Pallas kernels  76 us (29%)
  starting transfers between devices  56.3 us (21%)
  local copies, waits for them, and re-layouts  6.69 us (3%)
    ppermute x16, waiting for transfers between devices, along(): return lax.ppermute(values, 'col', pairs)  81.1 us
    pallas_call x7, Pallas kernels, call(): pl.pallas_call(kernel, in_specs=specs, out_specs=pl.BlockSpec(memory_spac...  76 us
    ppermute x18, waiting for transfers between devices, across(): return lax.ppermute(values, ('row', 'col'), pairs)  39.9 us
    ppermute x16, starting transfers between devices, along(): return lax.ppermute(values, 'col', pairs)  27.6 us
    ppermute x18, starting transfers between devices, across(): return lax.ppermute(values, ('row', 'col'), pairs)  26 us
  transfers between devices with their start and end apart: 54, of which 25 were waited for; matrix products, arithmetic and copies ran while one was open for 1% of the time, Pallas kernels for 16%

profile of v3, /device:TPU:0, one launch (start us, length us, event | category | flops | bytes accessed | tf_op | source)
XLA Modules:
  0.0 266.2 jit_solution(10266857776209748195)
XLA Ops:
  1.5 5.1 %collective-permute-start = (bf16[128,1536]{1,0:T(8,128)(2,1)S(1)}, bf16[128,1536]{1,0:T(8,128)(2,1)S(1)}, u32[]{:S(2)}, u32[]{:S(2)}) collective-permute-start(bf16[128,1536]{1,0:T(8,128)(2,1)S(1)} %get-tuple-element.36), channel_id=1, source_target_pairs={{0,6},{1,7},{2,0},{3,1},{4,2},{5,3},{6,4},{7,5},{8,14},{9,15},{10,... | collective-permute-start | bytes 1179656 | tf_op jit(solution)/shard_map/ppermute | solution.py:357
  7.6 8.5 %collective-permute-done = bf16[128,1536]{1,0:T(8,128)(2,1)S(1)} collective-permute-done((bf16[128,1536]{1,0:T(8,128)(2,1)S(1)}, bf16[128,1536]{1,0:T(8,128)(2,1)S(1)}, u32[]{:S(2)}, u32[]{:S(2)}) %collective-permute-start) | collective-permute-done | bytes 393248 | tf_op jit(solution)/shard_map/ppermute | solution.py:357
  16.1 9.4 %collective-permute-done.2 = bf16[128,1536]{1,0:T(8,128)(2,1)S(1)} collective-permute-done((bf16[128,1536]{1,0:T(8,128)(2,1)S(1)}, bf16[128,1536]{1,0:T(8,128)(2,1)S(1)}, u32[]{:S(2)}, u32[]{:S(2)}) %collective-permute-start.2) | collective-permute-done | bytes 393248 | tf_op jit(solution)/shard_map/ppermute | solution.py:357
  25.5 14.6 %collective-permute-done.1 = bf16[128,1536]{1,0:T(8,128)(2,1)S(1)} collective-permute-done((bf16[128,1536]{1,0:T(8,128)(2,1)S(1)}, bf16[128,1536]{1,0:T(8,128)(2,1)S(1)}, u32[]{:S(2)}, u32[]{:S(2)}) %collective-permute-start.1) | collective-permute-done | bytes 393248 | tf_op jit(solution)/shard_map/ppermute | solution.py:357
  43.8 4.0 %shard_map.17 = bf16[4,128,1024]{2,1,0:T(8,128)(2,1)S(1)} custom-call(s32[4]{0:T(128)S(1)} %pad_add_fusion.meta_ref, bf16[512,1536]{1,0:T(8,128)(2,1)S(1)} %pad_maximum_fusion.refs_0_, bf16[512,1536]{1,0:T(8,128)(2,1)} %collective-permute-done.3.refs_1_.refs_3_), custom_call_target="tpu_custom_call" | custom-call | flops 1610612736 | bytes 3145744 | tf_op jit(solution)/shard_map/pallas_call | solution.py:66
  52.9 12.6 %collective-permute-done.4 = bf16[128,1024]{1,0:T(8,128)(2,1)S(1)} collective-permute-done((bf16[128,1024]{1,0:T(8,128)(2,1)}, bf16[128,1024]{1,0:T(8,128)(2,1)S(1)}, u32[]{:S(2)}, u32[]{:S(2)}) %collective-permute-start.4) | collective-permute-done | bytes 262176 | tf_op jit(solution)/shard_map/ppermute | solution.py:357
  65.5 9.0 %collective-permute-done.5 = bf16[128,1024]{1,0:T(8,128)(2,1)} collective-permute-done((bf16[128,1024]{1,0:T(8,128)(2,1)}, bf16[128,1024]{1,0:T(8,128)(2,1)}, u32[]{:S(2)}, u32[]{:S(2)}) %collective-permute-start.5) | collective-permute-done | bytes 262176 | tf_op jit(solution)/shard_map/ppermute | solution.py:357
  84.2 5.1 %shard_map.19 = bf16[4,128,1024]{2,1,0:T(8,128)(2,1)S(1)} custom-call(s32[4]{0:T(128)S(1)} %pad_add_fusion.meta_ref, bf16[512,1536]{1,0:T(8,128)(2,1)S(1)} %pad_maximum_fusion.refs_0_, bf16[512,1536]{1,0:T(8,128)(2,1)} %collective-permute-done.8.refs_1_, bf16[512,1536]{1,0:T(8,128)(2,1)S(1)} %collective-permute-done.9.refs_2_, bf16[512,1536]{1,0:T(8,128)(2,1)} %copy-done.2, ...), custom_call_target="tpu_custom_call" | custom-call | flops 1610612736 | bytes 7864336 | tf_op jit(solution)/shard_map/pallas_call | solution.py:66
  89.5 3.8 %collective-permute-start.13 = (bf16[128,1024]{1,0:T(8,128)(2,1)S(1)}, bf16[128,1024]{1,0:T(8,128)(2,1)S(1)}, u32[]{:S(2)}, u32[]{:S(2)}) collective-permute-start(bf16[128,1024]{1,0:T(8,128)(2,1)S(1)} %get-tuple-element.41), channel_id=1, source_target_pairs={{0,6},{1,7},{2,0},{3,1},{4,2},{5,3},{6,4},{7,5},{8,14},{9,15},{10,... | collective-permute-start | bytes 786440 | tf_op jit(solution)/shard_map/ppermute | solution.py:357
  93.3 8.0 %shard_map.18.near_hbm = bf16[3,2,4,768,128]{4,3,2,1,0:T(8,128)(2,1)} custom-call(s32[4]{0:T(128)S(1)} %pad_add_fusion.meta_ref, bf16[512,1536]{1,0:T(8,128)(2,1)S(1)} %pad_maximum_fusion.refs_0_, bf16[512,1536]{1,0:T(8,128)(2,1)} %collective-permute-done.8.refs_1_, bf16[512,1536]{1,0:T(8,128)(2,1)S(1)} %collective-permute-done.9.refs_2_, ...), custom_call_target="tpu_custom_call" | custom-call | flops 150994944 | bytes 9437200 | tf_op jit(solution)/shard_map/pallas_call | solution.py:66
  103.6 2.7 %collective-permute-start.19 = (bf16[128,1024]{1,0:T(8,128)(2,1)S(1)}, bf16[128,1024]{1,0:T(8,128)(2,1)S(1)}, u32[]{:S(2)}, u32[]{:S(2)}) collective-permute-start(bf16[128,1024]{1,0:T(8,128)(2,1)S(1)} %fusion.5), channel_id=1, source_target_pairs={{0,8},{1,17},{2,10},{3,19},{4,12},{5,21},{6,14},{7,23},{8,0},{9,25... | collective-permute-start | bytes 786440 | tf_op jit(solution)/shard_map/ppermute | solution.py:369
  114.9 3.6 %collective-permute-start.17 = (bf16[128,512]{1,0:T(8,128)(2,1)S(1)}, bf16[128,512]{1,0:T(8,128)(2,1)S(1)}, u32[]{:S(2)}, u32[]{:S(2)}) collective-permute-start(bf16[128,512]{1,0:T(8,128)(2,1)S(1)} %get-tuple-element.45), channel_id=1, source_target_pairs={{0,6},{1,7},{2,0},{3,1},{4,2},{5,3},{6,4},{7,5},{8,14},{9,15},{10,... | collective-permute-start | bytes 393224 | tf_op jit(solution)/shard_map/ppermute | solution.py:357
  121.4 3.4 %collective-permute-done.17 = bf16[128,512]{1,0:T(8,128)(2,1)S(1)} collective-permute-done((bf16[128,512]{1,0:T(8,128)(2,1)S(1)}, bf16[128,512]{1,0:T(8,128)(2,1)S(1)}, u32[]{:S(2)}, u32[]{:S(2)}) %collective-permute-start.17) | collective-permute-done | bytes 131104 | tf_op jit(solution)/shard_map/ppermute | solution.py:357
  127.3 4.0 %collective-permute-done.21 = bf16[128,512]{1,0:T(8,128)(2,1)S(1)} collective-permute-done((bf16[128,512]{1,0:T(8,128)(2,1)S(1)}, bf16[128,512]{1,0:T(8,128)(2,1)S(1)}, u32[]{:S(2)}, u32[]{:S(2)}) %collective-permute-start.21) | collective-permute-done | bytes 131104 | tf_op jit(solution)/shard_map/ppermute | solution.py:357
  138.9 3.0 %collective-permute-done.25 = bf16[128,1536]{1,0:T(8,128)(2,1)S(1)} collective-permute-done((bf16[128,1536]{1,0:T(8,128)(2,1)S(1)}, bf16[128,1536]{1,0:T(8,128)(2,1)S(1)}, u32[]{:S(2)}, u32[]{:S(2)}) %collective-permute-start.25) | collective-permute-done | bytes 393248 | tf_op jit(solution)/shard_map/ppermute | solution.py:357
  141.9 3.8 %collective-permute-done.24 = bf16[128,1536]{1,0:T(8,128)(2,1)S(1)} collective-permute-done((bf16[128,1536]{1,0:T(8,128)(2,1)S(1)}, bf16[128,1536]{1,0:T(8,128)(2,1)S(1)}, u32[]{:S(2)}, u32[]{:S(2)}) %collective-permute-start.24) | collective-permute-done | bytes 393248 | tf_op jit(solution)/shard_map/ppermute | solution.py:369
  151.1 3.1 %collective-permute-done.26 = bf16[128,1536]{1,0:T(8,128)(2,1)S(1)} collective-permute-done((bf16[128,1536]{1,0:T(8,128)(2,1)S(1)}, bf16[128,1536]{1,0:T(8,128)(2,1)S(1)}, u32[]{:S(2)}, u32[]{:S(2)}) %collective-permute-start.26) | collective-permute-done | bytes 393248 | tf_op jit(solution)/shard_map/ppermute | solution.py:369
  154.4 9.1 %collective-permute-done.33.refs_16_ = bf16[128,2560]{1,0:T(8,128)(2,1)S(1)} collective-permute-done((bf16[128,2560]{1,0:T(8,128)(2,1)S(1)}, bf16[128,2560]{1,0:T(8,128)(2,1)S(1)}, u32[]{:S(2)}, u32[]{:S(2)}) %collective-permute-start.33) | collective-permute-done | bytes 655392 | tf_op jit(solution)/shard_map/ppermute | solution.py:357
  163.5 4.1 %collective-permute-done.32.refs_10_ = bf16[128,2560]{1,0:T(8,128)(2,1)S(1)} collective-permute-done((bf16[128,2560]{1,0:T(8,128)(2,1)S(1)}, bf16[128,2560]{1,0:T(8,128)(2,1)S(1)}, u32[]{:S(2)}, u32[]{:S(2)}) %collective-permute-start.32) | collective-permute-done | bytes 655392 | tf_op jit(solution)/shard_map/ppermute | solution.py:369
  173.0 11.4 %collective-permute-done.34.refs_11_ = bf16[128,2560]{1,0:T(8,128)(2,1)S(1)} collective-permute-done((bf16[128,2560]{1,0:T(8,128)(2,1)S(1)}, bf16[128,2560]{1,0:T(8,128)(2,1)S(1)}, u32[]{:S(2)}, u32[]{:S(2)}) %collective-permute-start.34) | collective-permute-done | bytes 655392 | tf_op jit(solution)/shard_map/ppermute | solution.py:369
  184.9 7.3 %collective-permute-done.40.refs_18_ = bf16[128,2560]{1,0:T(8,128)(2,1)S(1)} collective-permute-done((bf16[128,2560]{1,0:T(8,128)(2,1)S(1)}, bf16[128,2560]{1,0:T(8,128)(2,1)S(1)}, u32[]{:S(2)}, u32[]{:S(2)}) %collective-permute-start.40) | collective-permute-done | bytes 655392 | tf_op jit(solution)/shard_map/ppermute | solution.py:369
  196.8 22.8 %shard_map.22.acc_hbm = f32[4,2,4,768,128]{4,3,2,1,0:T(8,128)} custom-call(s32[4]{0:T(128)S(1)} %pad_add_fusion.meta_ref, bf16[3,2,4,768,128]{4,3,2,1,0:T(8,128)(2,1)} %shard_map.18.near_hbm, bf16[1,2,4,768,128]{4,3,2,1,0:T(8,128)(2,1)} %copy-done, bf16[128,2560]{1,0:T(8,128)(2,1)S(1)} %pad_maximum_fusion.1.refs_0_, ...), custom_call_target="tpu_custom_call" | custom-call | flops 12884901888 | bytes 16777232 | tf_op jit(solution)/shard_map/pallas_call | solution.py:66
  222.0 8.5 %collective-permute-done.49.refs_27_ = bf16[128,2560]{1,0:T(8,128)(2,1)S(1)} collective-permute-done((bf16[128,2560]{1,0:T(8,128)(2,1)S(1)}, bf16[128,2560]{1,0:T(8,128)(2,1)S(1)}, u32[]{:S(2)}, u32[]{:S(2)}) %collective-permute-start.49) | collective-permute-done | bytes 655392 | tf_op jit(solution)/shard_map/ppermute | solution.py:369
  233.5 32.5 %shard_map.23 = bf16[4,2,128,768]{3,2,1,0:T(8,128)(2,1)} custom-call(s32[4]{0:T(128)S(1)} %pad_add_fusion.meta_ref, bf16[3,2,4,768,128]{4,3,2,1,0:T(8,128)(2,1)} %shard_map.18.near_hbm, bf16[1,2,4,768,128]{4,3,2,1,0:T(8,128)(2,1)} %copy-done, f32[4,2,4,768,128]{4,3,2,1,0:T(8,128)} %shard_map.22.acc_hbm, bf16[128,2560]{1,0:T(8,128)(2,1)S(1)} %pad_maximum_fusion.1.refs_0_, ...), custom_call_target="tpu_custom_call" | custom-call | flops 19327352832 | bytes 39845904 | tf_op jit(solution)/shard_map/pallas_call | solution.py:66
  (162 shorter events, 66.0 us)
Async XLA Ops:
  1.5 14.6 %collective-permute-start = (bf16[128,1536]{1,0:T(8,128)(2,1)S(1)}, bf16[128,1536]{1,0:T(8,128)(2,1)S(1)}, u32[]{:S(2)}, u32[]{:S(2)}) collective-permute-start(bf16[128,1536]{1,0:T(8,128)(2,1)S(1)} %get-tuple-element.36), channel_id=1, source_target_pairs={{0,6},{1,7},{2,0},{3,1},{4,2},{5,3},{6,4},{7,5},{8,14},{9,15},{10,... | collective-permute-start | bytes 1179656 | tf_op jit(solution)/shard_map/ppermute | solution.py:357
  6.6 19.0 %collective-permute-start.2 = (bf16[128,1536]{1,0:T(8,128)(2,1)S(1)}, bf16[128,1536]{1,0:T(8,128)(2,1)S(1)}, u32[]{:S(2)}, u32[]{:S(2)}) collective-permute-start(bf16[128,1536]{1,0:T(8,128)(2,1)S(1)} %get-tuple-element.37), channel_id=1, source_target_pairs={{0,2},{1,3},{2,4},{3,5},{4,6},{5,7},{6,0},{7,1},{8,10},{9,11},{10,... | collective-permute-start | bytes 1179656 | tf_op jit(solution)/shard_map/ppermute | solution.py:357
  6.6 33.5 %collective-permute-start.1 = (bf16[128,1536]{1,0:T(8,128)(2,1)S(1)}, bf16[128,1536]{1,0:T(8,128)(2,1)S(1)}, u32[]{:S(2)}, u32[]{:S(2)}) collective-permute-start(bf16[128,1536]{1,0:T(8,128)(2,1)S(1)} %get-tuple-element.38), channel_id=1, source_target_pairs={{0,4},{1,5},{2,6},{3,7},{4,0},{5,1},{6,2},{7,3},{8,12},{9,13},{10,... | collective-permute-start | bytes 1179656 | tf_op jit(solution)/shard_map/ppermute | solution.py:357
  40.3 36.7 %collective-permute-start.9 = (bf16[512,1536]{1,0:T(8,128)(2,1)S(1)}, bf16[512,1536]{1,0:T(8,128)(2,1)S(1)}, u32[]{:S(2)}, u32[]{:S(2)}) collective-permute-start(bf16[512,1536]{1,0:T(8,128)(2,1)S(1)} %pad_maximum_fusion.refs_0_), channel_id=1, source_target_pairs={{0,16},{1,9},{2,18},{3,11},{4,20},{5,13},{6,22},{7,15},{8,24},{9,1... | collective-permute-start | bytes 4718600 | tf_op jit(solution)/shard_map/ppermute | solution.py:369
  41.9 35.3 %collective-permute-start.8 = (bf16[512,1536]{1,0:T(8,128)(2,1)S(1)}, bf16[512,1536]{1,0:T(8,128)(2,1)}, u32[]{:S(2)}, u32[]{:S(2)}) collective-permute-start(bf16[512,1536]{1,0:T(8,128)(2,1)S(1)} %pad_maximum_fusion.refs_0_), channel_id=1, source_target_pairs={{0,8},{1,17},{2,10},{3,19},{4,12},{5,21},{6,14},{7,23},{8,0},{9,25... | collective-permute-start | bytes 4718600 | tf_op jit(solution)/shard_map/ppermute | solution.py:369
  49.7 15.8 %collective-permute-start.4 = (bf16[128,1024]{1,0:T(8,128)(2,1)}, bf16[128,1024]{1,0:T(8,128)(2,1)S(1)}, u32[]{:S(2)}, u32[]{:S(2)}) collective-permute-start(bf16[128,1024]{1,0:T(8,128)(2,1)} %get-tuple-element.42), channel_id=1, source_target_pairs={{0,6},{1,7},{2,0},{3,1},{4,2},{5,3},{6,4},{7,5},{8,14},{9,15},{10,... | collective-permute-start | bytes 786440 | tf_op jit(solution)/shard_map/ppermute | solution.py:357
  52.4 22.2 %collective-permute-start.5 = (bf16[128,1024]{1,0:T(8,128)(2,1)}, bf16[128,1024]{1,0:T(8,128)(2,1)}, u32[]{:S(2)}, u32[]{:S(2)}) collective-permute-start(bf16[128,1024]{1,0:T(8,128)(2,1)} %get-tuple-element.44), channel_id=1, source_target_pairs={{0,4},{1,5},{2,6},{3,7},{4,0},{5,1},{6,2},{7,3},{8,12},{9,13},{10,... | collective-permute-start | bytes 786440 | tf_op jit(solution)/shard_map/ppermute | solution.py:357
  77.7 23.6 %collective-permute-start.12 = (bf16[512,1536]{1,0:T(8,128)(2,1)}, bf16[512,1536]{1,0:T(8,128)(2,1)S(1)}, u32[]{:S(2)}, u32[]{:S(2)}) collective-permute-start(bf16[512,1536]{1,0:T(8,128)(2,1)} %collective-permute-done.8.refs_1_), channel_id=1, source_target_pairs={{0,16},{1,9},{2,18},{3,11},{4,20},{5,13},{6,22},{7,15},{8,24},{9,1... | collective-permute-start | bytes 4718600 | tf_op jit(solution)/shard_map/ppermute | solution.py:369
  106.3 14.7 %collective-permute-start.16 = (bf16[128,1024]{1,0:T(8,128)(2,1)S(1)}, bf16[128,1024]{1,0:T(8,128)(2,1)S(1)}, u32[]{:S(2)}, u32[]{:S(2)}) collective-permute-start(bf16[128,1024]{1,0:T(8,128)(2,1)S(1)} %get-tuple-element.39), channel_id=1, source_target_pairs={{0,4},{1,5},{2,6},{3,7},{4,0},{5,1},{6,2},{7,3},{8,12},{9,13},{10,... | collective-permute-start | bytes 786440 | tf_op jit(solution)/shard_map/ppermute | solution.py:357
  146.2 23.1 %collective-permute-start.27 = (bf16[128,2560]{1,0:T(8,128)(2,1)S(1)}, bf16[128,2560]{1,0:T(8,128)(2,1)S(1)}, u32[]{:S(2)}, u32[]{:S(2)}) collective-permute-start(bf16[128,2560]{1,0:T(8,128)(2,1)S(1)} %pad_maximum_fusion.1.refs_0_), channel_id=1, source_target_pairs={{0,1},{1,0},{2,3},{3,2},{4,5},{5,4},{6,7},{7,6},{8,9},{9,8},{10,11... | collective-permute-start | bytes 1966088 | tf_op jit(solution)/shard_map/ppermute | solution.py:361
  146.3 17.2 %collective-permute-start.33 = (bf16[128,2560]{1,0:T(8,128)(2,1)S(1)}, bf16[128,2560]{1,0:T(8,128)(2,1)S(1)}, u32[]{:S(2)}, u32[]{:S(2)}) collective-permute-start(bf16[128,2560]{1,0:T(8,128)(2,1)S(1)} %constant_dynamic-update-slice_fusion.6.refs_8_), channel_id=1, source_target_pairs={{0,6},{1,7},{2,0},{3,1},{4,2},{5,3},{6,4},{7,5},{8,14},{9,15},{10,... | collective-permute-start | bytes 1966088 | tf_op jit(solution)/shard_map/ppermute | solution.py:357
  148.1 19.4 %collective-permute-start.32 = (bf16[128,2560]{1,0:T(8,128)(2,1)S(1)}, bf16[128,2560]{1,0:T(8,128)(2,1)S(1)}, u32[]{:S(2)}, u32[]{:S(2)}) collective-permute-start(bf16[128,2560]{1,0:T(8,128)(2,1)S(1)} %constant_dynamic-update-slice_fusion.6.refs_8_), channel_id=1, source_target_pairs={{0,16},{1,9},{2,18},{3,11},{4,20},{5,13},{6,22},{7,15},{8,24},{9,1... | collective-permute-start | bytes 1966088 | tf_op jit(solution)/shard_map/ppermute | solution.py:369
  148.8 18.7 %collective-permute-start.31 = (bf16[128,2560]{1,0:T(8,128)(2,1)S(1)}, bf16[128,2560]{1,0:T(8,128)(2,1)S(1)}, u32[]{:S(2)}, u32[]{:S(2)}) collective-permute-start(bf16[128,2560]{1,0:T(8,128)(2,1)S(1)} %constant_dynamic-update-slice_fusion.6.refs_8_), channel_id=1, source_target_pairs={{0,8},{1,17},{2,10},{3,19},{4,12},{5,21},{6,14},{7,23},{8,0},{9,25... | collective-permute-start | bytes 1966088 | tf_op jit(solution)/shard_map/ppermute | solution.py:369
  154.2 15.9 %collective-permute-start.35 = (bf16[128,2560]{1,0:T(8,128)(2,1)S(1)}, bf16[128,2560]{1,0:T(8,128)(2,1)S(1)}, u32[]{:S(2)}, u32[]{:S(2)}) collective-permute-start(bf16[128,2560]{1,0:T(8,128)(2,1)S(1)} %constant_dynamic-update-slice_fusion.6.refs_8_), channel_id=1, source_target_pairs={{0,1},{1,0},{2,3},{3,2},{4,5},{5,4},{6,7},{7,6},{8,9},{9,8},{10,11... | collective-permute-start | bytes 1966088 | tf_op jit(solution)/shard_map/ppermute | solution.py:361
  167.5 16.9 %collective-permute-start.34 = (bf16[128,2560]{1,0:T(8,128)(2,1)S(1)}, bf16[128,2560]{1,0:T(8,128)(2,1)S(1)}, u32[]{:S(2)}, u32[]{:S(2)}) collective-permute-start(bf16[128,2560]{1,0:T(8,128)(2,1)S(1)} %collective-permute-done.31.refs_9_), channel_id=1, source_target_pairs={{0,16},{1,9},{2,18},{3,11},{4,20},{5,13},{6,22},{7,15},{8,24},{9,1... | collective-permute-start | bytes 1966088 | tf_op jit(solution)/shard_map/ppermute | solution.py:369
  168.0 16.4 %collective-permute-start.41 = (bf16[128,2560]{1,0:T(8,128)(2,1)S(1)}, bf16[128,2560]{1,0:T(8,128)(2,1)S(1)}, u32[]{:S(2)}, u32[]{:S(2)}) collective-permute-start(bf16[128,2560]{1,0:T(8,128)(2,1)S(1)} %collective-permute-done.33.refs_16_), channel_id=1, source_target_pairs={{0,6},{1,7},{2,0},{3,1},{4,2},{5,3},{6,4},{7,5},{8,14},{9,15},{10,... | collective-permute-start | bytes 1966088 | tf_op jit(solution)/shard_map/ppermute | solution.py:357
  169.3 22.9 %collective-permute-start.40 = (bf16[128,2560]{1,0:T(8,128)(2,1)S(1)}, bf16[128,2560]{1,0:T(8,128)(2,1)S(1)}, u32[]{:S(2)}, u32[]{:S(2)}) collective-permute-start(bf16[128,2560]{1,0:T(8,128)(2,1)S(1)} %collective-permute-done.33.refs_16_), channel_id=1, source_target_pairs={{0,16},{1,9},{2,18},{3,11},{4,20},{5,13},{6,22},{7,15},{8,24},{9,1... | collective-permute-start | bytes 1966088 | tf_op jit(solution)/shard_map/ppermute | solution.py:369
  170.1 22.1 %collective-permute-start.39 = (bf16[128,2560]{1,0:T(8,128)(2,1)S(1)}, bf16[128,2560]{1,0:T(8,128)(2,1)S(1)}, u32[]{:S(2)}, u32[]{:S(2)}) collective-permute-start(bf16[128,2560]{1,0:T(8,128)(2,1)S(1)} %collective-permute-done.33.refs_16_), channel_id=1, source_target_pairs={{0,8},{1,17},{2,10},{3,19},{4,12},{5,21},{6,14},{7,23},{8,0},{9,25... | collective-permute-start | bytes 1966088 | tf_op jit(solution)/shard_map/ppermute | solution.py:369
  172.9 19.8 %collective-permute-start.29 = (bf16[128,2560]{1,0:T(8,128)(2,1)S(1)}, bf16[128,2560]{1,0:T(8,128)(2,1)S(1)}, u32[]{:S(2)}, u32[]{:S(2)}) collective-permute-start(bf16[128,2560]{1,0:T(8,128)(2,1)S(1)} %constant_dynamic-update-slice_fusion.2.refs_2_), channel_id=1, source_target_pairs={{0,1},{1,0},{2,3},{3,2},{4,5},{5,4},{6,7},{7,6},{8,9},{9,8},{10,11... | collective-permute-start | bytes 1966088 | tf_op jit(solution)/shard_map/ppermute | solution.py:361
  192.8 28.2 %collective-permute-start.43 = (bf16[128,2560]{1,0:T(8,128)(2,1)S(1)}, bf16[128,2560]{1,0:T(8,128)(2,1)S(1)}, u32[]{:S(2)}, u32[]{:S(2)}) collective-permute-start(bf16[128,2560]{1,0:T(8,128)(2,1)S(1)} %collective-permute-done.33.refs_16_), channel_id=1, source_target_pairs={{0,1},{1,0},{2,3},{3,2},{4,5},{5,4},{6,7},{7,6},{8,9},{9,8},{10,11... | collective-permute-start | bytes 1966088 | tf_op jit(solution)/shard_map/ppermute | solution.py:361
  192.8 26.9 %collective-permute-start.48 = (bf16[128,2560]{1,0:T(8,128)(2,1)S(1)}, bf16[128,2560]{1,0:T(8,128)(2,1)S(1)}, u32[]{:S(2)}, u32[]{:S(2)}) collective-permute-start(bf16[128,2560]{1,0:T(8,128)(2,1)S(1)} %collective-permute-done.41.refs_24_), channel_id=1, source_target_pairs={{0,16},{1,9},{2,18},{3,11},{4,20},{5,13},{6,22},{7,15},{8,24},{9,1... | collective-permute-start | bytes 1966088 | tf_op jit(solution)/shard_map/ppermute | solution.py:369
  193.3 26.5 %collective-permute-start.47 = (bf16[128,2560]{1,0:T(8,128)(2,1)S(1)}, bf16[128,2560]{1,0:T(8,128)(2,1)S(1)}, u32[]{:S(2)}, u32[]{:S(2)}) collective-permute-start(bf16[128,2560]{1,0:T(8,128)(2,1)S(1)} %collective-permute-done.41.refs_24_), channel_id=1, source_target_pairs={{0,8},{1,17},{2,10},{3,19},{4,12},{5,21},{6,14},{7,23},{8,0},{9,25... | collective-permute-start | bytes 1966088 | tf_op jit(solution)/shard_map/ppermute | solution.py:369
  195.0 24.6 %collective-permute-start.42 = (bf16[128,2560]{1,0:T(8,128)(2,1)S(1)}, bf16[128,2560]{1,0:T(8,128)(2,1)S(1)}, u32[]{:S(2)}, u32[]{:S(2)}) collective-permute-start(bf16[128,2560]{1,0:T(8,128)(2,1)S(1)} %collective-permute-done.39.refs_17_), channel_id=1, source_target_pairs={{0,16},{1,9},{2,18},{3,11},{4,20},{5,13},{6,22},{7,15},{8,24},{9,1... | collective-permute-start | bytes 1966088 | tf_op jit(solution)/shard_map/ppermute | solution.py:369
  196.0 25.5 %collective-permute-start.50 = (bf16[128,2560]{1,0:T(8,128)(2,1)S(1)}, bf16[128,2560]{1,0:T(8,128)(2,1)}, u32[]{:S(2)}, u32[]{:S(2)}) collective-permute-start(bf16[128,2560]{1,0:T(8,128)(2,1)S(1)} %collective-permute-done.41.refs_24_), channel_id=1, source_target_pairs={{0,1},{1,0},{2,3},{3,2},{4,5},{5,4},{6,7},{7,6},{8,9},{9,8},{10,11... | collective-permute-start | bytes 1966088 | tf_op jit(solution)/shard_map/ppermute | solution.py:361
  (56 other events, 599.6 us)

commit v4 on v3

--- a/solution.py
+++ b/solution.py
@@ -432,7 +432,7 @@
     far_columns = columns((3,), three, pair_three)
     side_shard = summed(side_blocks, side_sent)
     own_three = across(own_one, 1)
-    corner_sent = [after(chunk, own_two, own_three) for chunk in sent(corner_blocks)]
+    corner_sent = [after(chunk, own_two, own_three, far_columns) for chunk in sent(corner_blocks)]
     corner_shard = summed(corner_blocks, corner_sent)
     cross_shard = jnp.concatenate([side_shard, corner_shard], axis=1)
 
@@ -444,7 +444,7 @@
 
     cross_ring = along(cross_shard, 1)
     cross_one, cross_two = across(cross_shard, 0), across(cross_shard, 1)
-    held_back = [cross_ring, cross_one, cross_two, far_columns]
+    held_back = [cross_ring, cross_one, cross_two]
     near = [wide(own_shard, cross_shard), wide(own_ring, after(cross_ring, *held_back))]
     one, two = [wide(own_one, cross_one)], [wide(own_two, cross_two)]
     three, ring = [], [near[1]]
@@ -470,20 +470,25 @@
             out_space=pl.ANY,
         )
 
+    late = line - 2 if line > 3 else line
     for step in range(1, line + 1):
         done = held_back if step == 1 else [b[-1] for b in (ring, one, two, three)]
         if step == line:
             acc = early()
-            done = done + [acc]
+            done = done + [two[-2], acc]
         if step == 1:
             cross_three = across(after(cross_one, *done), 1)
             three.append(wide(own_three, cross_three))
+        elif step == late + 1:
+            two.append(across(after(near[late], *done), 1))
+            three.append(along(after(three[-1], *done), 1))
         else:
             three.append(across(after(one[-1], *done), 1))
         if step < line:
             here = after(near[step], *done)
             one.append(across(here, 0))
-            two.append(across(here, 1))
+            if step != late:
+                two.append(across(here, 1))
         if step < line - 1:
             ring.append(along(here, 1))
             near.append(ring[-1])

time: 266 us -> 262 us (0.985)
  waiting for transfers between devices: 125 us -> 122 us
    ppermute x16 -> x17, waiting for transfers between devices: 81.1 us -> 71.8 us  [along(): return lax.ppermute(values, 'col', pairs)]
    ppermute x18 -> x17, waiting for transfers between devices: 39.9 us -> 45.5 us  [across(): return lax.ppermute(values, ('row', 'col'), pairs)]
    ppermute x18 -> x17, starting transfers between devices: 26 us -> 24.6 us  [across(): return lax.ppermute(values, ('row', 'col'), pairs)]
    ppermute x16 -> x17, starting transfers between devices: 27.6 us -> 27.1 us  [along(): return lax.ppermute(values, 'col', pairs)]
  transfers between devices with their start and end apart: 54 -> 54, of which waited for: 25 -> 24; matrix products, arithmetic and copies ran while one was open for 1% -> 1% of each run, Pallas kernels for 16% -> 17%
where the time goes in v4:
time: 262 us
  waiting for transfers between devices  122 us (47%)
  Pallas kernels  76 us (29%)
  starting transfers between devices  55.5 us (21%)
  local copies, waits for them, and re-layouts  5.93 us (2%)
    pallas_call x7, Pallas kernels, call(): pl.pallas_call(kernel, in_specs=specs, out_specs=pl.BlockSpec(memory_spac...  76 us
    ppermute x17, waiting for transfers between devices, along(): return lax.ppermute(values, 'col', pairs)  71.8 us
    ppermute x17, waiting for transfers between devices, across(): return lax.ppermute(values, ('row', 'col'), pairs)  45.5 us
    ppermute x17, starting transfers between devices, along(): return lax.ppermute(values, 'col', pairs)  27.1 us
    ppermute x17, starting transfers between devices, across(): return lax.ppermute(values, ('row', 'col'), pairs)  24.6 us
  transfers between devices with their start and end apart: 54, of which 24 were waited for; matrix products, arithmetic and copies ran while one was open for 1% of the time, Pallas kernels for 17%

profile of v4, /device:TPU:0, one launch (start us, length us, event | category | flops | bytes accessed | tf_op | source)
XLA Modules:
  0.0 261.9 jit_solution(10303643961626014536)
XLA Ops:
  1.5 5.1 %collective-permute-start = (bf16[128,1536]{1,0:T(8,128)(2,1)S(1)}, bf16[128,1536]{1,0:T(8,128)(2,1)S(1)}, u32[]{:S(2)}, u32[]{:S(2)}) collective-permute-start(bf16[128,1536]{1,0:T(8,128)(2,1)S(1)} %get-tuple-element.38), channel_id=1, source_target_pairs={{0,6},{1,7},{2,0},{3,1},{4,2},{5,3},{6,4},{7,5},{8,14},{9,15},{10,... | collective-permute-start | bytes 1179656 | tf_op jit(solution)/shard_map/ppermute | solution.py:357
  7.6 8.5 %collective-permute-done = bf16[128,1536]{1,0:T(8,128)(2,1)S(1)} collective-permute-done((bf16[128,1536]{1,0:T(8,128)(2,1)S(1)}, bf16[128,1536]{1,0:T(8,128)(2,1)S(1)}, u32[]{:S(2)}, u32[]{:S(2)}) %collective-permute-start) | collective-permute-done | bytes 393248 | tf_op jit(solution)/shard_map/ppermute | solution.py:357
  16.1 9.4 %collective-permute-done.2 = bf16[128,1536]{1,0:T(8,128)(2,1)S(1)} collective-permute-done((bf16[128,1536]{1,0:T(8,128)(2,1)S(1)}, bf16[128,1536]{1,0:T(8,128)(2,1)S(1)}, u32[]{:S(2)}, u32[]{:S(2)}) %collective-permute-start.2) | collective-permute-done | bytes 393248 | tf_op jit(solution)/shard_map/ppermute | solution.py:357
  25.5 14.6 %collective-permute-done.1 = bf16[128,1536]{1,0:T(8,128)(2,1)S(1)} collective-permute-done((bf16[128,1536]{1,0:T(8,128)(2,1)S(1)}, bf16[128,1536]{1,0:T(8,128)(2,1)S(1)}, u32[]{:S(2)}, u32[]{:S(2)}) %collective-permute-start.1) | collective-permute-done | bytes 393248 | tf_op jit(solution)/shard_map/ppermute | solution.py:357
  43.8 4.0 %shard_map.17 = bf16[4,128,1024]{2,1,0:T(8,128)(2,1)S(1)} custom-call(s32[4]{0:T(128)S(1)} %pad_add_fusion.meta_ref, bf16[512,1536]{1,0:T(8,128)(2,1)S(1)} %pad_maximum_fusion.refs_0_, bf16[512,1536]{1,0:T(8,128)(2,1)} %collective-permute-done.3.refs_1_.refs_3_), custom_call_target="tpu_custom_call" | custom-call | flops 1610612736 | bytes 3145744 | tf_op jit(solution)/shard_map/pallas_call | solution.py:66
  49.7 2.6 %collective-permute-start.4 = (bf16[128,1024]{1,0:T(8,128)(2,1)}, bf16[128,1024]{1,0:T(8,128)(2,1)S(1)}, u32[]{:S(2)}, u32[]{:S(2)}) collective-permute-start(bf16[128,1024]{1,0:T(8,128)(2,1)} %get-tuple-element.44), channel_id=1, source_target_pairs={{0,6},{1,7},{2,0},{3,1},{4,2},{5,3},{6,4},{7,5},{8,14},{9,15},{10,... | collective-permute-start | bytes 786440 | tf_op jit(solution)/shard_map/ppermute | solution.py:357
  53.0 12.6 %collective-permute-done.4 = bf16[128,1024]{1,0:T(8,128)(2,1)S(1)} collective-permute-done((bf16[128,1024]{1,0:T(8,128)(2,1)}, bf16[128,1024]{1,0:T(8,128)(2,1)S(1)}, u32[]{:S(2)}, u32[]{:S(2)}) %collective-permute-start.4) | collective-permute-done | bytes 262176 | tf_op jit(solution)/shard_map/ppermute | solution.py:357
  65.5 9.0 %collective-permute-done.5 = bf16[128,1024]{1,0:T(8,128)(2,1)} collective-permute-done((bf16[128,1024]{1,0:T(8,128)(2,1)}, bf16[128,1024]{1,0:T(8,128)(2,1)}, u32[]{:S(2)}, u32[]{:S(2)}) %collective-permute-start.5) | collective-permute-done | bytes 262176 | tf_op jit(solution)/shard_map/ppermute | solution.py:357
  79.2 2.6 %collective-permute-start.7 = (bf16[128,1024]{1,0:T(8,128)(2,1)S(1)}, bf16[128,1024]{1,0:T(8,128)(2,1)S(1)}, u32[]{:S(2)}, u32[]{:S(2)}) collective-permute-start(bf16[128,1024]{1,0:T(8,128)(2,1)S(1)} %fusion.5), channel_id=1, source_target_pairs={{0,6},{1,7},{2,0},{3,1},{4,2},{5,3},{6,4},{7,5},{8,14},{9,15},{10,... | collective-permute-start | bytes 786440 | tf_op jit(solution)/shard_map/ppermute | solution.py:357
  84.2 5.1 %shard_map.19 = bf16[4,128,1024]{2,1,0:T(8,128)(2,1)S(1)} custom-call(s32[4]{0:T(128)S(1)} %pad_add_fusion.meta_ref, bf16[512,1536]{1,0:T(8,128)(2,1)S(1)} %pad_maximum_fusion.refs_0_, bf16[512,1536]{1,0:T(8,128)(2,1)} %collective-permute-done.8.refs_1_, bf16[512,1536]{1,0:T(8,128)(2,1)S(1)} %collective-permute-done.9.refs_2_, bf16[512,1536]{1,0:T(8,128)(2,1)} %copy-done.2, ...), custom_call_target="tpu_custom_call" | custom-call | flops 1610612736 | bytes 7864336 | tf_op jit(solution)/shard_map/pallas_call | solution.py:66
  89.5 3.8 %collective-permute-start.13 = (bf16[128,1024]{1,0:T(8,128)(2,1)S(1)}, bf16[128,1024]{1,0:T(8,128)(2,1)S(1)}, u32[]{:S(2)}, u32[]{:S(2)}) collective-permute-start(bf16[128,1024]{1,0:T(8,128)(2,1)S(1)} %get-tuple-element.43), channel_id=1, source_target_pairs={{0,6},{1,7},{2,0},{3,1},{4,2},{5,3},{6,4},{7,5},{8,14},{9,15},{10,... | collective-permute-start | bytes 786440 | tf_op jit(solution)/shard_map/ppermute | solution.py:357
  93.3 8.0 %shard_map.18.near_hbm = bf16[3,2,4,768,128]{4,3,2,1,0:T(8,128)(2,1)} custom-call(s32[4]{0:T(128)S(1)} %pad_add_fusion.meta_ref, bf16[512,1536]{1,0:T(8,128)(2,1)S(1)} %pad_maximum_fusion.refs_0_, bf16[512,1536]{1,0:T(8,128)(2,1)} %collective-permute-done.8.refs_1_, bf16[512,1536]{1,0:T(8,128)(2,1)S(1)} %collective-permute-done.9.refs_2_, ...), custom_call_target="tpu_custom_call" | custom-call | flops 150994944 | bytes 9437200 | tf_op jit(solution)/shard_map/pallas_call | solution.py:66
  103.6 2.7 %collective-permute-start.19 = (bf16[128,1024]{1,0:T(8,128)(2,1)S(1)}, bf16[128,1024]{1,0:T(8,128)(2,1)S(1)}, u32[]{:S(2)}, u32[]{:S(2)}) collective-permute-start(bf16[128,1024]{1,0:T(8,128)(2,1)S(1)} %fusion.5), channel_id=1, source_target_pairs={{0,8},{1,17},{2,10},{3,19},{4,12},{5,21},{6,14},{7,23},{8,0},{9,25... | collective-permute-start | bytes 786440 | tf_op jit(solution)/shard_map/ppermute | solution.py:369
  114.9 3.5 %collective-permute-start.17 = (bf16[128,512]{1,0:T(8,128)(2,1)S(1)}, bf16[128,512]{1,0:T(8,128)(2,1)S(1)}, u32[]{:S(2)}, u32[]{:S(2)}) collective-permute-start(bf16[128,512]{1,0:T(8,128)(2,1)S(1)} %get-tuple-element.47), channel_id=1, source_target_pairs={{0,6},{1,7},{2,0},{3,1},{4,2},{5,3},{6,4},{7,5},{8,14},{9,15},{10,... | collective-permute-start | bytes 393224 | tf_op jit(solution)/shard_map/ppermute | solution.py:357
  127.3 4.0 %collective-permute-done.21 = bf16[128,512]{1,0:T(8,128)(2,1)S(1)} collective-permute-done((bf16[128,512]{1,0:T(8,128)(2,1)S(1)}, bf16[128,512]{1,0:T(8,128)(2,1)S(1)}, u32[]{:S(2)}, u32[]{:S(2)}) %collective-permute-start.21) | collective-permute-done | bytes 131104 | tf_op jit(solution)/shard_map/ppermute | solution.py:357
  131.4 2.7 %collective-permute-start.25 = (bf16[128,1536]{1,0:T(8,128)(2,1)S(1)}, bf16[128,1536]{1,0:T(8,128)(2,1)S(1)}, u32[]{:S(2)}, u32[]{:S(2)}) collective-permute-start(bf16[128,1536]{1,0:T(8,128)(2,1)S(1)} %pad_maximum_fusion.2), channel_id=1, source_target_pairs={{0,6},{1,7},{2,0},{3,1},{4,2},{5,3},{6,4},{7,5},{8,14},{9,15},{10,... | collective-permute-start | bytes 1179656 | tf_op jit(solution)/shard_map/ppermute | solution.py:357
  134.7 2.6 collective-permute-start.23
  137.5 4.4 %collective-permute-done.25 = bf16[128,1536]{1,0:T(8,128)(2,1)S(1)} collective-permute-done((bf16[128,1536]{1,0:T(8,128)(2,1)S(1)}, bf16[128,1536]{1,0:T(8,128)(2,1)S(1)}, u32[]{:S(2)}, u32[]{:S(2)}) %collective-permute-start.25) | collective-permute-done | bytes 393248 | tf_op jit(solution)/shard_map/ppermute | solution.py:357
  141.9 3.8 %collective-permute-done.24 = bf16[128,1536]{1,0:T(8,128)(2,1)S(1)} collective-permute-done((bf16[128,1536]{1,0:T(8,128)(2,1)S(1)}, bf16[128,1536]{1,0:T(8,128)(2,1)S(1)}, u32[]{:S(2)}, u32[]{:S(2)}) %collective-permute-start.24) | collective-permute-done | bytes 393248 | tf_op jit(solution)/shard_map/ppermute | solution.py:369
  151.1 17.0 %collective-permute-done.26 = bf16[128,1536]{1,0:T(8,128)(2,1)S(1)} collective-permute-done((bf16[128,1536]{1,0:T(8,128)(2,1)S(1)}, bf16[128,1536]{1,0:T(8,128)(2,1)S(1)}, u32[]{:S(2)}, u32[]{:S(2)}) %collective-permute-start.26) | collective-permute-done | bytes 393248 | tf_op jit(solution)/shard_map/ppermute | solution.py:369
  171.4 14.7 %collective-permute-done.34.refs_11_ = bf16[128,2560]{1,0:T(8,128)(2,1)S(1)} collective-permute-done((bf16[128,2560]{1,0:T(8,128)(2,1)S(1)}, bf16[128,2560]{1,0:T(8,128)(2,1)S(1)}, u32[]{:S(2)}, u32[]{:S(2)}) %collective-permute-start.34) | collective-permute-done | bytes 655392 | tf_op jit(solution)/shard_map/ppermute | solution.py:369
  192.0 22.8 %shard_map.22.acc_hbm = f32[4,2,4,768,128]{4,3,2,1,0:T(8,128)} custom-call(s32[4]{0:T(128)S(1)} %pad_add_fusion.meta_ref, bf16[3,2,4,768,128]{4,3,2,1,0:T(8,128)(2,1)} %shard_map.18.near_hbm, bf16[1,2,4,768,128]{4,3,2,1,0:T(8,128)(2,1)} %copy-done, bf16[128,2560]{1,0:T(8,128)(2,1)S(1)} %pad_maximum_fusion.1.refs_0_, ...), custom_call_target="tpu_custom_call" | custom-call | flops 12884901888 | bytes 16777232 | tf_op jit(solution)/shard_map/pallas_call | solution.py:66
  218.1 8.1 %collective-permute-done.49.refs_27_ = bf16[128,2560]{1,0:T(8,128)(2,1)S(1)} collective-permute-done((bf16[128,2560]{1,0:T(8,128)(2,1)S(1)}, bf16[128,2560]{1,0:T(8,128)(2,1)S(1)}, u32[]{:S(2)}, u32[]{:S(2)}) %collective-permute-start.49) | collective-permute-done | bytes 655392 | tf_op jit(solution)/shard_map/ppermute | solution.py:369
  229.3 32.5 %shard_map.23 = bf16[4,2,128,768]{3,2,1,0:T(8,128)(2,1)} custom-call(s32[4]{0:T(128)S(1)} %pad_add_fusion.meta_ref, bf16[3,2,4,768,128]{4,3,2,1,0:T(8,128)(2,1)} %shard_map.18.near_hbm, bf16[1,2,4,768,128]{4,3,2,1,0:T(8,128)(2,1)} %copy-done, f32[4,2,4,768,128]{4,3,2,1,0:T(8,128)} %shard_map.22.acc_hbm, bf16[128,2560]{1,0:T(8,128)(2,1)S(1)} %pad_maximum_fusion.1.refs_0_, ...), custom_call_target="tpu_custom_call" | custom-call | flops 19327352832 | bytes 39845904 | tf_op jit(solution)/shard_map/pallas_call | solution.py:66
  (164 shorter events, 56.7 us)
Async XLA Ops:
  1.5 14.6 %collective-permute-start = (bf16[128,1536]{1,0:T(8,128)(2,1)S(1)}, bf16[128,1536]{1,0:T(8,128)(2,1)S(1)}, u32[]{:S(2)}, u32[]{:S(2)}) collective-permute-start(bf16[128,1536]{1,0:T(8,128)(2,1)S(1)} %get-tuple-element.38), channel_id=1, source_target_pairs={{0,6},{1,7},{2,0},{3,1},{4,2},{5,3},{6,4},{7,5},{8,14},{9,15},{10,... | collective-permute-start | bytes 1179656 | tf_op jit(solution)/shard_map/ppermute | solution.py:357
  6.6 19.0 %collective-permute-start.2 = (bf16[128,1536]{1,0:T(8,128)(2,1)S(1)}, bf16[128,1536]{1,0:T(8,128)(2,1)S(1)}, u32[]{:S(2)}, u32[]{:S(2)}) collective-permute-start(bf16[128,1536]{1,0:T(8,128)(2,1)S(1)} %get-tuple-element.39), channel_id=1, source_target_pairs={{0,2},{1,3},{2,4},{3,5},{4,6},{5,7},{6,0},{7,1},{8,10},{9,11},{10,... | collective-permute-start | bytes 1179656 | tf_op jit(solution)/shard_map/ppermute | solution.py:357
  6.6 33.5 %collective-permute-start.1 = (bf16[128,1536]{1,0:T(8,128)(2,1)S(1)}, bf16[128,1536]{1,0:T(8,128)(2,1)S(1)}, u32[]{:S(2)}, u32[]{:S(2)}) collective-permute-start(bf16[128,1536]{1,0:T(8,128)(2,1)S(1)} %get-tuple-element.40), channel_id=1, source_target_pairs={{0,4},{1,5},{2,6},{3,7},{4,0},{5,1},{6,2},{7,3},{8,12},{9,13},{10,... | collective-permute-start | bytes 1179656 | tf_op jit(solution)/shard_map/ppermute | solution.py:357
  40.3 36.7 %collective-permute-start.9 = (bf16[512,1536]{1,0:T(8,128)(2,1)S(1)}, bf16[512,1536]{1,0:T(8,128)(2,1)S(1)}, u32[]{:S(2)}, u32[]{:S(2)}) collective-permute-start(bf16[512,1536]{1,0:T(8,128)(2,1)S(1)} %pad_maximum_fusion.refs_0_), channel_id=1, source_target_pairs={{0,16},{1,9},{2,18},{3,11},{4,20},{5,13},{6,22},{7,15},{8,24},{9,1... | collective-permute-start | bytes 4718600 | tf_op jit(solution)/shard_map/ppermute | solution.py:369
  41.9 35.3 %collective-permute-start.8 = (bf16[512,1536]{1,0:T(8,128)(2,1)S(1)}, bf16[512,1536]{1,0:T(8,128)(2,1)}, u32[]{:S(2)}, u32[]{:S(2)}) collective-permute-start(bf16[512,1536]{1,0:T(8,128)(2,1)S(1)} %pad_maximum_fusion.refs_0_), channel_id=1, source_target_pairs={{0,8},{1,17},{2,10},{3,19},{4,12},{5,21},{6,14},{7,23},{8,0},{9,25... | collective-permute-start | bytes 4718600 | tf_op jit(solution)/shard_map/ppermute | solution.py:369
  49.7 15.8 %collective-permute-start.4 = (bf16[128,1024]{1,0:T(8,128)(2,1)}, bf16[128,1024]{1,0:T(8,128)(2,1)S(1)}, u32[]{:S(2)}, u32[]{:S(2)}) collective-permute-start(bf16[128,1024]{1,0:T(8,128)(2,1)} %get-tuple-element.44), channel_id=1, source_target_pairs={{0,6},{1,7},{2,0},{3,1},{4,2},{5,3},{6,4},{7,5},{8,14},{9,15},{10,... | collective-permute-start | bytes 786440 | tf_op jit(solution)/shard_map/ppermute | solution.py:357
  52.4 22.2 %collective-permute-start.5 = (bf16[128,1024]{1,0:T(8,128)(2,1)}, bf16[128,1024]{1,0:T(8,128)(2,1)}, u32[]{:S(2)}, u32[]{:S(2)}) collective-permute-start(bf16[128,1024]{1,0:T(8,128)(2,1)} %get-tuple-element.46), channel_id=1, source_target_pairs={{0,4},{1,5},{2,6},{3,7},{4,0},{5,1},{6,2},{7,3},{8,12},{9,13},{10,... | collective-permute-start | bytes 786440 | tf_op jit(solution)/shard_map/ppermute | solution.py:357
  77.7 23.6 %collective-permute-start.12 = (bf16[512,1536]{1,0:T(8,128)(2,1)}, bf16[512,1536]{1,0:T(8,128)(2,1)S(1)}, u32[]{:S(2)}, u32[]{:S(2)}) collective-permute-start(bf16[512,1536]{1,0:T(8,128)(2,1)} %collective-permute-done.8.refs_1_), channel_id=1, source_target_pairs={{0,16},{1,9},{2,18},{3,11},{4,20},{5,13},{6,22},{7,15},{8,24},{9,1... | collective-permute-start | bytes 4718600 | tf_op jit(solution)/shard_map/ppermute | solution.py:369
  106.3 14.7 %collective-permute-start.16 = (bf16[128,1024]{1,0:T(8,128)(2,1)S(1)}, bf16[128,1024]{1,0:T(8,128)(2,1)S(1)}, u32[]{:S(2)}, u32[]{:S(2)}) collective-permute-start(bf16[128,1024]{1,0:T(8,128)(2,1)S(1)} %get-tuple-element.41), channel_id=1, source_target_pairs={{0,4},{1,5},{2,6},{3,7},{4,0},{5,1},{6,2},{7,3},{8,12},{9,13},{10,... | collective-permute-start | bytes 786440 | tf_op jit(solution)/shard_map/ppermute | solution.py:357
  137.4 32.7 %collective-permute-start.27 = (bf16[128,2560]{1,0:T(8,128)(2,1)S(1)}, bf16[128,2560]{1,0:T(8,128)(2,1)S(1)}, u32[]{:S(2)}, u32[]{:S(2)}) collective-permute-start(bf16[128,2560]{1,0:T(8,128)(2,1)S(1)} %pad_maximum_fusion.1.refs_0_), channel_id=1, source_target_pairs={{0,1},{1,0},{2,3},{3,2},{4,5},{5,4},{6,7},{7,6},{8,9},{9,8},{10,11... | collective-permute-start | bytes 1966088 | tf_op jit(solution)/shard_map/ppermute | solution.py:361
  145.7 22.4 %collective-permute-start.33 = (bf16[128,2560]{1,0:T(8,128)(2,1)S(1)}, bf16[128,2560]{1,0:T(8,128)(2,1)S(1)}, u32[]{:S(2)}, u32[]{:S(2)}) collective-permute-start(bf16[128,2560]{1,0:T(8,128)(2,1)S(1)} %constant_dynamic-update-slice_fusion.6.refs_8_), channel_id=1, source_target_pairs={{0,6},{1,7},{2,0},{3,1},{4,2},{5,3},{6,4},{7,5},{8,14},{9,15},{10,... | collective-permute-start | bytes 1966088 | tf_op jit(solution)/shard_map/ppermute | solution.py:357
  146.3 22.5 %collective-permute-start.32 = (bf16[128,2560]{1,0:T(8,128)(2,1)S(1)}, bf16[128,2560]{1,0:T(8,128)(2,1)S(1)}, u32[]{:S(2)}, u32[]{:S(2)}) collective-permute-start(bf16[128,2560]{1,0:T(8,128)(2,1)S(1)} %constant_dynamic-update-slice_fusion.6.refs_8_), channel_id=1, source_target_pairs={{0,16},{1,9},{2,18},{3,11},{4,20},{5,13},{6,22},{7,15},{8,24},{9,1... | collective-permute-start | bytes 1966088 | tf_op jit(solution)/shard_map/ppermute | solution.py:369
  147.5 21.2 %collective-permute-start.31 = (bf16[128,2560]{1,0:T(8,128)(2,1)S(1)}, bf16[128,2560]{1,0:T(8,128)(2,1)S(1)}, u32[]{:S(2)}, u32[]{:S(2)}) collective-permute-start(bf16[128,2560]{1,0:T(8,128)(2,1)S(1)} %constant_dynamic-update-slice_fusion.6.refs_8_), channel_id=1, source_target_pairs={{0,8},{1,17},{2,10},{3,19},{4,12},{5,21},{6,14},{7,23},{8,0},{9,25... | collective-permute-start | bytes 1966088 | tf_op jit(solution)/shard_map/ppermute | solution.py:369
  150.1 18.1 %collective-permute-start.26 = (bf16[128,1536]{1,0:T(8,128)(2,1)S(1)}, bf16[128,1536]{1,0:T(8,128)(2,1)S(1)}, u32[]{:S(2)}, u32[]{:S(2)}) collective-permute-start(bf16[128,1536]{1,0:T(8,128)(2,1)S(1)} %collective-permute-done.23), channel_id=1, source_target_pairs={{0,16},{1,9},{2,18},{3,11},{4,20},{5,13},{6,22},{7,15},{8,24},{9,1... | collective-permute-start | bytes 1179656 | tf_op jit(solution)/shard_map/ppermute | solution.py:369
  168.8 17.3 %collective-permute-start.34 = (bf16[128,2560]{1,0:T(8,128)(2,1)S(1)}, bf16[128,2560]{1,0:T(8,128)(2,1)S(1)}, u32[]{:S(2)}, u32[]{:S(2)}) collective-permute-start(bf16[128,2560]{1,0:T(8,128)(2,1)S(1)} %collective-permute-done.31.refs_9_), channel_id=1, source_target_pairs={{0,16},{1,9},{2,18},{3,11},{4,20},{5,13},{6,22},{7,15},{8,24},{9,1... | collective-permute-start | bytes 1966088 | tf_op jit(solution)/shard_map/ppermute | solution.py:369
  170.0 16.1 %collective-permute-start.40 = (bf16[128,2560]{1,0:T(8,128)(2,1)S(1)}, bf16[128,2560]{1,0:T(8,128)(2,1)S(1)}, u32[]{:S(2)}, u32[]{:S(2)}) collective-permute-start(bf16[128,2560]{1,0:T(8,128)(2,1)S(1)} %collective-permute-done.33.refs_16_), channel_id=1, source_target_pairs={{0,6},{1,7},{2,0},{3,1},{4,2},{5,3},{6,4},{7,5},{8,14},{9,15},{10,... | collective-permute-start | bytes 1966088 | tf_op jit(solution)/shard_map/ppermute | solution.py:357
  170.1 16.5 %collective-permute-start.39 = (bf16[128,2560]{1,0:T(8,128)(2,1)S(1)}, bf16[128,2560]{1,0:T(8,128)(2,1)S(1)}, u32[]{:S(2)}, u32[]{:S(2)}) collective-permute-start(bf16[128,2560]{1,0:T(8,128)(2,1)S(1)} %collective-permute-done.33.refs_16_), channel_id=1, source_target_pairs={{0,8},{1,17},{2,10},{3,19},{4,12},{5,21},{6,14},{7,23},{8,0},{9,25... | collective-permute-start | bytes 1966088 | tf_op jit(solution)/shard_map/ppermute | solution.py:369
  170.8 15.9 %collective-permute-start.29 = (bf16[128,2560]{1,0:T(8,128)(2,1)S(1)}, bf16[128,2560]{1,0:T(8,128)(2,1)S(1)}, u32[]{:S(2)}, u32[]{:S(2)}) collective-permute-start(bf16[128,2560]{1,0:T(8,128)(2,1)S(1)} %constant_dynamic-update-slice_fusion.2.refs_2_), channel_id=1, source_target_pairs={{0,1},{1,0},{2,3},{3,2},{4,5},{5,4},{6,7},{7,6},{8,9},{9,8},{10,11... | collective-permute-start | bytes 1966088 | tf_op jit(solution)/shard_map/ppermute | solution.py:361
  171.2 16.0 %collective-permute-start.30 = (bf16[128,2560]{1,0:T(8,128)(2,1)S(1)}, bf16[128,2560]{1,0:T(8,128)(2,1)S(1)}, u32[]{:S(2)}, u32[]{:S(2)}) collective-permute-start(bf16[128,2560]{1,0:T(8,128)(2,1)S(1)} %constant_dynamic-update-slice_fusion.4.refs_3_), channel_id=1, source_target_pairs={{0,1},{1,0},{2,3},{3,2},{4,5},{5,4},{6,7},{7,6},{8,9},{9,8},{10,11... | collective-permute-start | bytes 1966088 | tf_op jit(solution)/shard_map/ppermute | solution.py:361
  186.7 30.1 %collective-permute-start.43 = (bf16[128,2560]{1,0:T(8,128)(2,1)S(1)}, bf16[128,2560]{1,0:T(8,128)(2,1)S(1)}, u32[]{:S(2)}, u32[]{:S(2)}) collective-permute-start(bf16[128,2560]{1,0:T(8,128)(2,1)S(1)} %collective-permute-done.33.refs_16_), channel_id=1, source_target_pairs={{0,1},{1,0},{2,3},{3,2},{4,5},{5,4},{6,7},{7,6},{8,9},{9,8},{10,11... | collective-permute-start | bytes 1966088 | tf_op jit(solution)/shard_map/ppermute | solution.py:361
  187.2 28.4 %collective-permute-start.48 = (bf16[128,2560]{1,0:T(8,128)(2,1)S(1)}, bf16[128,2560]{1,0:T(8,128)(2,1)S(1)}, u32[]{:S(2)}, u32[]{:S(2)}) collective-permute-start(bf16[128,2560]{1,0:T(8,128)(2,1)S(1)} %collective-permute-done.40.refs_24_), channel_id=1, source_target_pairs={{0,16},{1,9},{2,18},{3,11},{4,20},{5,13},{6,22},{7,15},{8,24},{9,1... | collective-permute-start | bytes 1966088 | tf_op jit(solution)/shard_map/ppermute | solution.py:369
  188.2 27.3 %collective-permute-start.47 = (bf16[128,2560]{1,0:T(8,128)(2,1)S(1)}, bf16[128,2560]{1,0:T(8,128)(2,1)S(1)}, u32[]{:S(2)}, u32[]{:S(2)}) collective-permute-start(bf16[128,2560]{1,0:T(8,128)(2,1)S(1)} %collective-permute-done.40.refs_24_), channel_id=1, source_target_pairs={{0,8},{1,17},{2,10},{3,19},{4,12},{5,21},{6,14},{7,23},{8,0},{9,25... | collective-permute-start | bytes 1966088 | tf_op jit(solution)/shard_map/ppermute | solution.py:369
  189.2 25.7 %collective-permute-start.41 = (bf16[128,2560]{1,0:T(8,128)(2,1)S(1)}, bf16[128,2560]{1,0:T(8,128)(2,1)S(1)}, u32[]{:S(2)}, u32[]{:S(2)}) collective-permute-start(bf16[128,2560]{1,0:T(8,128)(2,1)S(1)} %collective-permute-done.33.refs_16_), channel_id=1, source_target_pairs={{0,16},{1,9},{2,18},{3,11},{4,20},{5,13},{6,22},{7,15},{8,24},{9,1... | collective-permute-start | bytes 1966088 | tf_op jit(solution)/shard_map/ppermute | solution.py:369
  190.2 24.8 %collective-permute-start.42 = (bf16[128,2560]{1,0:T(8,128)(2,1)S(1)}, bf16[128,2560]{1,0:T(8,128)(2,1)S(1)}, u32[]{:S(2)}, u32[]{:S(2)}) collective-permute-start(bf16[128,2560]{1,0:T(8,128)(2,1)S(1)} %collective-permute-done.34.refs_11_), channel_id=1, source_target_pairs={{0,6},{1,7},{2,0},{3,1},{4,2},{5,3},{6,4},{7,5},{8,14},{9,15},{10,... | collective-permute-start | bytes 1966088 | tf_op jit(solution)/shard_map/ppermute | solution.py:357
  (57 other events, 540.9 us)

commit v5 on v4

--- a/solution.py
+++ b/solution.py
@@ -100,16 +100,12 @@
 def left_products(mine_ref, right, out_ref, index):
     line, count, depth = mine_ref.shape
     size = line * count
-
-    def step(i, carry):
-        left = mine_ref[pl.ds(2 * i, 2)].reshape(2 * count, depth)
-        product = row_product(left, right[...].reshape(size, depth))
-        out_ref[pl.ds(2 * i, 2), :, index * size:(index + 1) * size] = product.astype(
-            out_ref.dtype
-        ).reshape(2, count, size)
-        return carry
-
-    lax.fori_loop(0, line // 2, step, 0)
+    product = row_product(
+        mine_ref[...].reshape(size, depth), right[...].reshape(size, depth)
+    )
+    out_ref[:, :, index * size:(index + 1) * size] = product.astype(out_ref.dtype).reshape(
+        line, count, size
+    )
 
 
 def own_blocks_kernel(meta_ref, *refs):
@@ -218,23 +214,45 @@
     ]
 
 
-def image_parts(meta_ref, xt_ref, held_ref, levels, e, k):
+def by_columns(meta_ref, xt_ref, held_ref, levels, e, k):
     line, width, count = xt_ref.shape[2:]
     size = line * count
-    slots = len(levels)
     left, right = [], []
     for d in (1, 2, 3):
         a = e ^ d
         b = k ^ taken_core(meta_ref, a, d)
-        for n in range(slots):
-            left.append(xt_ref[a, b, levels[n]])
+        for n, level in enumerate(levels):
+            left.append(xt_ref[a, b, level])
             right.append(held_ref[a, b, n, :, (1 + d) * size:(2 + d) * size])
-    back = matmul(jnp.concatenate(left, axis=1), jnp.concatenate(right))
-    forth = row_product(
+    return matmul(jnp.concatenate(left, axis=1), jnp.concatenate(right))
+
+
+def by_rows(meta_ref, xt_ref, held_ref, e, k):
+    slots, count, width = held_ref.shape[2:]
+    return row_product(
         side_by_side(xt_ref, met_places(meta_ref, e, k)),
-        held_ref[e, k].reshape(slots * count, 5 * size),
-    )
-    return back, forth
+        held_ref[e, k].reshape(slots * count, width),
+    )
+
+
+def when_held(copies, xt_copies, slots, body):
+    wait_all(xt_copies)
+    for e in range(4):
+        if e == 1:
+            wait_all([copies[8 * i + 4 * k + o] for i in range(slots) for k in (0, 1) for o in (1, 2)])
+        if e in (0, 3):
+            wait_all([copies[8 * i + 4 * k + e] for i in range(slots) for k in (0, 1)])
+
+        def step(k, carry, e=e):
+            body(e, k)
+            return carry
+
+        lax.fori_loop(0, 2, step, 0)
+
+
+def image_parts(meta_ref, xt_ref, held_ref, levels, e, k):
+    back = by_columns(meta_ref, xt_ref, held_ref, levels, e, k)
+    return back, by_rows(meta_ref, xt_ref, held_ref, e, k)
 
 
 def early_kernel(slots, meta_ref, near_hbm, far_hbm, *refs):
@@ -242,8 +260,18 @@
     line, width, count = xt_ref.shape[2:]
     levels = [level_of(meta_ref, i, line) for i in range(slots)]
     copies = shard_copies(meta_ref, refs, range(slots), held_ref, sems)
-    copies += column_copies(near_hbm, far_hbm, xt_ref, sems, len(copies))
-    wait_all(start_all(copies))
+    xt_copies = start_all(column_copies(near_hbm, far_hbm, xt_ref, sems, len(copies)))
+    start_all(copies)
+    other_levels = [level_of(meta_ref, i, line) for i in range(slots, line)]
+
+    def rows_first(e, k):
+        forth = by_rows(meta_ref, xt_ref, held_ref, e, k)
+        for n, level in enumerate(levels):
+            acc_ref[e, k, level] = forth[:, n * count:(n + 1) * count]
+        for level in other_levels:
+            acc_ref[e, k, level] = jnp.zeros((width, count), acc_ref.dtype)
+
+    when_held(copies, xt_copies, slots, rows_first)
 
     def out_copy(i):
         return pltpu.make_async_copy(
@@ -252,11 +280,9 @@
 
     def step(i, carry):
         e, k = i // 2, lax.rem(i, 2)
-        back, forth = image_parts(meta_ref, xt_ref, held_ref, levels, e, k)
+        back = by_columns(meta_ref, xt_ref, held_ref, levels, e, k)
         for level in range(line):
-            acc_ref[e, k, level] = back[:, level * count:(level + 1) * count]
-        for n in range(slots):
-            acc_ref[e, k, levels[n]] += forth[:, n * count:(n + 1) * count]
+            acc_ref[e, k, level] += back[:, level * count:(level + 1) * count]
         out_copy(i).start()
         return carry
 

time: 262 us -> 261 us (level)
  transfers between devices with their start and end apart: 54 -> 54, of which waited for: 24 -> 24; matrix products, arithmetic and copies ran while one was open for 1% -> 1% of each run, Pallas kernels for 17% -> 16%
where the time goes in v5:
time: 261 us
  waiting for transfers between devices  123 us (47%)
  Pallas kernels  74.1 us (28%)
  starting transfers between devices  55.3 us (21%)
  local copies, waits for them, and re-layouts  5.93 us (2%)
    pallas_call x7, Pallas kernels, call(): pl.pallas_call(kernel, in_specs=specs, out_specs=pl.BlockSpec(memory_spac...  74.1 us
    ppermute x17, waiting for transfers between devices, along(): return lax.ppermute(values, 'col', pairs)  72.1 us
    ppermute x17, waiting for transfers between devices, across(): return lax.ppermute(values, ('row', 'col'), pairs)  46.3 us
    ppermute x17, starting transfers between devices, along(): return lax.ppermute(values, 'col', pairs)  26.9 us
    ppermute x17, starting transfers between devices, across(): return lax.ppermute(values, ('row', 'col'), pairs)  24.6 us
  transfers between devices with their start and end apart: 54, of which 24 were waited for; matrix products, arithmetic and copies ran while one was open for 1% of the time, Pallas kernels for 16%

profile of v5, /device:TPU:0, one launch (start us, length us, event | category | flops | bytes accessed | tf_op | source)
XLA Modules:
  0.0 261.0 jit_solution(12997439801920568287)
XLA Ops:
  1.5 5.1 %collective-permute-start = (bf16[128,1536]{1,0:T(8,128)(2,1)S(1)}, bf16[128,1536]{1,0:T(8,128)(2,1)S(1)}, u32[]{:S(2)}, u32[]{:S(2)}) collective-permute-start(bf16[128,1536]{1,0:T(8,128)(2,1)S(1)} %get-tuple-element.38), channel_id=1, source_target_pairs={{0,6},{1,7},{2,0},{3,1},{4,2},{5,3},{6,4},{7,5},{8,14},{9,15},{10,... | collective-permute-start | bytes 1179656 | tf_op jit(solution)/shard_map/ppermute | solution.py:383
  7.6 8.5 %collective-permute-done = bf16[128,1536]{1,0:T(8,128)(2,1)S(1)} collective-permute-done((bf16[128,1536]{1,0:T(8,128)(2,1)S(1)}, bf16[128,1536]{1,0:T(8,128)(2,1)S(1)}, u32[]{:S(2)}, u32[]{:S(2)}) %collective-permute-start) | collective-permute-done | bytes 393248 | tf_op jit(solution)/shard_map/ppermute | solution.py:383
  16.1 9.4 %collective-permute-done.2 = bf16[128,1536]{1,0:T(8,128)(2,1)S(1)} collective-permute-done((bf16[128,1536]{1,0:T(8,128)(2,1)S(1)}, bf16[128,1536]{1,0:T(8,128)(2,1)S(1)}, u32[]{:S(2)}, u32[]{:S(2)}) %collective-permute-start.2) | collective-permute-done | bytes 393248 | tf_op jit(solution)/shard_map/ppermute | solution.py:383
  25.5 14.6 %collective-permute-done.1 = bf16[128,1536]{1,0:T(8,128)(2,1)S(1)} collective-permute-done((bf16[128,1536]{1,0:T(8,128)(2,1)S(1)}, bf16[128,1536]{1,0:T(8,128)(2,1)S(1)}, u32[]{:S(2)}, u32[]{:S(2)}) %collective-permute-start.1) | collective-permute-done | bytes 393248 | tf_op jit(solution)/shard_map/ppermute | solution.py:383
  43.8 3.3 %shard_map.17 = bf16[4,128,1024]{2,1,0:T(8,128)(2,1)S(1)} custom-call(s32[4]{0:T(128)S(1)} %pad_add_fusion.meta_ref, bf16[512,1536]{1,0:T(8,128)(2,1)S(1)} %pad_maximum_fusion.refs_0_, bf16[512,1536]{1,0:T(8,128)(2,1)} %collective-permute-done.3.refs_1_.refs_3_), custom_call_target="tpu_custom_call" | custom-call | flops 1610612736 | bytes 3145744 | tf_op jit(solution)/shard_map/pallas_call | solution.py:66
  49.0 2.7 %collective-permute-start.4 = (bf16[128,1024]{1,0:T(8,128)(2,1)}, bf16[128,1024]{1,0:T(8,128)(2,1)S(1)}, u32[]{:S(2)}, u32[]{:S(2)}) collective-permute-start(bf16[128,1024]{1,0:T(8,128)(2,1)} %get-tuple-element.44), channel_id=1, source_target_pairs={{0,6},{1,7},{2,0},{3,1},{4,2},{5,3},{6,4},{7,5},{8,14},{9,15},{10,... | collective-permute-start | bytes 786440 | tf_op jit(solution)/shard_map/ppermute | solution.py:383
  52.2 12.5 %collective-permute-done.4 = bf16[128,1024]{1,0:T(8,128)(2,1)S(1)} collective-permute-done((bf16[128,1024]{1,0:T(8,128)(2,1)}, bf16[128,1024]{1,0:T(8,128)(2,1)S(1)}, u32[]{:S(2)}, u32[]{:S(2)}) %collective-permute-start.4) | collective-permute-done | bytes 262176 | tf_op jit(solution)/shard_map/ppermute | solution.py:383
  64.7 9.1 %collective-permute-done.5 = bf16[128,1024]{1,0:T(8,128)(2,1)} collective-permute-done((bf16[128,1024]{1,0:T(8,128)(2,1)}, bf16[128,1024]{1,0:T(8,128)(2,1)}, u32[]{:S(2)}, u32[]{:S(2)}) %collective-permute-start.5) | collective-permute-done | bytes 262176 | tf_op jit(solution)/shard_map/ppermute | solution.py:383
  79.2 2.6 %collective-permute-start.7 = (bf16[128,1024]{1,0:T(8,128)(2,1)S(1)}, bf16[128,1024]{1,0:T(8,128)(2,1)S(1)}, u32[]{:S(2)}, u32[]{:S(2)}) collective-permute-start(bf16[128,1024]{1,0:T(8,128)(2,1)S(1)} %fusion.5), channel_id=1, source_target_pairs={{0,6},{1,7},{2,0},{3,1},{4,2},{5,3},{6,4},{7,5},{8,14},{9,15},{10,... | collective-permute-start | bytes 786440 | tf_op jit(solution)/shard_map/ppermute | solution.py:383
  84.2 4.7 %shard_map.19 = bf16[4,128,1024]{2,1,0:T(8,128)(2,1)S(1)} custom-call(s32[4]{0:T(128)S(1)} %pad_add_fusion.meta_ref, bf16[512,1536]{1,0:T(8,128)(2,1)S(1)} %pad_maximum_fusion.refs_0_, bf16[512,1536]{1,0:T(8,128)(2,1)} %collective-permute-done.8.refs_1_, bf16[512,1536]{1,0:T(8,128)(2,1)S(1)} %collective-permute-done.9.refs_2_, bf16[512,1536]{1,0:T(8,128)(2,1)} %copy-done.2, ...), custom_call_target="tpu_custom_call" | custom-call | flops 1610612736 | bytes 7864336 | tf_op jit(solution)/shard_map/pallas_call | solution.py:66
  89.1 3.8 %collective-permute-start.13 = (bf16[128,1024]{1,0:T(8,128)(2,1)S(1)}, bf16[128,1024]{1,0:T(8,128)(2,1)S(1)}, u32[]{:S(2)}, u32[]{:S(2)}) collective-permute-start(bf16[128,1024]{1,0:T(8,128)(2,1)S(1)} %get-tuple-element.43), channel_id=1, source_target_pairs={{0,6},{1,7},{2,0},{3,1},{4,2},{5,3},{6,4},{7,5},{8,14},{9,15},{10,... | collective-permute-start | bytes 786440 | tf_op jit(solution)/shard_map/ppermute | solution.py:383
  92.9 8.0 %shard_map.18.near_hbm = bf16[3,2,4,768,128]{4,3,2,1,0:T(8,128)(2,1)} custom-call(s32[4]{0:T(128)S(1)} %pad_add_fusion.meta_ref, bf16[512,1536]{1,0:T(8,128)(2,1)S(1)} %pad_maximum_fusion.refs_0_, bf16[512,1536]{1,0:T(8,128)(2,1)} %collective-permute-done.8.refs_1_, bf16[512,1536]{1,0:T(8,128)(2,1)S(1)} %collective-permute-done.9.refs_2_, ...), custom_call_target="tpu_custom_call" | custom-call | flops 150994944 | bytes 9437200 | tf_op jit(solution)/shard_map/pallas_call | solution.py:66
  103.2 2.7 %collective-permute-start.19 = (bf16[128,1024]{1,0:T(8,128)(2,1)S(1)}, bf16[128,1024]{1,0:T(8,128)(2,1)S(1)}, u32[]{:S(2)}, u32[]{:S(2)}) collective-permute-start(bf16[128,1024]{1,0:T(8,128)(2,1)S(1)} %fusion.5), channel_id=1, source_target_pairs={{0,8},{1,17},{2,10},{3,19},{4,12},{5,21},{6,14},{7,23},{8,0},{9,25... | collective-permute-start | bytes 786440 | tf_op jit(solution)/shard_map/ppermute | solution.py:395
  114.3 3.6 %collective-permute-start.17 = (bf16[128,512]{1,0:T(8,128)(2,1)S(1)}, bf16[128,512]{1,0:T(8,128)(2,1)S(1)}, u32[]{:S(2)}, u32[]{:S(2)}) collective-permute-start(bf16[128,512]{1,0:T(8,128)(2,1)S(1)} %get-tuple-element.47), channel_id=1, source_target_pairs={{0,6},{1,7},{2,0},{3,1},{4,2},{5,3},{6,4},{7,5},{8,14},{9,15},{10,... | collective-permute-start | bytes 393224 | tf_op jit(solution)/shard_map/ppermute | solution.py:383
  117.8 3.0 %collective-permute-done.16 = bf16[128,1024]{1,0:T(8,128)(2,1)S(1)} collective-permute-done((bf16[128,1024]{1,0:T(8,128)(2,1)S(1)}, bf16[128,1024]{1,0:T(8,128)(2,1)S(1)}, u32[]{:S(2)}, u32[]{:S(2)}) %collective-permute-start.16) | collective-permute-done | bytes 262176 | tf_op jit(solution)/shard_map/ppermute | solution.py:383
  126.8 4.2 %collective-permute-done.21 = bf16[128,512]{1,0:T(8,128)(2,1)S(1)} collective-permute-done((bf16[128,512]{1,0:T(8,128)(2,1)S(1)}, bf16[128,512]{1,0:T(8,128)(2,1)S(1)}, u32[]{:S(2)}, u32[]{:S(2)}) %collective-permute-start.21) | collective-permute-done | bytes 131104 | tf_op jit(solution)/shard_map/ppermute | solution.py:383
  134.1 2.8 %collective-permute-start.23 = (bf16[128,1536]{1,0:T(8,128)(2,1)S(1)}, bf16[128,1536]{1,0:T(8,128)(2,1)S(1)}, u32[]{:S(2)}, u32[]{:S(2)}) collective-permute-start(bf16[128,1536]{1,0:T(8,128)(2,1)S(1)} %pad_maximum_fusion.2), channel_id=1, source_target_pairs={{0,8},{1,17},{2,10},{3,19},{4,12},{5,21},{6,14},{7,23},{8,0},{9,25... | collective-permute-start | bytes 1179656 | tf_op jit(solution)/shard_map/ppermute | solution.py:395
  137.1 4.4 %collective-permute-done.25 = bf16[128,1536]{1,0:T(8,128)(2,1)S(1)} collective-permute-done((bf16[128,1536]{1,0:T(8,128)(2,1)S(1)}, bf16[128,1536]{1,0:T(8,128)(2,1)S(1)}, u32[]{:S(2)}, u32[]{:S(2)}) %collective-permute-start.25) | collective-permute-done | bytes 393248 | tf_op jit(solution)/shard_map/ppermute | solution.py:383
  141.5 3.8 %collective-permute-done.24 = bf16[128,1536]{1,0:T(8,128)(2,1)S(1)} collective-permute-done((bf16[128,1536]{1,0:T(8,128)(2,1)S(1)}, bf16[128,1536]{1,0:T(8,128)(2,1)S(1)}, u32[]{:S(2)}, u32[]{:S(2)}) %collective-permute-start.24) | collective-permute-done | bytes 393248 | tf_op jit(solution)/shard_map/ppermute | solution.py:395
  150.5 17.1 %collective-permute-done.26 = bf16[128,1536]{1,0:T(8,128)(2,1)S(1)} collective-permute-done((bf16[128,1536]{1,0:T(8,128)(2,1)S(1)}, bf16[128,1536]{1,0:T(8,128)(2,1)S(1)}, u32[]{:S(2)}, u32[]{:S(2)}) %collective-permute-start.26) | collective-permute-done | bytes 393248 | tf_op jit(solution)/shard_map/ppermute | solution.py:395
  170.9 14.7 %collective-permute-done.34.refs_11_ = bf16[128,2560]{1,0:T(8,128)(2,1)S(1)} collective-permute-done((bf16[128,2560]{1,0:T(8,128)(2,1)S(1)}, bf16[128,2560]{1,0:T(8,128)(2,1)S(1)}, u32[]{:S(2)}, u32[]{:S(2)}) %collective-permute-start.34) | collective-permute-done | bytes 655392 | tf_op jit(solution)/shard_map/ppermute | solution.py:395
  191.6 22.3 %shard_map.22.acc_hbm = f32[4,2,4,768,128]{4,3,2,1,0:T(8,128)} custom-call(s32[4]{0:T(128)S(1)} %pad_add_fusion.meta_ref, bf16[3,2,4,768,128]{4,3,2,1,0:T(8,128)(2,1)} %shard_map.18.near_hbm, bf16[1,2,4,768,128]{4,3,2,1,0:T(8,128)(2,1)} %copy-done, bf16[128,2560]{1,0:T(8,128)(2,1)S(1)} %pad_maximum_fusion.1.refs_0_, ...), custom_call_target="tpu_custom_call" | custom-call | flops 12884901888 | bytes 16777232 | tf_op jit(solution)/shard_map/pallas_call | solution.py:66
  217.2 8.1 %collective-permute-done.49.refs_27_ = bf16[128,2560]{1,0:T(8,128)(2,1)S(1)} collective-permute-done((bf16[128,2560]{1,0:T(8,128)(2,1)S(1)}, bf16[128,2560]{1,0:T(8,128)(2,1)S(1)}, u32[]{:S(2)}, u32[]{:S(2)}) %collective-permute-start.49) | collective-permute-done | bytes 655392 | tf_op jit(solution)/shard_map/ppermute | solution.py:395
  228.3 32.5 %shard_map.23 = bf16[4,2,128,768]{3,2,1,0:T(8,128)(2,1)} custom-call(s32[4]{0:T(128)S(1)} %pad_add_fusion.meta_ref, bf16[3,2,4,768,128]{4,3,2,1,0:T(8,128)(2,1)} %shard_map.18.near_hbm, bf16[1,2,4,768,128]{4,3,2,1,0:T(8,128)(2,1)} %copy-done, f32[4,2,4,768,128]{4,3,2,1,0:T(8,128)} %shard_map.22.acc_hbm, bf16[128,2560]{1,0:T(8,128)(2,1)S(1)} %pad_maximum_fusion.1.refs_0_, ...), custom_call_target="tpu_custom_call" | custom-call | flops 19327352832 | bytes 39845904 | tf_op jit(solution)/shard_map/pallas_call | solution.py:66
  (164 shorter events, 56.7 us)
Async XLA Ops:
  1.5 14.6 %collective-permute-start = (bf16[128,1536]{1,0:T(8,128)(2,1)S(1)}, bf16[128,1536]{1,0:T(8,128)(2,1)S(1)}, u32[]{:S(2)}, u32[]{:S(2)}) collective-permute-start(bf16[128,1536]{1,0:T(8,128)(2,1)S(1)} %get-tuple-element.38), channel_id=1, source_target_pairs={{0,6},{1,7},{2,0},{3,1},{4,2},{5,3},{6,4},{7,5},{8,14},{9,15},{10,... | collective-permute-start | bytes 1179656 | tf_op jit(solution)/shard_map/ppermute | solution.py:383
  6.6 19.0 %collective-permute-start.2 = (bf16[128,1536]{1,0:T(8,128)(2,1)S(1)}, bf16[128,1536]{1,0:T(8,128)(2,1)S(1)}, u32[]{:S(2)}, u32[]{:S(2)}) collective-permute-start(bf16[128,1536]{1,0:T(8,128)(2,1)S(1)} %get-tuple-element.39), channel_id=1, source_target_pairs={{0,2},{1,3},{2,4},{3,5},{4,6},{5,7},{6,0},{7,1},{8,10},{9,11},{10,... | collective-permute-start | bytes 1179656 | tf_op jit(solution)/shard_map/ppermute | solution.py:383
  6.6 33.5 %collective-permute-start.1 = (bf16[128,1536]{1,0:T(8,128)(2,1)S(1)}, bf16[128,1536]{1,0:T(8,128)(2,1)S(1)}, u32[]{:S(2)}, u32[]{:S(2)}) collective-permute-start(bf16[128,1536]{1,0:T(8,128)(2,1)S(1)} %get-tuple-element.40), channel_id=1, source_target_pairs={{0,4},{1,5},{2,6},{3,7},{4,0},{5,1},{6,2},{7,3},{8,12},{9,13},{10,... | collective-permute-start | bytes 1179656 | tf_op jit(solution)/shard_map/ppermute | solution.py:383
  40.3 36.7 %collective-permute-start.9 = (bf16[512,1536]{1,0:T(8,128)(2,1)S(1)}, bf16[512,1536]{1,0:T(8,128)(2,1)S(1)}, u32[]{:S(2)}, u32[]{:S(2)}) collective-permute-start(bf16[512,1536]{1,0:T(8,128)(2,1)S(1)} %pad_maximum_fusion.refs_0_), channel_id=1, source_target_pairs={{0,16},{1,9},{2,18},{3,11},{4,20},{5,13},{6,22},{7,15},{8,24},{9,1... | collective-permute-start | bytes 4718600 | tf_op jit(solution)/shard_map/ppermute | solution.py:395
  41.9 35.3 %collective-permute-start.8 = (bf16[512,1536]{1,0:T(8,128)(2,1)S(1)}, bf16[512,1536]{1,0:T(8,128)(2,1)}, u32[]{:S(2)}, u32[]{:S(2)}) collective-permute-start(bf16[512,1536]{1,0:T(8,128)(2,1)S(1)} %pad_maximum_fusion.refs_0_), channel_id=1, source_target_pairs={{0,8},{1,17},{2,10},{3,19},{4,12},{5,21},{6,14},{7,23},{8,0},{9,25... | collective-permute-start | bytes 4718600 | tf_op jit(solution)/shard_map/ppermute | solution.py:395
  49.0 15.8 %collective-permute-start.4 = (bf16[128,1024]{1,0:T(8,128)(2,1)}, bf16[128,1024]{1,0:T(8,128)(2,1)S(1)}, u32[]{:S(2)}, u32[]{:S(2)}) collective-permute-start(bf16[128,1024]{1,0:T(8,128)(2,1)} %get-tuple-element.44), channel_id=1, source_target_pairs={{0,6},{1,7},{2,0},{3,1},{4,2},{5,3},{6,4},{7,5},{8,14},{9,15},{10,... | collective-permute-start | bytes 786440 | tf_op jit(solution)/shard_map/ppermute | solution.py:383
  51.6 22.2 %collective-permute-start.5 = (bf16[128,1024]{1,0:T(8,128)(2,1)}, bf16[128,1024]{1,0:T(8,128)(2,1)}, u32[]{:S(2)}, u32[]{:S(2)}) collective-permute-start(bf16[128,1024]{1,0:T(8,128)(2,1)} %get-tuple-element.46), channel_id=1, source_target_pairs={{0,4},{1,5},{2,6},{3,7},{4,0},{5,1},{6,2},{7,3},{8,12},{9,13},{10,... | collective-permute-start | bytes 786440 | tf_op jit(solution)/shard_map/ppermute | solution.py:383
  77.7 23.2 %collective-permute-start.12 = (bf16[512,1536]{1,0:T(8,128)(2,1)}, bf16[512,1536]{1,0:T(8,128)(2,1)S(1)}, u32[]{:S(2)}, u32[]{:S(2)}) collective-permute-start(bf16[512,1536]{1,0:T(8,128)(2,1)} %collective-permute-done.8.refs_1_), channel_id=1, source_target_pairs={{0,16},{1,9},{2,18},{3,11},{4,20},{5,13},{6,22},{7,15},{8,24},{9,1... | collective-permute-start | bytes 4718600 | tf_op jit(solution)/shard_map/ppermute | solution.py:395
  105.9 14.9 %collective-permute-start.16 = (bf16[128,1024]{1,0:T(8,128)(2,1)S(1)}, bf16[128,1024]{1,0:T(8,128)(2,1)S(1)}, u32[]{:S(2)}, u32[]{:S(2)}) collective-permute-start(bf16[128,1024]{1,0:T(8,128)(2,1)S(1)} %get-tuple-element.41), channel_id=1, source_target_pairs={{0,4},{1,5},{2,6},{3,7},{4,0},{5,1},{6,2},{7,3},{8,12},{9,13},{10,... | collective-permute-start | bytes 786440 | tf_op jit(solution)/shard_map/ppermute | solution.py:383
  137.0 32.6 %collective-permute-start.27 = (bf16[128,2560]{1,0:T(8,128)(2,1)S(1)}, bf16[128,2560]{1,0:T(8,128)(2,1)S(1)}, u32[]{:S(2)}, u32[]{:S(2)}) collective-permute-start(bf16[128,2560]{1,0:T(8,128)(2,1)S(1)} %pad_maximum_fusion.1.refs_0_), channel_id=1, source_target_pairs={{0,1},{1,0},{2,3},{3,2},{4,5},{5,4},{6,7},{7,6},{8,9},{9,8},{10,11... | collective-permute-start | bytes 1966088 | tf_op jit(solution)/shard_map/ppermute | solution.py:387
  145.3 22.4 %collective-permute-start.33 = (bf16[128,2560]{1,0:T(8,128)(2,1)S(1)}, bf16[128,2560]{1,0:T(8,128)(2,1)S(1)}, u32[]{:S(2)}, u32[]{:S(2)}) collective-permute-start(bf16[128,2560]{1,0:T(8,128)(2,1)S(1)} %constant_dynamic-update-slice_fusion.6.refs_8_), channel_id=1, source_target_pairs={{0,6},{1,7},{2,0},{3,1},{4,2},{5,3},{6,4},{7,5},{8,14},{9,15},{10,... | collective-permute-start | bytes 1966088 | tf_op jit(solution)/shard_map/ppermute | solution.py:383
  145.9 22.5 %collective-permute-start.32 = (bf16[128,2560]{1,0:T(8,128)(2,1)S(1)}, bf16[128,2560]{1,0:T(8,128)(2,1)S(1)}, u32[]{:S(2)}, u32[]{:S(2)}) collective-permute-start(bf16[128,2560]{1,0:T(8,128)(2,1)S(1)} %constant_dynamic-update-slice_fusion.6.refs_8_), channel_id=1, source_target_pairs={{0,16},{1,9},{2,18},{3,11},{4,20},{5,13},{6,22},{7,15},{8,24},{9,1... | collective-permute-start | bytes 1966088 | tf_op jit(solution)/shard_map/ppermute | solution.py:395
  147.0 21.3 %collective-permute-start.31 = (bf16[128,2560]{1,0:T(8,128)(2,1)S(1)}, bf16[128,2560]{1,0:T(8,128)(2,1)S(1)}, u32[]{:S(2)}, u32[]{:S(2)}) collective-permute-start(bf16[128,2560]{1,0:T(8,128)(2,1)S(1)} %constant_dynamic-update-slice_fusion.6.refs_8_), channel_id=1, source_target_pairs={{0,8},{1,17},{2,10},{3,19},{4,12},{5,21},{6,14},{7,23},{8,0},{9,25... | collective-permute-start | bytes 1966088 | tf_op jit(solution)/shard_map/ppermute | solution.py:395
  149.6 18.1 %collective-permute-start.26 = (bf16[128,1536]{1,0:T(8,128)(2,1)S(1)}, bf16[128,1536]{1,0:T(8,128)(2,1)S(1)}, u32[]{:S(2)}, u32[]{:S(2)}) collective-permute-start(bf16[128,1536]{1,0:T(8,128)(2,1)S(1)} %collective-permute-done.23), channel_id=1, source_target_pairs={{0,16},{1,9},{2,18},{3,11},{4,20},{5,13},{6,22},{7,15},{8,24},{9,1... | collective-permute-start | bytes 1179656 | tf_op jit(solution)/shard_map/ppermute | solution.py:395
  168.3 17.3 %collective-permute-start.34 = (bf16[128,2560]{1,0:T(8,128)(2,1)S(1)}, bf16[128,2560]{1,0:T(8,128)(2,1)S(1)}, u32[]{:S(2)}, u32[]{:S(2)}) collective-permute-start(bf16[128,2560]{1,0:T(8,128)(2,1)S(1)} %collective-permute-done.31.refs_9_), channel_id=1, source_target_pairs={{0,16},{1,9},{2,18},{3,11},{4,20},{5,13},{6,22},{7,15},{8,24},{9,1... | collective-permute-start | bytes 1966088 | tf_op jit(solution)/shard_map/ppermute | solution.py:395
  169.5 16.1 %collective-permute-start.40 = (bf16[128,2560]{1,0:T(8,128)(2,1)S(1)}, bf16[128,2560]{1,0:T(8,128)(2,1)S(1)}, u32[]{:S(2)}, u32[]{:S(2)}) collective-permute-start(bf16[128,2560]{1,0:T(8,128)(2,1)S(1)} %collective-permute-done.33.refs_16_), channel_id=1, source_target_pairs={{0,6},{1,7},{2,0},{3,1},{4,2},{5,3},{6,4},{7,5},{8,14},{9,15},{10,... | collective-permute-start | bytes 1966088 | tf_op jit(solution)/shard_map/ppermute | solution.py:383
  169.6 16.5 %collective-permute-start.39 = (bf16[128,2560]{1,0:T(8,128)(2,1)S(1)}, bf16[128,2560]{1,0:T(8,128)(2,1)S(1)}, u32[]{:S(2)}, u32[]{:S(2)}) collective-permute-start(bf16[128,2560]{1,0:T(8,128)(2,1)S(1)} %collective-permute-done.33.refs_16_), channel_id=1, source_target_pairs={{0,8},{1,17},{2,10},{3,19},{4,12},{5,21},{6,14},{7,23},{8,0},{9,25... | collective-permute-start | bytes 1966088 | tf_op jit(solution)/shard_map/ppermute | solution.py:395
  170.3 15.9 %collective-permute-start.29 = (bf16[128,2560]{1,0:T(8,128)(2,1)S(1)}, bf16[128,2560]{1,0:T(8,128)(2,1)S(1)}, u32[]{:S(2)}, u32[]{:S(2)}) collective-permute-start(bf16[128,2560]{1,0:T(8,128)(2,1)S(1)} %constant_dynamic-update-slice_fusion.2.refs_2_), channel_id=1, source_target_pairs={{0,1},{1,0},{2,3},{3,2},{4,5},{5,4},{6,7},{7,6},{8,9},{9,8},{10,11... | collective-permute-start | bytes 1966088 | tf_op jit(solution)/shard_map/ppermute | solution.py:387
  170.7 15.9 %collective-permute-start.30 = (bf16[128,2560]{1,0:T(8,128)(2,1)S(1)}, bf16[128,2560]{1,0:T(8,128)(2,1)S(1)}, u32[]{:S(2)}, u32[]{:S(2)}) collective-permute-start(bf16[128,2560]{1,0:T(8,128)(2,1)S(1)} %constant_dynamic-update-slice_fusion.4.refs_3_), channel_id=1, source_target_pairs={{0,1},{1,0},{2,3},{3,2},{4,5},{5,4},{6,7},{7,6},{8,9},{9,8},{10,11... | collective-permute-start | bytes 1966088 | tf_op jit(solution)/shard_map/ppermute | solution.py:387
  186.2 29.6 %collective-permute-start.43 = (bf16[128,2560]{1,0:T(8,128)(2,1)S(1)}, bf16[128,2560]{1,0:T(8,128)(2,1)S(1)}, u32[]{:S(2)}, u32[]{:S(2)}) collective-permute-start(bf16[128,2560]{1,0:T(8,128)(2,1)S(1)} %collective-permute-done.33.refs_16_), channel_id=1, source_target_pairs={{0,1},{1,0},{2,3},{3,2},{4,5},{5,4},{6,7},{7,6},{8,9},{9,8},{10,11... | collective-permute-start | bytes 1966088 | tf_op jit(solution)/shard_map/ppermute | solution.py:387
  186.6 27.9 %collective-permute-start.48 = (bf16[128,2560]{1,0:T(8,128)(2,1)S(1)}, bf16[128,2560]{1,0:T(8,128)(2,1)S(1)}, u32[]{:S(2)}, u32[]{:S(2)}) collective-permute-start(bf16[128,2560]{1,0:T(8,128)(2,1)S(1)} %collective-permute-done.40.refs_24_), channel_id=1, source_target_pairs={{0,16},{1,9},{2,18},{3,11},{4,20},{5,13},{6,22},{7,15},{8,24},{9,1... | collective-permute-start | bytes 1966088 | tf_op jit(solution)/shard_map/ppermute | solution.py:395
  187.7 26.9 %collective-permute-start.47 = (bf16[128,2560]{1,0:T(8,128)(2,1)S(1)}, bf16[128,2560]{1,0:T(8,128)(2,1)S(1)}, u32[]{:S(2)}, u32[]{:S(2)}) collective-permute-start(bf16[128,2560]{1,0:T(8,128)(2,1)S(1)} %collective-permute-done.40.refs_24_), channel_id=1, source_target_pairs={{0,8},{1,17},{2,10},{3,19},{4,12},{5,21},{6,14},{7,23},{8,0},{9,25... | collective-permute-start | bytes 1966088 | tf_op jit(solution)/shard_map/ppermute | solution.py:395
  188.6 25.3 %collective-permute-start.41 = (bf16[128,2560]{1,0:T(8,128)(2,1)S(1)}, bf16[128,2560]{1,0:T(8,128)(2,1)S(1)}, u32[]{:S(2)}, u32[]{:S(2)}) collective-permute-start(bf16[128,2560]{1,0:T(8,128)(2,1)S(1)} %collective-permute-done.33.refs_16_), channel_id=1, source_target_pairs={{0,16},{1,9},{2,18},{3,11},{4,20},{5,13},{6,22},{7,15},{8,24},{9,1... | collective-permute-start | bytes 1966088 | tf_op jit(solution)/shard_map/ppermute | solution.py:395
  189.6 24.4 %collective-permute-start.42 = (bf16[128,2560]{1,0:T(8,128)(2,1)S(1)}, bf16[128,2560]{1,0:T(8,128)(2,1)S(1)}, u32[]{:S(2)}, u32[]{:S(2)}) collective-permute-start(bf16[128,2560]{1,0:T(8,128)(2,1)S(1)} %collective-permute-done.34.refs_11_), channel_id=1, source_target_pairs={{0,6},{1,7},{2,0},{3,1},{4,2},{5,3},{6,4},{7,5},{8,14},{9,15},{10,... | collective-permute-start | bytes 1966088 | tf_op jit(solution)/shard_map/ppermute | solution.py:383
  (57 other events, 540.2 us)

commit v6 on v5

--- a/solution.py
+++ b/solution.py
@@ -492,8 +492,8 @@
                 pltpu.SemaphoreType.DMA((8 * cut + 2,)),
                 pltpu.SemaphoreType.DMA((8,)),
             ],
-            space=pl.ANY,
-            out_space=pl.ANY,
+            space=pltpu.HBM,
+            out_space=pltpu.HBM,
         )
 
     late = line - 2 if line > 3 else line
@@ -535,7 +535,7 @@
             pltpu.SemaphoreType.DMA((2,)),
             pltpu.SemaphoreType.DMA((8 * line,)),
         ],
-        space=pl.ANY,
+        space=pltpu.HBM,
     )
     return update.reshape(2 * size, slab)
 

time: 261 us -> 261 us (level)
  no operation moved by 1% of the time
where the time goes in v6:
time: 261 us
  waiting for transfers between devices  123 us (47%)
  Pallas kernels  74.1 us (28%)
  starting transfers between devices  55.3 us (21%)
  local copies, waits for them, and re-layouts  5.93 us (2%)
    pallas_call x7, Pallas kernels, call(): pl.pallas_call(kernel, in_specs=specs, out_specs=pl.BlockSpec(memory_spac...  74.1 us
    ppermute x17, waiting for transfers between devices, along(): return lax.ppermute(values, 'col', pairs)  72.1 us
    ppermute x17, waiting for transfers between devices, across(): return lax.ppermute(values, ('row', 'col'), pairs)  46.3 us
    ppermute x17, starting transfers between devices, along(): return lax.ppermute(values, 'col', pairs)  26.9 us
    ppermute x17, starting transfers between devices, across(): return lax.ppermute(values, ('row', 'col'), pairs)  24.6 us
  transfers between devices with their start and end apart: 54, of which 24 were waited for; matrix products, arithmetic and copies ran while one was open for 1% of the time, Pallas kernels for 16%

profile of v6, /device:TPU:0, one launch (start us, length us, event | category | flops | bytes accessed | tf_op | source)
XLA Modules:
  0.0 261.0 jit_solution(12997439801920568287)
XLA Ops:
  1.5 5.1 %collective-permute-start = (bf16[128,1536]{1,0:T(8,128)(2,1)S(1)}, bf16[128,1536]{1,0:T(8,128)(2,1)S(1)}, u32[]{:S(2)}, u32[]{:S(2)}) collective-permute-start(bf16[128,1536]{1,0:T(8,128)(2,1)S(1)} %get-tuple-element.38), channel_id=1, source_target_pairs={{0,6},{1,7},{2,0},{3,1},{4,2},{5,3},{6,4},{7,5},{8,14},{9,15},{10,... | collective-permute-start | bytes 1179656 | tf_op jit(solution)/shard_map/ppermute | solution.py:383
  7.6 8.5 %collective-permute-done = bf16[128,1536]{1,0:T(8,128)(2,1)S(1)} collective-permute-done((bf16[128,1536]{1,0:T(8,128)(2,1)S(1)}, bf16[128,1536]{1,0:T(8,128)(2,1)S(1)}, u32[]{:S(2)}, u32[]{:S(2)}) %collective-permute-start) | collective-permute-done | bytes 393248 | tf_op jit(solution)/shard_map/ppermute | solution.py:383
  16.1 9.4 %collective-permute-done.2 = bf16[128,1536]{1,0:T(8,128)(2,1)S(1)} collective-permute-done((bf16[128,1536]{1,0:T(8,128)(2,1)S(1)}, bf16[128,1536]{1,0:T(8,128)(2,1)S(1)}, u32[]{:S(2)}, u32[]{:S(2)}) %collective-permute-start.2) | collective-permute-done | bytes 393248 | tf_op jit(solution)/shard_map/ppermute | solution.py:383
  25.5 14.6 %collective-permute-done.1 = bf16[128,1536]{1,0:T(8,128)(2,1)S(1)} collective-permute-done((bf16[128,1536]{1,0:T(8,128)(2,1)S(1)}, bf16[128,1536]{1,0:T(8,128)(2,1)S(1)}, u32[]{:S(2)}, u32[]{:S(2)}) %collective-permute-start.1) | collective-permute-done | bytes 393248 | tf_op jit(solution)/shard_map/ppermute | solution.py:383
  43.8 3.3 %shard_map.17 = bf16[4,128,1024]{2,1,0:T(8,128)(2,1)S(1)} custom-call(s32[4]{0:T(128)S(1)} %pad_add_fusion.meta_ref, bf16[512,1536]{1,0:T(8,128)(2,1)S(1)} %pad_maximum_fusion.refs_0_, bf16[512,1536]{1,0:T(8,128)(2,1)} %collective-permute-done.3.refs_1_.refs_3_), custom_call_target="tpu_custom_call" | custom-call | flops 1610612736 | bytes 3145744 | tf_op jit(solution)/shard_map/pallas_call | solution.py:66
  49.0 2.7 %collective-permute-start.4 = (bf16[128,1024]{1,0:T(8,128)(2,1)}, bf16[128,1024]{1,0:T(8,128)(2,1)S(1)}, u32[]{:S(2)}, u32[]{:S(2)}) collective-permute-start(bf16[128,1024]{1,0:T(8,128)(2,1)} %get-tuple-element.44), channel_id=1, source_target_pairs={{0,6},{1,7},{2,0},{3,1},{4,2},{5,3},{6,4},{7,5},{8,14},{9,15},{10,... | collective-permute-start | bytes 786440 | tf_op jit(solution)/shard_map/ppermute | solution.py:383
  52.2 12.5 %collective-permute-done.4 = bf16[128,1024]{1,0:T(8,128)(2,1)S(1)} collective-permute-done((bf16[128,1024]{1,0:T(8,128)(2,1)}, bf16[128,1024]{1,0:T(8,128)(2,1)S(1)}, u32[]{:S(2)}, u32[]{:S(2)}) %collective-permute-start.4) | collective-permute-done | bytes 262176 | tf_op jit(solution)/shard_map/ppermute | solution.py:383
  64.7 9.1 %collective-permute-done.5 = bf16[128,1024]{1,0:T(8,128)(2,1)} collective-permute-done((bf16[128,1024]{1,0:T(8,128)(2,1)}, bf16[128,1024]{1,0:T(8,128)(2,1)}, u32[]{:S(2)}, u32[]{:S(2)}) %collective-permute-start.5) | collective-permute-done | bytes 262176 | tf_op jit(solution)/shard_map/ppermute | solution.py:383
  79.2 2.6 %collective-permute-start.7 = (bf16[128,1024]{1,0:T(8,128)(2,1)S(1)}, bf16[128,1024]{1,0:T(8,128)(2,1)S(1)}, u32[]{:S(2)}, u32[]{:S(2)}) collective-permute-start(bf16[128,1024]{1,0:T(8,128)(2,1)S(1)} %fusion.5), channel_id=1, source_target_pairs={{0,6},{1,7},{2,0},{3,1},{4,2},{5,3},{6,4},{7,5},{8,14},{9,15},{10,... | collective-permute-start | bytes 786440 | tf_op jit(solution)/shard_map/ppermute | solution.py:383
  84.2 4.7 %shard_map.19 = bf16[4,128,1024]{2,1,0:T(8,128)(2,1)S(1)} custom-call(s32[4]{0:T(128)S(1)} %pad_add_fusion.meta_ref, bf16[512,1536]{1,0:T(8,128)(2,1)S(1)} %pad_maximum_fusion.refs_0_, bf16[512,1536]{1,0:T(8,128)(2,1)} %collective-permute-done.8.refs_1_, bf16[512,1536]{1,0:T(8,128)(2,1)S(1)} %collective-permute-done.9.refs_2_, bf16[512,1536]{1,0:T(8,128)(2,1)} %copy-done.2, ...), custom_call_target="tpu_custom_call" | custom-call | flops 1610612736 | bytes 7864336 | tf_op jit(solution)/shard_map/pallas_call | solution.py:66
  89.1 3.8 %collective-permute-start.13 = (bf16[128,1024]{1,0:T(8,128)(2,1)S(1)}, bf16[128,1024]{1,0:T(8,128)(2,1)S(1)}, u32[]{:S(2)}, u32[]{:S(2)}) collective-permute-start(bf16[128,1024]{1,0:T(8,128)(2,1)S(1)} %get-tuple-element.43), channel_id=1, source_target_pairs={{0,6},{1,7},{2,0},{3,1},{4,2},{5,3},{6,4},{7,5},{8,14},{9,15},{10,... | collective-permute-start | bytes 786440 | tf_op jit(solution)/shard_map/ppermute | solution.py:383
  92.9 8.0 %shard_map.18.near_hbm = bf16[3,2,4,768,128]{4,3,2,1,0:T(8,128)(2,1)} custom-call(s32[4]{0:T(128)S(1)} %pad_add_fusion.meta_ref, bf16[512,1536]{1,0:T(8,128)(2,1)S(1)} %pad_maximum_fusion.refs_0_, bf16[512,1536]{1,0:T(8,128)(2,1)} %collective-permute-done.8.refs_1_, bf16[512,1536]{1,0:T(8,128)(2,1)S(1)} %collective-permute-done.9.refs_2_, ...), custom_call_target="tpu_custom_call" | custom-call | flops 150994944 | bytes 9437200 | tf_op jit(solution)/shard_map/pallas_call | solution.py:66
  103.2 2.7 %collective-permute-start.19 = (bf16[128,1024]{1,0:T(8,128)(2,1)S(1)}, bf16[128,1024]{1,0:T(8,128)(2,1)S(1)}, u32[]{:S(2)}, u32[]{:S(2)}) collective-permute-start(bf16[128,1024]{1,0:T(8,128)(2,1)S(1)} %fusion.5), channel_id=1, source_target_pairs={{0,8},{1,17},{2,10},{3,19},{4,12},{5,21},{6,14},{7,23},{8,0},{9,25... | collective-permute-start | bytes 786440 | tf_op jit(solution)/shard_map/ppermute | solution.py:395
  114.3 3.6 %collective-permute-start.17 = (bf16[128,512]{1,0:T(8,128)(2,1)S(1)}, bf16[128,512]{1,0:T(8,128)(2,1)S(1)}, u32[]{:S(2)}, u32[]{:S(2)}) collective-permute-start(bf16[128,512]{1,0:T(8,128)(2,1)S(1)} %get-tuple-element.47), channel_id=1, source_target_pairs={{0,6},{1,7},{2,0},{3,1},{4,2},{5,3},{6,4},{7,5},{8,14},{9,15},{10,... | collective-permute-start | bytes 393224 | tf_op jit(solution)/shard_map/ppermute | solution.py:383
  117.8 3.0 %collective-permute-done.16 = bf16[128,1024]{1,0:T(8,128)(2,1)S(1)} collective-permute-done((bf16[128,1024]{1,0:T(8,128)(2,1)S(1)}, bf16[128,1024]{1,0:T(8,128)(2,1)S(1)}, u32[]{:S(2)}, u32[]{:S(2)}) %collective-permute-start.16) | collective-permute-done | bytes 262176 | tf_op jit(solution)/shard_map/ppermute | solution.py:383
  126.8 4.2 %collective-permute-done.21 = bf16[128,512]{1,0:T(8,128)(2,1)S(1)} collective-permute-done((bf16[128,512]{1,0:T(8,128)(2,1)S(1)}, bf16[128,512]{1,0:T(8,128)(2,1)S(1)}, u32[]{:S(2)}, u32[]{:S(2)}) %collective-permute-start.21) | collective-permute-done | bytes 131104 | tf_op jit(solution)/shard_map/ppermute | solution.py:383
  134.1 2.8 %collective-permute-start.23 = (bf16[128,1536]{1,0:T(8,128)(2,1)S(1)}, bf16[128,1536]{1,0:T(8,128)(2,1)S(1)}, u32[]{:S(2)}, u32[]{:S(2)}) collective-permute-start(bf16[128,1536]{1,0:T(8,128)(2,1)S(1)} %pad_maximum_fusion.2), channel_id=1, source_target_pairs={{0,8},{1,17},{2,10},{3,19},{4,12},{5,21},{6,14},{7,23},{8,0},{9,25... | collective-permute-start | bytes 1179656 | tf_op jit(solution)/shard_map/ppermute | solution.py:395
  137.1 4.4 %collective-permute-done.25 = bf16[128,1536]{1,0:T(8,128)(2,1)S(1)} collective-permute-done((bf16[128,1536]{1,0:T(8,128)(2,1)S(1)}, bf16[128,1536]{1,0:T(8,128)(2,1)S(1)}, u32[]{:S(2)}, u32[]{:S(2)}) %collective-permute-start.25) | collective-permute-done | bytes 393248 | tf_op jit(solution)/shard_map/ppermute | solution.py:383
  141.5 3.8 %collective-permute-done.24 = bf16[128,1536]{1,0:T(8,128)(2,1)S(1)} collective-permute-done((bf16[128,1536]{1,0:T(8,128)(2,1)S(1)}, bf16[128,1536]{1,0:T(8,128)(2,1)S(1)}, u32[]{:S(2)}, u32[]{:S(2)}) %collective-permute-start.24) | collective-permute-done | bytes 393248 | tf_op jit(solution)/shard_map/ppermute | solution.py:395
  150.5 17.1 %collective-permute-done.26 = bf16[128,1536]{1,0:T(8,128)(2,1)S(1)} collective-permute-done((bf16[128,1536]{1,0:T(8,128)(2,1)S(1)}, bf16[128,1536]{1,0:T(8,128)(2,1)S(1)}, u32[]{:S(2)}, u32[]{:S(2)}) %collective-permute-start.26) | collective-permute-done | bytes 393248 | tf_op jit(solution)/shard_map/ppermute | solution.py:395
  170.9 14.7 %collective-permute-done.34.refs_11_ = bf16[128,2560]{1,0:T(8,128)(2,1)S(1)} collective-permute-done((bf16[128,2560]{1,0:T(8,128)(2,1)S(1)}, bf16[128,2560]{1,0:T(8,128)(2,1)S(1)}, u32[]{:S(2)}, u32[]{:S(2)}) %collective-permute-start.34) | collective-permute-done | bytes 655392 | tf_op jit(solution)/shard_map/ppermute | solution.py:395
  191.6 22.3 %shard_map.22.acc_hbm = f32[4,2,4,768,128]{4,3,2,1,0:T(8,128)} custom-call(s32[4]{0:T(128)S(1)} %pad_add_fusion.meta_ref, bf16[3,2,4,768,128]{4,3,2,1,0:T(8,128)(2,1)} %shard_map.18.near_hbm, bf16[1,2,4,768,128]{4,3,2,1,0:T(8,128)(2,1)} %copy-done, bf16[128,2560]{1,0:T(8,128)(2,1)S(1)} %pad_maximum_fusion.1.refs_0_, ...), custom_call_target="tpu_custom_call" | custom-call | flops 12884901888 | bytes 16777232 | tf_op jit(solution)/shard_map/pallas_call | solution.py:66
  217.2 8.1 %collective-permute-done.49.refs_27_ = bf16[128,2560]{1,0:T(8,128)(2,1)S(1)} collective-permute-done((bf16[128,2560]{1,0:T(8,128)(2,1)S(1)}, bf16[128,2560]{1,0:T(8,128)(2,1)S(1)}, u32[]{:S(2)}, u32[]{:S(2)}) %collective-permute-start.49) | collective-permute-done | bytes 655392 | tf_op jit(solution)/shard_map/ppermute | solution.py:395
  228.3 32.5 %shard_map.23 = bf16[4,2,128,768]{3,2,1,0:T(8,128)(2,1)} custom-call(s32[4]{0:T(128)S(1)} %pad_add_fusion.meta_ref, bf16[3,2,4,768,128]{4,3,2,1,0:T(8,128)(2,1)} %shard_map.18.near_hbm, bf16[1,2,4,768,128]{4,3,2,1,0:T(8,128)(2,1)} %copy-done, f32[4,2,4,768,128]{4,3,2,1,0:T(8,128)} %shard_map.22.acc_hbm, bf16[128,2560]{1,0:T(8,128)(2,1)S(1)} %pad_maximum_fusion.1.refs_0_, ...), custom_call_target="tpu_custom_call" | custom-call | flops 19327352832 | bytes 39845904 | tf_op jit(solution)/shard_map/pallas_call | solution.py:66
  (164 shorter events, 56.7 us)
Async XLA Ops:
  1.5 14.6 %collective-permute-start = (bf16[128,1536]{1,0:T(8,128)(2,1)S(1)}, bf16[128,1536]{1,0:T(8,128)(2,1)S(1)}, u32[]{:S(2)}, u32[]{:S(2)}) collective-permute-start(bf16[128,1536]{1,0:T(8,128)(2,1)S(1)} %get-tuple-element.38), channel_id=1, source_target_pairs={{0,6},{1,7},{2,0},{3,1},{4,2},{5,3},{6,4},{7,5},{8,14},{9,15},{10,... | collective-permute-start | bytes 1179656 | tf_op jit(solution)/shard_map/ppermute | solution.py:383
  6.6 19.0 %collective-permute-start.2 = (bf16[128,1536]{1,0:T(8,128)(2,1)S(1)}, bf16[128,1536]{1,0:T(8,128)(2,1)S(1)}, u32[]{:S(2)}, u32[]{:S(2)}) collective-permute-start(bf16[128,1536]{1,0:T(8,128)(2,1)S(1)} %get-tuple-element.39), channel_id=1, source_target_pairs={{0,2},{1,3},{2,4},{3,5},{4,6},{5,7},{6,0},{7,1},{8,10},{9,11},{10,... | collective-permute-start | bytes 1179656 | tf_op jit(solution)/shard_map/ppermute | solution.py:383
  6.6 33.5 %collective-permute-start.1 = (bf16[128,1536]{1,0:T(8,128)(2,1)S(1)}, bf16[128,1536]{1,0:T(8,128)(2,1)S(1)}, u32[]{:S(2)}, u32[]{:S(2)}) collective-permute-start(bf16[128,1536]{1,0:T(8,128)(2,1)S(1)} %get-tuple-element.40), channel_id=1, source_target_pairs={{0,4},{1,5},{2,6},{3,7},{4,0},{5,1},{6,2},{7,3},{8,12},{9,13},{10,... | collective-permute-start | bytes 1179656 | tf_op jit(solution)/shard_map/ppermute | solution.py:383
  40.3 36.7 %collective-permute-start.9 = (bf16[512,1536]{1,0:T(8,128)(2,1)S(1)}, bf16[512,1536]{1,0:T(8,128)(2,1)S(1)}, u32[]{:S(2)}, u32[]{:S(2)}) collective-permute-start(bf16[512,1536]{1,0:T(8,128)(2,1)S(1)} %pad_maximum_fusion.refs_0_), channel_id=1, source_target_pairs={{0,16},{1,9},{2,18},{3,11},{4,20},{5,13},{6,22},{7,15},{8,24},{9,1... | collective-permute-start | bytes 4718600 | tf_op jit(solution)/shard_map/ppermute | solution.py:395
  41.9 35.3 %collective-permute-start.8 = (bf16[512,1536]{1,0:T(8,128)(2,1)S(1)}, bf16[512,1536]{1,0:T(8,128)(2,1)}, u32[]{:S(2)}, u32[]{:S(2)}) collective-permute-start(bf16[512,1536]{1,0:T(8,128)(2,1)S(1)} %pad_maximum_fusion.refs_0_), channel_id=1, source_target_pairs={{0,8},{1,17},{2,10},{3,19},{4,12},{5,21},{6,14},{7,23},{8,0},{9,25... | collective-permute-start | bytes 4718600 | tf_op jit(solution)/shard_map/ppermute | solution.py:395
  49.0 15.8 %collective-permute-start.4 = (bf16[128,1024]{1,0:T(8,128)(2,1)}, bf16[128,1024]{1,0:T(8,128)(2,1)S(1)}, u32[]{:S(2)}, u32[]{:S(2)}) collective-permute-start(bf16[128,1024]{1,0:T(8,128)(2,1)} %get-tuple-element.44), channel_id=1, source_target_pairs={{0,6},{1,7},{2,0},{3,1},{4,2},{5,3},{6,4},{7,5},{8,14},{9,15},{10,... | collective-permute-start | bytes 786440 | tf_op jit(solution)/shard_map/ppermute | solution.py:383
  51.6 22.2 %collective-permute-start.5 = (bf16[128,1024]{1,0:T(8,128)(2,1)}, bf16[128,1024]{1,0:T(8,128)(2,1)}, u32[]{:S(2)}, u32[]{:S(2)}) collective-permute-start(bf16[128,1024]{1,0:T(8,128)(2,1)} %get-tuple-element.46), channel_id=1, source_target_pairs={{0,4},{1,5},{2,6},{3,7},{4,0},{5,1},{6,2},{7,3},{8,12},{9,13},{10,... | collective-permute-start | bytes 786440 | tf_op jit(solution)/shard_map/ppermute | solution.py:383
  77.7 23.2 %collective-permute-start.12 = (bf16[512,1536]{1,0:T(8,128)(2,1)}, bf16[512,1536]{1,0:T(8,128)(2,1)S(1)}, u32[]{:S(2)}, u32[]{:S(2)}) collective-permute-start(bf16[512,1536]{1,0:T(8,128)(2,1)} %collective-permute-done.8.refs_1_), channel_id=1, source_target_pairs={{0,16},{1,9},{2,18},{3,11},{4,20},{5,13},{6,22},{7,15},{8,24},{9,1... | collective-permute-start | bytes 4718600 | tf_op jit(solution)/shard_map/ppermute | solution.py:395
  105.9 14.9 %collective-permute-start.16 = (bf16[128,1024]{1,0:T(8,128)(2,1)S(1)}, bf16[128,1024]{1,0:T(8,128)(2,1)S(1)}, u32[]{:S(2)}, u32[]{:S(2)}) collective-permute-start(bf16[128,1024]{1,0:T(8,128)(2,1)S(1)} %get-tuple-element.41), channel_id=1, source_target_pairs={{0,4},{1,5},{2,6},{3,7},{4,0},{5,1},{6,2},{7,3},{8,12},{9,13},{10,... | collective-permute-start | bytes 786440 | tf_op jit(solution)/shard_map/ppermute | solution.py:383
  137.0 32.6 %collective-permute-start.27 = (bf16[128,2560]{1,0:T(8,128)(2,1)S(1)}, bf16[128,2560]{1,0:T(8,128)(2,1)S(1)}, u32[]{:S(2)}, u32[]{:S(2)}) collective-permute-start(bf16[128,2560]{1,0:T(8,128)(2,1)S(1)} %pad_maximum_fusion.1.refs_0_), channel_id=1, source_target_pairs={{0,1},{1,0},{2,3},{3,2},{4,5},{5,4},{6,7},{7,6},{8,9},{9,8},{10,11... | collective-permute-start | bytes 1966088 | tf_op jit(solution)/shard_map/ppermute | solution.py:387
  145.3 22.4 %collective-permute-start.33 = (bf16[128,2560]{1,0:T(8,128)(2,1)S(1)}, bf16[128,2560]{1,0:T(8,128)(2,1)S(1)}, u32[]{:S(2)}, u32[]{:S(2)}) collective-permute-start(bf16[128,2560]{1,0:T(8,128)(2,1)S(1)} %constant_dynamic-update-slice_fusion.6.refs_8_), channel_id=1, source_target_pairs={{0,6},{1,7},{2,0},{3,1},{4,2},{5,3},{6,4},{7,5},{8,14},{9,15},{10,... | collective-permute-start | bytes 1966088 | tf_op jit(solution)/shard_map/ppermute | solution.py:383
  145.9 22.5 %collective-permute-start.32 = (bf16[128,2560]{1,0:T(8,128)(2,1)S(1)}, bf16[128,2560]{1,0:T(8,128)(2,1)S(1)}, u32[]{:S(2)}, u32[]{:S(2)}) collective-permute-start(bf16[128,2560]{1,0:T(8,128)(2,1)S(1)} %constant_dynamic-update-slice_fusion.6.refs_8_), channel_id=1, source_target_pairs={{0,16},{1,9},{2,18},{3,11},{4,20},{5,13},{6,22},{7,15},{8,24},{9,1... | collective-permute-start | bytes 1966088 | tf_op jit(solution)/shard_map/ppermute | solution.py:395
  147.0 21.3 %collective-permute-start.31 = (bf16[128,2560]{1,0:T(8,128)(2,1)S(1)}, bf16[128,2560]{1,0:T(8,128)(2,1)S(1)}, u32[]{:S(2)}, u32[]{:S(2)}) collective-permute-start(bf16[128,2560]{1,0:T(8,128)(2,1)S(1)} %constant_dynamic-update-slice_fusion.6.refs_8_), channel_id=1, source_target_pairs={{0,8},{1,17},{2,10},{3,19},{4,12},{5,21},{6,14},{7,23},{8,0},{9,25... | collective-permute-start | bytes 1966088 | tf_op jit(solution)/shard_map/ppermute | solution.py:395
  149.6 18.1 %collective-permute-start.26 = (bf16[128,1536]{1,0:T(8,128)(2,1)S(1)}, bf16[128,1536]{1,0:T(8,128)(2,1)S(1)}, u32[]{:S(2)}, u32[]{:S(2)}) collective-permute-start(bf16[128,1536]{1,0:T(8,128)(2,1)S(1)} %collective-permute-done.23), channel_id=1, source_target_pairs={{0,16},{1,9},{2,18},{3,11},{4,20},{5,13},{6,22},{7,15},{8,24},{9,1... | collective-permute-start | bytes 1179656 | tf_op jit(solution)/shard_map/ppermute | solution.py:395
  168.3 17.3 %collective-permute-start.34 = (bf16[128,2560]{1,0:T(8,128)(2,1)S(1)}, bf16[128,2560]{1,0:T(8,128)(2,1)S(1)}, u32[]{:S(2)}, u32[]{:S(2)}) collective-permute-start(bf16[128,2560]{1,0:T(8,128)(2,1)S(1)} %collective-permute-done.31.refs_9_), channel_id=1, source_target_pairs={{0,16},{1,9},{2,18},{3,11},{4,20},{5,13},{6,22},{7,15},{8,24},{9,1... | collective-permute-start | bytes 1966088 | tf_op jit(solution)/shard_map/ppermute | solution.py:395
  169.5 16.1 %collective-permute-start.40 = (bf16[128,2560]{1,0:T(8,128)(2,1)S(1)}, bf16[128,2560]{1,0:T(8,128)(2,1)S(1)}, u32[]{:S(2)}, u32[]{:S(2)}) collective-permute-start(bf16[128,2560]{1,0:T(8,128)(2,1)S(1)} %collective-permute-done.33.refs_16_), channel_id=1, source_target_pairs={{0,6},{1,7},{2,0},{3,1},{4,2},{5,3},{6,4},{7,5},{8,14},{9,15},{10,... | collective-permute-start | bytes 1966088 | tf_op jit(solution)/shard_map/ppermute | solution.py:383
  169.6 16.5 %collective-permute-start.39 = (bf16[128,2560]{1,0:T(8,128)(2,1)S(1)}, bf16[128,2560]{1,0:T(8,128)(2,1)S(1)}, u32[]{:S(2)}, u32[]{:S(2)}) collective-permute-start(bf16[128,2560]{1,0:T(8,128)(2,1)S(1)} %collective-permute-done.33.refs_16_), channel_id=1, source_target_pairs={{0,8},{1,17},{2,10},{3,19},{4,12},{5,21},{6,14},{7,23},{8,0},{9,25... | collective-permute-start | bytes 1966088 | tf_op jit(solution)/shard_map/ppermute | solution.py:395
  170.3 15.9 %collective-permute-start.29 = (bf16[128,2560]{1,0:T(8,128)(2,1)S(1)}, bf16[128,2560]{1,0:T(8,128)(2,1)S(1)}, u32[]{:S(2)}, u32[]{:S(2)}) collective-permute-start(bf16[128,2560]{1,0:T(8,128)(2,1)S(1)} %constant_dynamic-update-slice_fusion.2.refs_2_), channel_id=1, source_target_pairs={{0,1},{1,0},{2,3},{3,2},{4,5},{5,4},{6,7},{7,6},{8,9},{9,8},{10,11... | collective-permute-start | bytes 1966088 | tf_op jit(solution)/shard_map/ppermute | solution.py:387
  170.7 15.9 %collective-permute-start.30 = (bf16[128,2560]{1,0:T(8,128)(2,1)S(1)}, bf16[128,2560]{1,0:T(8,128)(2,1)S(1)}, u32[]{:S(2)}, u32[]{:S(2)}) collective-permute-start(bf16[128,2560]{1,0:T(8,128)(2,1)S(1)} %constant_dynamic-update-slice_fusion.4.refs_3_), channel_id=1, source_target_pairs={{0,1},{1,0},{2,3},{3,2},{4,5},{5,4},{6,7},{7,6},{8,9},{9,8},{10,11... | collective-permute-start | bytes 1966088 | tf_op jit(solution)/shard_map/ppermute | solution.py:387
  186.2 29.6 %collective-permute-start.43 = (bf16[128,2560]{1,0:T(8,128)(2,1)S(1)}, bf16[128,2560]{1,0:T(8,128)(2,1)S(1)}, u32[]{:S(2)}, u32[]{:S(2)}) collective-permute-start(bf16[128,2560]{1,0:T(8,128)(2,1)S(1)} %collective-permute-done.33.refs_16_), channel_id=1, source_target_pairs={{0,1},{1,0},{2,3},{3,2},{4,5},{5,4},{6,7},{7,6},{8,9},{9,8},{10,11... | collective-permute-start | bytes 1966088 | tf_op jit(solution)/shard_map/ppermute | solution.py:387
  186.6 27.9 %collective-permute-start.48 = (bf16[128,2560]{1,0:T(8,128)(2,1)S(1)}, bf16[128,2560]{1,0:T(8,128)(2,1)S(1)}, u32[]{:S(2)}, u32[]{:S(2)}) collective-permute-start(bf16[128,2560]{1,0:T(8,128)(2,1)S(1)} %collective-permute-done.40.refs_24_), channel_id=1, source_target_pairs={{0,16},{1,9},{2,18},{3,11},{4,20},{5,13},{6,22},{7,15},{8,24},{9,1... | collective-permute-start | bytes 1966088 | tf_op jit(solution)/shard_map/ppermute | solution.py:395
  187.7 26.9 %collective-permute-start.47 = (bf16[128,2560]{1,0:T(8,128)(2,1)S(1)}, bf16[128,2560]{1,0:T(8,128)(2,1)S(1)}, u32[]{:S(2)}, u32[]{:S(2)}) collective-permute-start(bf16[128,2560]{1,0:T(8,128)(2,1)S(1)} %collective-permute-done.40.refs_24_), channel_id=1, source_target_pairs={{0,8},{1,17},{2,10},{3,19},{4,12},{5,21},{6,14},{7,23},{8,0},{9,25... | collective-permute-start | bytes 1966088 | tf_op jit(solution)/shard_map/ppermute | solution.py:395
  188.6 25.3 %collective-permute-start.41 = (bf16[128,2560]{1,0:T(8,128)(2,1)S(1)}, bf16[128,2560]{1,0:T(8,128)(2,1)S(1)}, u32[]{:S(2)}, u32[]{:S(2)}) collective-permute-start(bf16[128,2560]{1,0:T(8,128)(2,1)S(1)} %collective-permute-done.33.refs_16_), channel_id=1, source_target_pairs={{0,16},{1,9},{2,18},{3,11},{4,20},{5,13},{6,22},{7,15},{8,24},{9,1... | collective-permute-start | bytes 1966088 | tf_op jit(solution)/shard_map/ppermute | solution.py:395
  189.6 24.4 %collective-permute-start.42 = (bf16[128,2560]{1,0:T(8,128)(2,1)S(1)}, bf16[128,2560]{1,0:T(8,128)(2,1)S(1)}, u32[]{:S(2)}, u32[]{:S(2)}) collective-permute-start(bf16[128,2560]{1,0:T(8,128)(2,1)S(1)} %collective-permute-done.34.refs_11_), channel_id=1, source_target_pairs={{0,6},{1,7},{2,0},{3,1},{4,2},{5,3},{6,4},{7,5},{8,14},{9,15},{10,... | collective-permute-start | bytes 1966088 | tf_op jit(solution)/shard_map/ppermute | solution.py:383
  (57 other events, 540.2 us)

commit v7 on v5

--- a/solution.py
+++ b/solution.py
@@ -308,8 +308,6 @@
             acc_hbm.at[i // 2, held], acc_ref.at[held], acc_sems.at[held]
         )
 
-    for i in range(2):
-        acc_copy(i).start()
     later = []
     for i in range(line):
         for k in range(2):
@@ -321,8 +319,10 @@
                     first = pl.multiple_of(first, size) if order < 3 else first
                     source, target = source.at[:, pl.ds(first, size)], cross_ref.at[e - 1, k, i]
                 later.append(pltpu.make_async_copy(source, target, later_sems.at[len(later)]))
+    wait_all(copies)
+    for i in range(2):
+        acc_copy(i).start()
     start_all(later)
-    wait_all(copies)
 
     def step(i, carry):
         e, k = i // 2, lax.rem(i, 2)

time: 261 us -> 262 us (level)
  no operation moved by 1% of the time
where the time goes in v7:
time: 262 us; the launch traced here: 261 us
  waiting for transfers between devices  123 us (47%)
  Pallas kernels  74.5 us (28%)
  starting transfers between devices  55.3 us (21%)
  local copies, waits for them, and re-layouts  5.93 us (2%)
    pallas_call x7, Pallas kernels, call(): pl.pallas_call(kernel, in_specs=specs, out_specs=pl.BlockSpec(memory_spac...  74.5 us
    ppermute x17, waiting for transfers between devices, along(): return lax.ppermute(values, 'col', pairs)  72.1 us
    ppermute x17, waiting for transfers between devices, across(): return lax.ppermute(values, ('row', 'col'), pairs)  46.3 us
    ppermute x17, starting transfers between devices, along(): return lax.ppermute(values, 'col', pairs)  26.9 us
    ppermute x17, starting transfers between devices, across(): return lax.ppermute(values, ('row', 'col'), pairs)  24.6 us
  transfers between devices with their start and end apart: 54, of which 24 were waited for; matrix products, arithmetic and copies ran while one was open for 1% of the time, Pallas kernels for 16%

profile of v7, /device:TPU:0, one launch (start us, length us, event | category | flops | bytes accessed | tf_op | source)
XLA Modules:
  0.0 261.4 jit_solution(10209620013358112039)
XLA Ops:
  1.5 5.1 %collective-permute-start = (bf16[128,1536]{1,0:T(8,128)(2,1)S(1)}, bf16[128,1536]{1,0:T(8,128)(2,1)S(1)}, u32[]{:S(2)}, u32[]{:S(2)}) collective-permute-start(bf16[128,1536]{1,0:T(8,128)(2,1)S(1)} %get-tuple-element.38), channel_id=1, source_target_pairs={{0,6},{1,7},{2,0},{3,1},{4,2},{5,3},{6,4},{7,5},{8,14},{9,15},{10,... | collective-permute-start | bytes 1179656 | tf_op jit(solution)/shard_map/ppermute | solution.py:383
  7.6 8.5 %collective-permute-done = bf16[128,1536]{1,0:T(8,128)(2,1)S(1)} collective-permute-done((bf16[128,1536]{1,0:T(8,128)(2,1)S(1)}, bf16[128,1536]{1,0:T(8,128)(2,1)S(1)}, u32[]{:S(2)}, u32[]{:S(2)}) %collective-permute-start) | collective-permute-done | bytes 393248 | tf_op jit(solution)/shard_map/ppermute | solution.py:383
  16.1 9.4 %collective-permute-done.2 = bf16[128,1536]{1,0:T(8,128)(2,1)S(1)} collective-permute-done((bf16[128,1536]{1,0:T(8,128)(2,1)S(1)}, bf16[128,1536]{1,0:T(8,128)(2,1)S(1)}, u32[]{:S(2)}, u32[]{:S(2)}) %collective-permute-start.2) | collective-permute-done | bytes 393248 | tf_op jit(solution)/shard_map/ppermute | solution.py:383
  25.5 14.6 %collective-permute-done.1 = bf16[128,1536]{1,0:T(8,128)(2,1)S(1)} collective-permute-done((bf16[128,1536]{1,0:T(8,128)(2,1)S(1)}, bf16[128,1536]{1,0:T(8,128)(2,1)S(1)}, u32[]{:S(2)}, u32[]{:S(2)}) %collective-permute-start.1) | collective-permute-done | bytes 393248 | tf_op jit(solution)/shard_map/ppermute | solution.py:383
  43.8 3.3 %shard_map.17 = bf16[4,128,1024]{2,1,0:T(8,128)(2,1)S(1)} custom-call(s32[4]{0:T(128)S(1)} %pad_add_fusion.meta_ref, bf16[512,1536]{1,0:T(8,128)(2,1)S(1)} %pad_maximum_fusion.refs_0_, bf16[512,1536]{1,0:T(8,128)(2,1)} %collective-permute-done.3.refs_1_.refs_3_), custom_call_target="tpu_custom_call" | custom-call | flops 1610612736 | bytes 3145744 | tf_op jit(solution)/shard_map/pallas_call | solution.py:66
  49.0 2.7 %collective-permute-start.4 = (bf16[128,1024]{1,0:T(8,128)(2,1)}, bf16[128,1024]{1,0:T(8,128)(2,1)S(1)}, u32[]{:S(2)}, u32[]{:S(2)}) collective-permute-start(bf16[128,1024]{1,0:T(8,128)(2,1)} %get-tuple-element.44), channel_id=1, source_target_pairs={{0,6},{1,7},{2,0},{3,1},{4,2},{5,3},{6,4},{7,5},{8,14},{9,15},{10,... | collective-permute-start | bytes 786440 | tf_op jit(solution)/shard_map/ppermute | solution.py:383
  52.2 12.5 %collective-permute-done.4 = bf16[128,1024]{1,0:T(8,128)(2,1)S(1)} collective-permute-done((bf16[128,1024]{1,0:T(8,128)(2,1)}, bf16[128,1024]{1,0:T(8,128)(2,1)S(1)}, u32[]{:S(2)}, u32[]{:S(2)}) %collective-permute-start.4) | collective-permute-done | bytes 262176 | tf_op jit(solution)/shard_map/ppermute | solution.py:383
  64.7 9.1 %collective-permute-done.5 = bf16[128,1024]{1,0:T(8,128)(2,1)} collective-permute-done((bf16[128,1024]{1,0:T(8,128)(2,1)}, bf16[128,1024]{1,0:T(8,128)(2,1)}, u32[]{:S(2)}, u32[]{:S(2)}) %collective-permute-start.5) | collective-permute-done | bytes 262176 | tf_op jit(solution)/shard_map/ppermute | solution.py:383
  79.2 2.6 %collective-permute-start.7 = (bf16[128,1024]{1,0:T(8,128)(2,1)S(1)}, bf16[128,1024]{1,0:T(8,128)(2,1)S(1)}, u32[]{:S(2)}, u32[]{:S(2)}) collective-permute-start(bf16[128,1024]{1,0:T(8,128)(2,1)S(1)} %fusion.5), channel_id=1, source_target_pairs={{0,6},{1,7},{2,0},{3,1},{4,2},{5,3},{6,4},{7,5},{8,14},{9,15},{10,... | collective-permute-start | bytes 786440 | tf_op jit(solution)/shard_map/ppermute | solution.py:383
  84.2 4.7 %shard_map.19 = bf16[4,128,1024]{2,1,0:T(8,128)(2,1)S(1)} custom-call(s32[4]{0:T(128)S(1)} %pad_add_fusion.meta_ref, bf16[512,1536]{1,0:T(8,128)(2,1)S(1)} %pad_maximum_fusion.refs_0_, bf16[512,1536]{1,0:T(8,128)(2,1)} %collective-permute-done.8.refs_1_, bf16[512,1536]{1,0:T(8,128)(2,1)S(1)} %collective-permute-done.9.refs_2_, bf16[512,1536]{1,0:T(8,128)(2,1)} %copy-done.2, ...), custom_call_target="tpu_custom_call" | custom-call | flops 1610612736 | bytes 7864336 | tf_op jit(solution)/shard_map/pallas_call | solution.py:66
  89.1 3.8 %collective-permute-start.13 = (bf16[128,1024]{1,0:T(8,128)(2,1)S(1)}, bf16[128,1024]{1,0:T(8,128)(2,1)S(1)}, u32[]{:S(2)}, u32[]{:S(2)}) collective-permute-start(bf16[128,1024]{1,0:T(8,128)(2,1)S(1)} %get-tuple-element.43), channel_id=1, source_target_pairs={{0,6},{1,7},{2,0},{3,1},{4,2},{5,3},{6,4},{7,5},{8,14},{9,15},{10,... | collective-permute-start | bytes 786440 | tf_op jit(solution)/shard_map/ppermute | solution.py:383
  92.9 8.0 %shard_map.18.near_hbm = bf16[3,2,4,768,128]{4,3,2,1,0:T(8,128)(2,1)} custom-call(s32[4]{0:T(128)S(1)} %pad_add_fusion.meta_ref, bf16[512,1536]{1,0:T(8,128)(2,1)S(1)} %pad_maximum_fusion.refs_0_, bf16[512,1536]{1,0:T(8,128)(2,1)} %collective-permute-done.8.refs_1_, bf16[512,1536]{1,0:T(8,128)(2,1)S(1)} %collective-permute-done.9.refs_2_, ...), custom_call_target="tpu_custom_call" | custom-call | flops 150994944 | bytes 9437200 | tf_op jit(solution)/shard_map/pallas_call | solution.py:66
  103.2 2.7 %collective-permute-start.19 = (bf16[128,1024]{1,0:T(8,128)(2,1)S(1)}, bf16[128,1024]{1,0:T(8,128)(2,1)S(1)}, u32[]{:S(2)}, u32[]{:S(2)}) collective-permute-start(bf16[128,1024]{1,0:T(8,128)(2,1)S(1)} %fusion.5), channel_id=1, source_target_pairs={{0,8},{1,17},{2,10},{3,19},{4,12},{5,21},{6,14},{7,23},{8,0},{9,25... | collective-permute-start | bytes 786440 | tf_op jit(solution)/shard_map/ppermute | solution.py:395
  114.3 3.6 %collective-permute-start.17 = (bf16[128,512]{1,0:T(8,128)(2,1)S(1)}, bf16[128,512]{1,0:T(8,128)(2,1)S(1)}, u32[]{:S(2)}, u32[]{:S(2)}) collective-permute-start(bf16[128,512]{1,0:T(8,128)(2,1)S(1)} %get-tuple-element.47), channel_id=1, source_target_pairs={{0,6},{1,7},{2,0},{3,1},{4,2},{5,3},{6,4},{7,5},{8,14},{9,15},{10,... | collective-permute-start | bytes 393224 | tf_op jit(solution)/shard_map/ppermute | solution.py:383
  117.8 3.0 %collective-permute-done.16 = bf16[128,1024]{1,0:T(8,128)(2,1)S(1)} collective-permute-done((bf16[128,1024]{1,0:T(8,128)(2,1)S(1)}, bf16[128,1024]{1,0:T(8,128)(2,1)S(1)}, u32[]{:S(2)}, u32[]{:S(2)}) %collective-permute-start.16) | collective-permute-done | bytes 262176 | tf_op jit(solution)/shard_map/ppermute | solution.py:383
  126.8 4.2 %collective-permute-done.21 = bf16[128,512]{1,0:T(8,128)(2,1)S(1)} collective-permute-done((bf16[128,512]{1,0:T(8,128)(2,1)S(1)}, bf16[128,512]{1,0:T(8,128)(2,1)S(1)}, u32[]{:S(2)}, u32[]{:S(2)}) %collective-permute-start.21) | collective-permute-done | bytes 131104 | tf_op jit(solution)/shard_map/ppermute | solution.py:383
  134.1 2.8 %collective-permute-start.23 = (bf16[128,1536]{1,0:T(8,128)(2,1)S(1)}, bf16[128,1536]{1,0:T(8,128)(2,1)S(1)}, u32[]{:S(2)}, u32[]{:S(2)}) collective-permute-start(bf16[128,1536]{1,0:T(8,128)(2,1)S(1)} %pad_maximum_fusion.2), channel_id=1, source_target_pairs={{0,8},{1,17},{2,10},{3,19},{4,12},{5,21},{6,14},{7,23},{8,0},{9,25... | collective-permute-start | bytes 1179656 | tf_op jit(solution)/shard_map/ppermute | solution.py:395
  137.1 4.4 %collective-permute-done.25 = bf16[128,1536]{1,0:T(8,128)(2,1)S(1)} collective-permute-done((bf16[128,1536]{1,0:T(8,128)(2,1)S(1)}, bf16[128,1536]{1,0:T(8,128)(2,1)S(1)}, u32[]{:S(2)}, u32[]{:S(2)}) %collective-permute-start.25) | collective-permute-done | bytes 393248 | tf_op jit(solution)/shard_map/ppermute | solution.py:383
  141.5 3.8 %collective-permute-done.24 = bf16[128,1536]{1,0:T(8,128)(2,1)S(1)} collective-permute-done((bf16[128,1536]{1,0:T(8,128)(2,1)S(1)}, bf16[128,1536]{1,0:T(8,128)(2,1)S(1)}, u32[]{:S(2)}, u32[]{:S(2)}) %collective-permute-start.24) | collective-permute-done | bytes 393248 | tf_op jit(solution)/shard_map/ppermute | solution.py:395
  150.5 17.1 %collective-permute-done.26 = bf16[128,1536]{1,0:T(8,128)(2,1)S(1)} collective-permute-done((bf16[128,1536]{1,0:T(8,128)(2,1)S(1)}, bf16[128,1536]{1,0:T(8,128)(2,1)S(1)}, u32[]{:S(2)}, u32[]{:S(2)}) %collective-permute-start.26) | collective-permute-done | bytes 393248 | tf_op jit(solution)/shard_map/ppermute | solution.py:395
  170.9 14.7 %collective-permute-done.34.refs_11_ = bf16[128,2560]{1,0:T(8,128)(2,1)S(1)} collective-permute-done((bf16[128,2560]{1,0:T(8,128)(2,1)S(1)}, bf16[128,2560]{1,0:T(8,128)(2,1)S(1)}, u32[]{:S(2)}, u32[]{:S(2)}) %collective-permute-start.34) | collective-permute-done | bytes 655392 | tf_op jit(solution)/shard_map/ppermute | solution.py:395
  191.6 22.3 %shard_map.22.acc_hbm = f32[4,2,4,768,128]{4,3,2,1,0:T(8,128)} custom-call(s32[4]{0:T(128)S(1)} %pad_add_fusion.meta_ref, bf16[3,2,4,768,128]{4,3,2,1,0:T(8,128)(2,1)} %shard_map.18.near_hbm, bf16[1,2,4,768,128]{4,3,2,1,0:T(8,128)(2,1)} %copy-done, bf16[128,2560]{1,0:T(8,128)(2,1)S(1)} %pad_maximum_fusion.1.refs_0_, ...), custom_call_target="tpu_custom_call" | custom-call | flops 12884901888 | bytes 16777232 | tf_op jit(solution)/shard_map/pallas_call | solution.py:66
  217.2 8.1 %collective-permute-done.49.refs_27_ = bf16[128,2560]{1,0:T(8,128)(2,1)S(1)} collective-permute-done((bf16[128,2560]{1,0:T(8,128)(2,1)S(1)}, bf16[128,2560]{1,0:T(8,128)(2,1)S(1)}, u32[]{:S(2)}, u32[]{:S(2)}) %collective-permute-start.49) | collective-permute-done | bytes 655392 | tf_op jit(solution)/shard_map/ppermute | solution.py:395
  228.3 32.9 %shard_map.23 = bf16[4,2,128,768]{3,2,1,0:T(8,128)(2,1)} custom-call(s32[4]{0:T(128)S(1)} %pad_add_fusion.meta_ref, bf16[3,2,4,768,128]{4,3,2,1,0:T(8,128)(2,1)} %shard_map.18.near_hbm, bf16[1,2,4,768,128]{4,3,2,1,0:T(8,128)(2,1)} %copy-done, f32[4,2,4,768,128]{4,3,2,1,0:T(8,128)} %shard_map.22.acc_hbm, bf16[128,2560]{1,0:T(8,128)(2,1)S(1)} %pad_maximum_fusion.1.refs_0_, ...), custom_call_target="tpu_custom_call" | custom-call | flops 19327352832 | bytes 39845904 | tf_op jit(solution)/shard_map/pallas_call | solution.py:66
  (164 shorter events, 56.7 us)
Async XLA Ops:
  1.5 14.6 %collective-permute-start = (bf16[128,1536]{1,0:T(8,128)(2,1)S(1)}, bf16[128,1536]{1,0:T(8,128)(2,1)S(1)}, u32[]{:S(2)}, u32[]{:S(2)}) collective-permute-start(bf16[128,1536]{1,0:T(8,128)(2,1)S(1)} %get-tuple-element.38), channel_id=1, source_target_pairs={{0,6},{1,7},{2,0},{3,1},{4,2},{5,3},{6,4},{7,5},{8,14},{9,15},{10,... | collective-permute-start | bytes 1179656 | tf_op jit(solution)/shard_map/ppermute | solution.py:383
  6.6 19.0 %collective-permute-start.2 = (bf16[128,1536]{1,0:T(8,128)(2,1)S(1)}, bf16[128,1536]{1,0:T(8,128)(2,1)S(1)}, u32[]{:S(2)}, u32[]{:S(2)}) collective-permute-start(bf16[128,1536]{1,0:T(8,128)(2,1)S(1)} %get-tuple-element.39), channel_id=1, source_target_pairs={{0,2},{1,3},{2,4},{3,5},{4,6},{5,7},{6,0},{7,1},{8,10},{9,11},{10,... | collective-permute-start | bytes 1179656 | tf_op jit(solution)/shard_map/ppermute | solution.py:383
  6.6 33.5 %collective-permute-start.1 = (bf16[128,1536]{1,0:T(8,128)(2,1)S(1)}, bf16[128,1536]{1,0:T(8,128)(2,1)S(1)}, u32[]{:S(2)}, u32[]{:S(2)}) collective-permute-start(bf16[128,1536]{1,0:T(8,128)(2,1)S(1)} %get-tuple-element.40), channel_id=1, source_target_pairs={{0,4},{1,5},{2,6},{3,7},{4,0},{5,1},{6,2},{7,3},{8,12},{9,13},{10,... | collective-permute-start | bytes 1179656 | tf_op jit(solution)/shard_map/ppermute | solution.py:383
  40.3 36.7 %collective-permute-start.9 = (bf16[512,1536]{1,0:T(8,128)(2,1)S(1)}, bf16[512,1536]{1,0:T(8,128)(2,1)S(1)}, u32[]{:S(2)}, u32[]{:S(2)}) collective-permute-start(bf16[512,1536]{1,0:T(8,128)(2,1)S(1)} %pad_maximum_fusion.refs_0_), channel_id=1, source_target_pairs={{0,16},{1,9},{2,18},{3,11},{4,20},{5,13},{6,22},{7,15},{8,24},{9,1... | collective-permute-start | bytes 4718600 | tf_op jit(solution)/shard_map/ppermute | solution.py:395
  41.9 35.3 %collective-permute-start.8 = (bf16[512,1536]{1,0:T(8,128)(2,1)S(1)}, bf16[512,1536]{1,0:T(8,128)(2,1)}, u32[]{:S(2)}, u32[]{:S(2)}) collective-permute-start(bf16[512,1536]{1,0:T(8,128)(2,1)S(1)} %pad_maximum_fusion.refs_0_), channel_id=1, source_target_pairs={{0,8},{1,17},{2,10},{3,19},{4,12},{5,21},{6,14},{7,23},{8,0},{9,25... | collective-permute-start | bytes 4718600 | tf_op jit(solution)/shard_map/ppermute | solution.py:395
  49.0 15.8 %collective-permute-start.4 = (bf16[128,1024]{1,0:T(8,128)(2,1)}, bf16[128,1024]{1,0:T(8,128)(2,1)S(1)}, u32[]{:S(2)}, u32[]{:S(2)}) collective-permute-start(bf16[128,1024]{1,0:T(8,128)(2,1)} %get-tuple-element.44), channel_id=1, source_target_pairs={{0,6},{1,7},{2,0},{3,1},{4,2},{5,3},{6,4},{7,5},{8,14},{9,15},{10,... | collective-permute-start | bytes 786440 | tf_op jit(solution)/shard_map/ppermute | solution.py:383
  51.6 22.2 %collective-permute-start.5 = (bf16[128,1024]{1,0:T(8,128)(2,1)}, bf16[128,1024]{1,0:T(8,128)(2,1)}, u32[]{:S(2)}, u32[]{:S(2)}) collective-permute-start(bf16[128,1024]{1,0:T(8,128)(2,1)} %get-tuple-element.46), channel_id=1, source_target_pairs={{0,4},{1,5},{2,6},{3,7},{4,0},{5,1},{6,2},{7,3},{8,12},{9,13},{10,... | collective-permute-start | bytes 786440 | tf_op jit(solution)/shard_map/ppermute | solution.py:383
  77.7 23.2 %collective-permute-start.12 = (bf16[512,1536]{1,0:T(8,128)(2,1)}, bf16[512,1536]{1,0:T(8,128)(2,1)S(1)}, u32[]{:S(2)}, u32[]{:S(2)}) collective-permute-start(bf16[512,1536]{1,0:T(8,128)(2,1)} %collective-permute-done.8.refs_1_), channel_id=1, source_target_pairs={{0,16},{1,9},{2,18},{3,11},{4,20},{5,13},{6,22},{7,15},{8,24},{9,1... | collective-permute-start | bytes 4718600 | tf_op jit(solution)/shard_map/ppermute | solution.py:395
  105.9 14.9 %collective-permute-start.16 = (bf16[128,1024]{1,0:T(8,128)(2,1)S(1)}, bf16[128,1024]{1,0:T(8,128)(2,1)S(1)}, u32[]{:S(2)}, u32[]{:S(2)}) collective-permute-start(bf16[128,1024]{1,0:T(8,128)(2,1)S(1)} %get-tuple-element.41), channel_id=1, source_target_pairs={{0,4},{1,5},{2,6},{3,7},{4,0},{5,1},{6,2},{7,3},{8,12},{9,13},{10,... | collective-permute-start | bytes 786440 | tf_op jit(solution)/shard_map/ppermute | solution.py:383
  137.0 32.6 %collective-permute-start.27 = (bf16[128,2560]{1,0:T(8,128)(2,1)S(1)}, bf16[128,2560]{1,0:T(8,128)(2,1)S(1)}, u32[]{:S(2)}, u32[]{:S(2)}) collective-permute-start(bf16[128,2560]{1,0:T(8,128)(2,1)S(1)} %pad_maximum_fusion.1.refs_0_), channel_id=1, source_target_pairs={{0,1},{1,0},{2,3},{3,2},{4,5},{5,4},{6,7},{7,6},{8,9},{9,8},{10,11... | collective-permute-start | bytes 1966088 | tf_op jit(solution)/shard_map/ppermute | solution.py:387
  145.3 22.4 %collective-permute-start.33 = (bf16[128,2560]{1,0:T(8,128)(2,1)S(1)}, bf16[128,2560]{1,0:T(8,128)(2,1)S(1)}, u32[]{:S(2)}, u32[]{:S(2)}) collective-permute-start(bf16[128,2560]{1,0:T(8,128)(2,1)S(1)} %constant_dynamic-update-slice_fusion.6.refs_8_), channel_id=1, source_target_pairs={{0,6},{1,7},{2,0},{3,1},{4,2},{5,3},{6,4},{7,5},{8,14},{9,15},{10,... | collective-permute-start | bytes 1966088 | tf_op jit(solution)/shard_map/ppermute | solution.py:383
  145.9 22.5 %collective-permute-start.32 = (bf16[128,2560]{1,0:T(8,128)(2,1)S(1)}, bf16[128,2560]{1,0:T(8,128)(2,1)S(1)}, u32[]{:S(2)}, u32[]{:S(2)}) collective-permute-start(bf16[128,2560]{1,0:T(8,128)(2,1)S(1)} %constant_dynamic-update-slice_fusion.6.refs_8_), channel_id=1, source_target_pairs={{0,16},{1,9},{2,18},{3,11},{4,20},{5,13},{6,22},{7,15},{8,24},{9,1... | collective-permute-start | bytes 1966088 | tf_op jit(solution)/shard_map/ppermute | solution.py:395
  147.0 21.3 %collective-permute-start.31 = (bf16[128,2560]{1,0:T(8,128)(2,1)S(1)}, bf16[128,2560]{1,0:T(8,128)(2,1)S(1)}, u32[]{:S(2)}, u32[]{:S(2)}) collective-permute-start(bf16[128,2560]{1,0:T(8,128)(2,1)S(1)} %constant_dynamic-update-slice_fusion.6.refs_8_), channel_id=1, source_target_pairs={{0,8},{1,17},{2,10},{3,19},{4,12},{5,21},{6,14},{7,23},{8,0},{9,25... | collective-permute-start | bytes 1966088 | tf_op jit(solution)/shard_map/ppermute | solution.py:395
  149.6 18.1 %collective-permute-start.26 = (bf16[128,1536]{1,0:T(8,128)(2,1)S(1)}, bf16[128,1536]{1,0:T(8,128)(2,1)S(1)}, u32[]{:S(2)}, u32[]{:S(2)}) collective-permute-start(bf16[128,1536]{1,0:T(8,128)(2,1)S(1)} %collective-permute-done.23), channel_id=1, source_target_pairs={{0,16},{1,9},{2,18},{3,11},{4,20},{5,13},{6,22},{7,15},{8,24},{9,1... | collective-permute-start | bytes 1179656 | tf_op jit(solution)/shard_map/ppermute | solution.py:395
  168.3 17.3 %collective-permute-start.34 = (bf16[128,2560]{1,0:T(8,128)(2,1)S(1)}, bf16[128,2560]{1,0:T(8,128)(2,1)S(1)}, u32[]{:S(2)}, u32[]{:S(2)}) collective-permute-start(bf16[128,2560]{1,0:T(8,128)(2,1)S(1)} %collective-permute-done.31.refs_9_), channel_id=1, source_target_pairs={{0,16},{1,9},{2,18},{3,11},{4,20},{5,13},{6,22},{7,15},{8,24},{9,1... | collective-permute-start | bytes 1966088 | tf_op jit(solution)/shard_map/ppermute | solution.py:395
  169.5 16.1 %collective-permute-start.40 = (bf16[128,2560]{1,0:T(8,128)(2,1)S(1)}, bf16[128,2560]{1,0:T(8,128)(2,1)S(1)}, u32[]{:S(2)}, u32[]{:S(2)}) collective-permute-start(bf16[128,2560]{1,0:T(8,128)(2,1)S(1)} %collective-permute-done.33.refs_16_), channel_id=1, source_target_pairs={{0,6},{1,7},{2,0},{3,1},{4,2},{5,3},{6,4},{7,5},{8,14},{9,15},{10,... | collective-permute-start | bytes 1966088 | tf_op jit(solution)/shard_map/ppermute | solution.py:383
  169.6 16.5 %collective-permute-start.39 = (bf16[128,2560]{1,0:T(8,128)(2,1)S(1)}, bf16[128,2560]{1,0:T(8,128)(2,1)S(1)}, u32[]{:S(2)}, u32[]{:S(2)}) collective-permute-start(bf16[128,2560]{1,0:T(8,128)(2,1)S(1)} %collective-permute-done.33.refs_16_), channel_id=1, source_target_pairs={{0,8},{1,17},{2,10},{3,19},{4,12},{5,21},{6,14},{7,23},{8,0},{9,25... | collective-permute-start | bytes 1966088 | tf_op jit(solution)/shard_map/ppermute | solution.py:395
  170.3 15.9 %collective-permute-start.29 = (bf16[128,2560]{1,0:T(8,128)(2,1)S(1)}, bf16[128,2560]{1,0:T(8,128)(2,1)S(1)}, u32[]{:S(2)}, u32[]{:S(2)}) collective-permute-start(bf16[128,2560]{1,0:T(8,128)(2,1)S(1)} %constant_dynamic-update-slice_fusion.2.refs_2_), channel_id=1, source_target_pairs={{0,1},{1,0},{2,3},{3,2},{4,5},{5,4},{6,7},{7,6},{8,9},{9,8},{10,11... | collective-permute-start | bytes 1966088 | tf_op jit(solution)/shard_map/ppermute | solution.py:387
  170.7 15.9 %collective-permute-start.30 = (bf16[128,2560]{1,0:T(8,128)(2,1)S(1)}, bf16[128,2560]{1,0:T(8,128)(2,1)S(1)}, u32[]{:S(2)}, u32[]{:S(2)}) collective-permute-start(bf16[128,2560]{1,0:T(8,128)(2,1)S(1)} %constant_dynamic-update-slice_fusion.4.refs_3_), channel_id=1, source_target_pairs={{0,1},{1,0},{2,3},{3,2},{4,5},{5,4},{6,7},{7,6},{8,9},{9,8},{10,11... | collective-permute-start | bytes 1966088 | tf_op jit(solution)/shard_map/ppermute | solution.py:387
  186.2 29.6 %collective-permute-start.43 = (bf16[128,2560]{1,0:T(8,128)(2,1)S(1)}, bf16[128,2560]{1,0:T(8,128)(2,1)S(1)}, u32[]{:S(2)}, u32[]{:S(2)}) collective-permute-start(bf16[128,2560]{1,0:T(8,128)(2,1)S(1)} %collective-permute-done.33.refs_16_), channel_id=1, source_target_pairs={{0,1},{1,0},{2,3},{3,2},{4,5},{5,4},{6,7},{7,6},{8,9},{9,8},{10,11... | collective-permute-start | bytes 1966088 | tf_op jit(solution)/shard_map/ppermute | solution.py:387
  186.6 27.9 %collective-permute-start.48 = (bf16[128,2560]{1,0:T(8,128)(2,1)S(1)}, bf16[128,2560]{1,0:T(8,128)(2,1)S(1)}, u32[]{:S(2)}, u32[]{:S(2)}) collective-permute-start(bf16[128,2560]{1,0:T(8,128)(2,1)S(1)} %collective-permute-done.40.refs_24_), channel_id=1, source_target_pairs={{0,16},{1,9},{2,18},{3,11},{4,20},{5,13},{6,22},{7,15},{8,24},{9,1... | collective-permute-start | bytes 1966088 | tf_op jit(solution)/shard_map/ppermute | solution.py:395
  187.7 26.9 %collective-permute-start.47 = (bf16[128,2560]{1,0:T(8,128)(2,1)S(1)}, bf16[128,2560]{1,0:T(8,128)(2,1)S(1)}, u32[]{:S(2)}, u32[]{:S(2)}) collective-permute-start(bf16[128,2560]{1,0:T(8,128)(2,1)S(1)} %collective-permute-done.40.refs_24_), channel_id=1, source_target_pairs={{0,8},{1,17},{2,10},{3,19},{4,12},{5,21},{6,14},{7,23},{8,0},{9,25... | collective-permute-start | bytes 1966088 | tf_op jit(solution)/shard_map/ppermute | solution.py:395
  188.6 25.3 %collective-permute-start.41 = (bf16[128,2560]{1,0:T(8,128)(2,1)S(1)}, bf16[128,2560]{1,0:T(8,128)(2,1)S(1)}, u32[]{:S(2)}, u32[]{:S(2)}) collective-permute-start(bf16[128,2560]{1,0:T(8,128)(2,1)S(1)} %collective-permute-done.33.refs_16_), channel_id=1, source_target_pairs={{0,16},{1,9},{2,18},{3,11},{4,20},{5,13},{6,22},{7,15},{8,24},{9,1... | collective-permute-start | bytes 1966088 | tf_op jit(solution)/shard_map/ppermute | solution.py:395
  189.6 24.4 %collective-permute-start.42 = (bf16[128,2560]{1,0:T(8,128)(2,1)S(1)}, bf16[128,2560]{1,0:T(8,128)(2,1)S(1)}, u32[]{:S(2)}, u32[]{:S(2)}) collective-permute-start(bf16[128,2560]{1,0:T(8,128)(2,1)S(1)} %collective-permute-done.34.refs_11_), channel_id=1, source_target_pairs={{0,6},{1,7},{2,0},{3,1},{4,2},{5,3},{6,4},{7,5},{8,14},{9,15},{10,... | collective-permute-start | bytes 1966088 | tf_op jit(solution)/shard_map/ppermute | solution.py:383
  (57 other events, 540.2 us)
